TPU v7x, 128 devices: a whole 4x4x4 slice. The times are simulated.
128 devices in a mesh: elem: 8 (over z, y_lo), snap: 16 (over x, y_hi, core).
Axes of the slice: x: 4, y: 4 (y_hi: 2, y_lo: 2; y = y_hi * 2 + y_lo), z: 4, core: 2. Of those that a mesh axis runs over, the one named last changes fastest.
Arguments:
- snapshots: bfloat16 [2048, 6, 65536], P('snap', None, 'elem'), may hold values from -6 to 6
- coefficients: bfloat16 [2048, 128], P('snap'), may hold values from -0.125 to 0.125
- mass_weights: float32 [65536], P('elem'), may hold values from 3.90625e-05 to 0.000390625
- metric: float32 [3, 3, 65536], P(None, None, 'elem'), may hold values from -3 to 3
- out_modes: int32 [32], replicated, may hold values from 0 to 127, as said below
Outputs:
- tensor: float32 [32, 128, 128], P(None, 'snap', 'elem')
- diffusion: float32 [32, 128], P('elem', 'snap')
Inputs may be any that keep to these rules, and one draw needn't show every extreme that they name: `out_modes`: 32 distinct mode numbers; 0 and 127 are always among them.
All inputs are finite; a program needn't handle non-finite values.
Results may differ from a plain program's by a relative error of at most 0.035.
Values may be sent and summed in bfloat16 or wider, within the bound.
No kernel may reach another device: no remote copies, remote signals or barrier semaphores. Data moves between devices by JAX's collectives and lax.ppermute only.
A program may use at most 256 MiB of HBM per device.

v0:
```python
import math

import jax
import jax.numpy as jnp
import numpy as np
from jax import lax
from jax.sharding import PartitionSpec as P

GLL = 8


def legendre_pair(value, points):
    before, current = (1.0, value)
    for degree in range(2, points):
        before, current = (
            current,
            ((2 * degree - 1) * value * current - (degree - 1) * before) / degree,
        )
    return (before, current)


def derivative_tables(points):
    degree = points - 1
    nodes = [math.cos(math.pi * index / degree) for index in range(points)]
    for sweep in range(100):
        updated = []
        for value in nodes:
            before, current = legendre_pair(value, points)
            updated.append(value - (value * current - before) / (points * current))
        nodes = updated
    abscissae = sorted(nodes)
    evaluated = [legendre_pair(value, points)[1] for value in abscissae]
    matrix = np.zeros((points, points))
    for first in range(points):
        for second in range(points):
            if first != second:
                matrix[first, second] = evaluated[first] / (
                    evaluated[second] * (abscissae[first] - abscissae[second])
                )
    matrix[0, 0] = -degree * (degree + 1) / 4.0
    matrix[degree, degree] = degree * (degree + 1) / 4.0
    identity = np.eye(points)
    stacked = np.stack(
        [
            np.kron(identity, np.kron(identity, matrix.T)),
            np.kron(identity, np.kron(matrix.T, identity)),
            np.kron(matrix.T, np.kron(identity, identity)),
        ]
    )
    return jnp.asarray(stacked, jnp.float32).astype(jnp.bfloat16)


def gradients(field, tables, metric):
    row_count, components, node_count = field.shape
    element_size = tables.shape[1]
    blocks = field.reshape(row_count * components * (node_count // element_size), element_size)
    combined = jnp.zeros((row_count, components, 3, node_count), jnp.float32)
    for direction in range(3):
        derived = jnp.dot(blocks, tables[direction], preferred_element_type=jnp.float32)
        derived = derived.reshape(row_count, components, 1, node_count)
        combined = combined + metric[direction][None, None, :, :] * derived
    return combined.astype(jnp.bfloat16)


def weighted_pairs(chosen, grads, weights):
    swapped = jnp.concatenate([chosen[:, 3:], chosen[:, :3]], axis=1)
    paired = jnp.stack([chosen, -swapped], axis=1)
    total = None
    for component in range(6):
        left = paired[:, None, :, component, None, :].astype(jnp.float32)
        right = grads[None, :, None, component, :, :].astype(jnp.float32)
        term = left * right
        total = term if total is None else total + term
    return (total * weights).astype(jnp.bfloat16)


def on_device(snapshots, coefficients, mass_weights, metric, out_modes):
    snap_rows, components, node_count = snapshots.shape
    mode_count = coefficients.shape[1]
    owned = mode_count // lax.axis_size("snap")
    out_count = out_modes.shape[0]
    flat = snapshots.reshape(snap_rows, components * node_count)
    tables = derivative_tables(GLL)
    first_owned = lax.axis_index("snap") * owned
    own_flat = lax.psum_scatter(
        lax.dot_general(
            coefficients, flat, (((0,), (0,)), ((), ())), preferred_element_type=jnp.float32
        ).astype(jnp.bfloat16),
        "snap",
        scatter_dimension=0,
        tiled=True,
    )
    positions = first_owned + lax.iota(jnp.int32, owned)
    selector = (out_modes[:, None] == positions[None, :]).astype(jnp.bfloat16)
    picked = jnp.dot(selector, own_flat, preferred_element_type=jnp.float32)
    chosen = lax.psum(picked.astype(jnp.bfloat16), "snap")
    own_modes = own_flat.reshape(owned, components, node_count)
    chosen = chosen.reshape(out_count, components, node_count)
    grads_owned = gradients(own_modes, tables, metric)
    grads_chosen = gradients(chosen, tables, metric)
    product = weighted_pairs(chosen, grads_owned, mass_weights).reshape(
        out_count * owned, components * node_count
    )
    scaled_chosen = (grads_chosen.astype(jnp.float32) * mass_weights).reshape(
        out_count, components * 3 * node_count
    )
    diffusion = lax.dot_general(
        scaled_chosen,
        grads_owned.astype(jnp.float32).reshape(owned, components * 3 * node_count),
        (((1,), (1,)), ((), ())),
        precision=lax.Precision.HIGHEST,
        preferred_element_type=jnp.float32,
    )
    columns = lax.dot_general(
        product,
        lax.all_gather(own_flat, "snap", axis=0, tiled=True),
        (((1,), (1,)), ((), ())),
        preferred_element_type=jnp.float32,
    )
    tensor = columns
    tensor = tensor.reshape(out_count, owned, mode_count)
    tensor_share, diffusion_share = (
        lax.psum_scatter(
            tensor.astype(jnp.bfloat16), "elem", scatter_dimension=2, tiled=True
        ).astype(jnp.float32),
        lax.psum_scatter(
            diffusion.astype(jnp.bfloat16), "elem", scatter_dimension=0, tiled=True
        ).astype(jnp.float32),
    )
    return (tensor_share, diffusion_share)


def solution(mesh):
    return jax.shard_map(
        on_device,
        mesh=mesh,
        in_specs=(P("snap", None, "elem"), P("snap", None), P("elem"), P(None, None, "elem"), P()),
        out_specs=(P(None, "snap", "elem"), P("elem", "snap")),
        check_vma=False,
    )
```

profile of v0, /device:TPU:0, one launch (start us, length us, event | category | flops | bytes accessed | tf_op | source)
XLA Modules:
  0.0 616.0 jit_solution(5607485366467934647)
XLA Ops:
  7.2 16.6 %copy.35 = bf16[128,6,8192]{0,2,1:T(8,128)(2,1)} copy(bf16[128,6,8192]{2,0,1:T(8,128)(2,1)} %param.6) | data formatting | bytes 25165824 | tf_op args[0]
  23.8 9.1 %convolution_convert_fusion = bf16[128,49152]{1,0:T(8,128)(2,1)} fusion(bf16[128,128]{1,0:T(8,128)(2,1)S(1)} %copy-done, bf16[128,49152]{0,1:T(8,128)(2,1)} %bitcast.88), kind=kOutput, calls=%fused_computation | convolution fusion | flops 1616904192 | bytes 25198592 | tf_op jit(solution)/shard_map/dot_general | solution.py:86
  33.1 124.7 %reduce-scatter.3.cloned.1.call-done = bf16[8,49152]{1,0:T(8,128)(2,1)} async-done(((bf16[128,49152]{1,0:T(8,128)(2,1)}), bf16[8,49152]{1,0:T(8,128)(2,1)}) %reduce-scatter.3.cloned.1.call-update) | async-done | bytes 786448 | tf_op jit(solution)/shard_map/reduce_scatter | solution.py:85
  188.5 119.8 %all-reduce.3.cloned.1.call-done = bf16[32,49152]{1,0:T(8,128)(2,1)} async-done(((bf16[32,49152]{1,0:T(8,128)(2,1)}), bf16[32,49152]{1,0:T(8,128)(2,1)}) %all-reduce.3.cloned.1.call-update) | async-done | bytes 3145744 | tf_op jit(solution)/shard_map/psum | solution.py:96
  308.3 7.4 %reshape.217 = bf16[32,6,8192]{2,1,0:T(8,128)(2,1)} reshape(bf16[32,49152]{1,0:T(8,128)(2,1)} %all-reduce.3.cloned.1.call-done) | data formatting | bytes 6291456 | tf_op jit(solution)/shard_map/reshape | solution.py:98
  315.7 5.8 stack_reshape.3
  321.5 5.8 slice_bitcast_fusion.1
  329.9 14.2 %fusion.21 = (f32[32,2,1,8192]{3,2,0,1:T(1,128)S(1)}, f32[32,2,1,8192]{3,2,0,1:T(1,128)S(1)}, f32[32,2,1,8192]{3,2,0,1:T(1,128)}, f32[32,2,1,8192]{3,2,0,1:T(1,1...) fusion(bf16[32,1,6,8192]{3,2,0,1:T(8,128)(2,1)S(1)} %maximum_negate_fusion, ...), kind=kLoop, calls=%fused_computation.46 | loop fusion | flops 12582912 | bytes 18874368 | tf_op jit(solution)/shard_map/convert_element_type | solution.py:70
  344.1 5.9 copy_bitcast_fusion.4
  350.0 7.4 %mul.260 = f32[32,2,3,8192]{3,2,1,0:T(4,128)} broadcast(f32[32,2,8192]{2,1,0:T(2,128)} %get-tuple-element.30), dimensions={0,1,3} | broadcast | bytes 8388608 | tf_op jit(solution)/shard_map/mul | solution.py:72
  357.4 8.6 %mul.261 = f32[32,49152]{1,0:T(8,128)} reshape(f32[32,2,3,8192]{3,2,1,0:T(4,128)} %mul.260) | data formatting | bytes 12582912 | tf_op jit(solution)/shard_map/mul | solution.py:72
  366.1 6.8 %mul.282 = f32[32,2,3,8192]{3,2,1,0:T(4,128)} broadcast(f32[32,2,8192]{2,1,0:T(2,128)} %get-tuple-element.29), dimensions={0,1,3} | broadcast | bytes 8388608 | tf_op jit(solution)/shard_map/mul | solution.py:72
  372.9 8.8 %mul.283 = f32[32,49152]{1,0:T(8,128)} reshape(f32[32,2,3,8192]{3,2,1,0:T(4,128)} %mul.282) | data formatting | bytes 12582912 | tf_op jit(solution)/shard_map/mul | solution.py:72
  381.7 8.1 %copy_bitcast_fusion.2 = (f32[32,2,8192]{2,1,0:T(2,128)}, f32[32,2,8192]{2,1,0:T(2,128)}) fusion(f32[32,2,1,8192]{3,2,0,1:T(1,128)} %get-tuple-element.11, f32[32,2,1,8192]{3,2,0,1:T(1,128)} %get-tuple-element.10), kind=kLoop, calls=%fused_computation.39 | loop fusion | bytes 8388608 | tf_op jit(solution)/shard_map/convert_element_type | solution.py:70
  389.8 6.8 %mul.289 = f32[32,2,3,8192]{3,2,1,0:T(4,128)} broadcast(f32[32,2,8192]{2,1,0:T(2,128)} %get-tuple-element.28), dimensions={0,1,3} | broadcast | bytes 8388608 | tf_op jit(solution)/shard_map/mul | solution.py:72
  396.6 8.8 %mul.290 = f32[32,49152]{1,0:T(8,128)} reshape(f32[32,2,3,8192]{3,2,1,0:T(4,128)} %mul.289) | data formatting | bytes 12582912 | tf_op jit(solution)/shard_map/mul | solution.py:72
  405.4 6.8 %mul.296 = f32[32,2,3,8192]{3,2,1,0:T(4,128)} broadcast(f32[32,2,8192]{2,1,0:T(2,128)} %get-tuple-element.27), dimensions={0,1,3} | broadcast | bytes 8388608 | tf_op jit(solution)/shard_map/mul | solution.py:72
  412.2 9.0 %mul.297 = f32[32,49152]{1,0:T(8,128)} reshape(f32[32,2,3,8192]{3,2,1,0:T(4,128)} %mul.296) | data formatting | bytes 12582912 | tf_op jit(solution)/shard_map/mul | solution.py:72
  421.2 7.4 %copy_bitcast_fusion = (f32[32,2,8192]{2,1,0:T(2,128)}, f32[32,2,8192]{2,1,0:T(2,128)}) fusion(f32[32,2,1,8192]{3,2,0,1:T(1,128)S(1)} %get-tuple-element.12, f32[32,2,1,8192]{3,2,0,1:T(1,128)} %get-tuple-element.13), kind=kLoop, calls=%fused_computation.37 | loop fusion | bytes 8388608 | tf_op jit(solution)/shard_map/convert_element_type | solution.py:70
  428.6 6.8 %mul.303 = f32[32,2,3,8192]{3,2,1,0:T(4,128)} broadcast(f32[32,2,8192]{2,1,0:T(2,128)} %get-tuple-element.26), dimensions={0,1,3} | broadcast | bytes 8388608 | tf_op jit(solution)/shard_map/mul | solution.py:72
  435.4 8.7 %mul.304 = f32[32,49152]{1,0:T(8,128)} reshape(f32[32,2,3,8192]{3,2,1,0:T(4,128)} %mul.303) | data formatting | bytes 12582912 | tf_op jit(solution)/shard_map/mul | solution.py:72
  449.3 8.6 %mul.311 = f32[32,49152]{1,0:T(8,128)} reshape(f32[32,2,3,8192]{3,2,1,0:T(4,128)} %mul.310) | data formatting | bytes 12582912 | tf_op jit(solution)/shard_map/mul | solution.py:72
  461.4 5.5 fusion.44
  466.8 9.1 %mul.322 = f32[32,6,8192]{2,1,0:T(8,128)} reshape(f32[3072,512]{1,0:T(8,128)} %fusion.44) | data formatting | bytes 12582912 | tf_op jit(solution)/shard_map/mul | solution.py:61
  476.0 9.7 %copy.46 = f32[32,6,8192]{2,0,1:T(8,128)} copy(f32[32,6,8192]{2,1,0:T(8,128)} %mul.322) | data formatting | bytes 12582912 | tf_op jit(solution)/shard_map/mul | solution.py:61
  490.1 9.0 %mul.326 = f32[32,6,8192]{2,1,0:T(8,128)} reshape(f32[3072,512]{1,0:T(8,128)} %fusion.45) | data formatting | bytes 12582912 | tf_op jit(solution)/shard_map/mul | solution.py:61
  499.1 9.7 %copy.47 = f32[32,6,8192]{2,0,1:T(8,128)} copy(f32[32,6,8192]{2,1,0:T(8,128)} %mul.326) | data formatting | bytes 12582912 | tf_op jit(solution)/shard_map/mul | solution.py:61
  513.2 9.2 %mul.330 = f32[32,6,8192]{2,1,0:T(8,128)} reshape(f32[3072,512]{1,0:T(8,128)} %fusion.46) | data formatting | bytes 12582912 | tf_op jit(solution)/shard_map/mul | solution.py:61
  522.4 9.8 %copy.48 = f32[32,6,8192]{2,0,1:T(8,128)} copy(f32[32,6,8192]{2,1,0:T(8,128)} %mul.330) | data formatting | bytes 12582912 | tf_op jit(solution)/shard_map/mul | solution.py:61
  534.4 32.0 %fusion.23 = bf16[32,8,128]{2,1,0:T(8,128)(2,1)S(1)} fusion(bf16[128,49152]{1,0:T(8,128)(2,1)} %all-gather.2.cloned.1.call-done, f32[49152]{0:T(1024)S(1)} %copy-done.28, f32[8,49152]{1,0:T(8,128)S(1)} %bitcast.93, f32[32,49152]{1,0:T(8,128)} %mul.311, f32[8,49152]{1,0:T(8,128)S(1)} %bitcast.92, f32[32,49152]{1,0:T(8,128)} %mul.304, ...), kind=kOutput, calls=%fused_computation.48 | convolution fusion | flops 3384836096 | bytes 60030976 | tf_op jit(solution)/shard_map/dot_general | solution.py:114
  567.4 20.1 %fusion.29 = bf16[32,8]{1,0:T(8,128)(2,1)S(1)} fusion(bf16[8,6,3,8192]{3,0,2,1:T(8,128)(2,1)S(1)} %copy-done.5, f32[8192]{0:T(1024)S(1)} %copy-done.30, f32[32,6,8192]{2,0,1:T(8,128)} %copy.48, f32[3,8192]{1,0:T(4,128)S(1)} %copy-done.24, f32[32,6,8192]{2,0,1:T(8,128)} %copy.47, f32[3,8192]{1,0:T(4,128)S(1)} %copy-done.26, f32[32,6,8192]{2,0,1:T(8,128)} %copy.46, ...), kind=kOutput, calls=%fused_computation.50 | convolution fusion | flops 490733824 | bytes 21561856 | tf_op jit(solution)/shard_map/dot_general | solution.py:107
  587.5 19.7 %all-reduce = bf16[32,8]{1,0:T(8,128)(2,1)S(1)} all-reduce(bf16[32,8]{1,0:T(8,128)(2,1)S(1)} %fusion.29), channel_id=4, replica_groups=mesh['elem'=8,'snap'=16] {'elem'}, use_global_device_ids=true, to_apply=%region_3.0.clone | all-reduce | flops 256 | bytes 1024
  (108 shorter events, 55.2 us)
Async XLA Ops:
  7.2 16.7 %copy-start = (bf16[128,128]{1,0:T(8,128)(2,1)S(1)}, bf16[128,128]{1,0:T(8,128)(2,1)}, u32[]{:S(2)}) copy-start(bf16[128,128]{1,0:T(8,128)(2,1)} %param.7) | copy-start | bytes 98308
  7.2 150.6 %reduce-scatter.3.cloned.1.call-start = ((), (), s32[]{:S(2)}) async-start(), calls=%async_computation.2 | async-start | bytes 13369344 | tf_op jit(solution)/shard_map/reduce_scatter | solution.py:85
  33.0 124.8 %copy-start.31 = (s32[32]{0:T(128)S(1)}, s32[32]{0:T(128)}, u32[]{:S(2)}) copy-start(s32[32]{0:T(128)} %param.10) | copy-start | bytes 388
  33.0 129.5 %copy-start.29 = (f32[8192]{0:T(1024)S(1)}, f32[8192]{0:T(1024)}, u32[]{:S(2)}) copy-start(f32[8192]{0:T(1024)} %param.8) | copy-start | bytes 98308
  33.0 275.3 %all-reduce.3.cloned.1.call-start = ((), (), s32[]{:S(2)}) async-start(), calls=%async_computation.3 | async-start | bytes 6291456 | tf_op jit(solution)/shard_map/psum | solution.py:96
  157.8 5.6 copy-start.32
  157.8 6.8 %copy-start.27 = (f32[3,3,8192]{2,1,0:T(4,128)S(1)}, f32[3,3,8192]{2,1,0:T(4,128)}, u32[]{:S(2)}) copy-start(f32[3,3,8192]{2,1,0:T(4,128)} %param.9) | copy-start | bytes 884740
  157.8 7.6 %copy-start.7 = (bf16[8,49152]{1,0:T(8,128)(2,1)S(1)}, bf16[8,49152]{1,0:T(8,128)(2,1)}, u32[]{:S(2)}) copy-start(bf16[8,49152]{1,0:T(8,128)(2,1)} %reduce-scatter.3.cloned.1.call-done) | copy-start | bytes 2359300
  161.7 4.1 copy-start.20
  161.7 370.5 %all-gather.2.cloned.1.call-start = ((), (), s32[]{:S(2)}) async-start(), calls=%async_computation.4 | async-start | bytes 13369344 | tf_op jit(solution)/shard_map/all_gather | solution.py:116
  162.4 445.4 %reduce-scatter.5.cloned.1.call-start = ((), (), s32[]{:S(2)}) async-start(), calls=%async_computation.5 | async-start | bytes 294912 | tf_op jit(solution)/shard_map/reduce_scatter | solution.py:123
  167.5 4.7 copy-start.18
  173.9 4.2 copy-start.16
  179.8 3.1 copy-start.21
  179.8 3.1 copy-start.23
  179.8 3.1 copy-start.25
  182.0 1.9 copy-start.9
  308.3 7.4 %copy-start.2 = (bf16[32,49152]{1,0:T(8,128)(2,1)S(1)}, bf16[32,49152]{1,0:T(8,128)(2,1)}, u32[]{:S(2)}) copy-start(bf16[32,49152]{1,0:T(8,128)(2,1)} %all-reduce.3.cloned.1.call-done) | copy-start | bytes 9437188
  327.3 2.6 copy-start.3
  435.4 8.7 %copy-start.6 = (f32[32,2,8192]{2,1,0:T(2,128)S(1)}, f32[32,2,8192]{2,1,0:T(2,128)}, u32[]{:S(2)}) copy-start(f32[32,2,8192]{2,1,0:T(2,128)} %get-tuple-element.25) | copy-start | bytes 6291460
  476.0 9.7 %copy-start.19 = (bf16[512,512]{1,0:T(8,128)(2,1)S(1)}, bf16[512,512]{1,0:T(8,128)(2,1)}, u32[]{:S(2)}) copy-start(bf16[512,512]{1,0:T(8,128)(2,1)} %constant.13) | copy-start | bytes 1572868
  499.1 9.7 %copy-start.17 = (bf16[512,512]{1,0:T(8,128)(2,1)S(1)}, bf16[512,512]{1,0:T(8,128)(2,1)}, u32[]{:S(2)}) copy-start(bf16[512,512]{1,0:T(8,128)(2,1)} %constant.15) | copy-start | bytes 1572868
  522.4 9.8 %copy-start.15 = (f32[8,3,8192]{2,0,1:T(8,128)S(1)}, f32[8,3,8192]{2,0,1:T(8,128)}, u32[]{:S(2)}) copy-start(f32[8,3,8192]{2,0,1:T(8,128)} %get-tuple-element.21) | copy-start | bytes 2359300
  522.4 9.9 %copy-start.14 = (f32[8,3,8192]{2,0,1:T(8,128)S(1)}, f32[8,3,8192]{2,0,1:T(8,128)}, u32[]{:S(2)}) copy-start(f32[8,3,8192]{2,0,1:T(8,128)} %get-tuple-element.20) | copy-start | bytes 2359300
  532.1 1.6 copy-start.11
  532.3 1.7 copy-start.10
  534.4 33.0 %copy-start.5 = (bf16[8,6,3,8192]{3,0,2,1:T(8,128)(2,1)S(1)}, bf16[8,6,3,8192]{3,0,2,1:T(8,128)(2,1)}, u32[]{:S(2)}) copy-start(bf16[8,6,3,8192]{3,0,2,1:T(8,128)(2,1)} %copy-done.4) | copy-start | bytes 7077892
  534.4 33.0 %copy-start.22 = (f32[3,8192]{1,0:T(4,128)S(1)}, f32[3,8192]{1,0:T(4,128)}, u32[]{:S(2)}) copy-start(f32[3,8192]{1,0:T(4,128)} %get-tuple-element.22) | copy-start | bytes 294916
  534.4 33.0 %copy-start.24 = (f32[3,8192]{1,0:T(4,128)S(1)}, f32[3,8192]{1,0:T(4,128)}, u32[]{:S(2)}) copy-start(f32[3,8192]{1,0:T(4,128)} %get-tuple-element.23) | copy-start | bytes 294916
  534.4 33.0 %copy-start.26 = (f32[3,8192]{1,0:T(4,128)S(1)}, f32[3,8192]{1,0:T(4,128)}, u32[]{:S(2)}) copy-start(f32[3,8192]{1,0:T(4,128)} %get-tuple-element.24) | copy-start | bytes 294916
  534.4 33.0 %copy-start.30 = (f32[8192]{0:T(1024)S(1)}, f32[8192]{0:T(1024)}, u32[]{:S(2)}) copy-start(f32[8192]{0:T(1024)} %param.8) | copy-start | bytes 98308
  567.4 41.8 %copy-start.1 = (bf16[128,128]{1,0:T(8,128)(2,1)S(1)}, bf16[128,128]{1,0:T(8,128)(2,1)}, u32[]{:S(2)}) copy-start(bf16[128,128]{1,0:T(8,128)(2,1)} %param.7) | copy-start | bytes 98308
  (5 other events, 6.6 us)
Sparse Core Ops, SparseCore 0:
  33.1 124.5 reduce-scatter.2
  161.8 146.4 all-reduce.2
  311.0 91.7 all-gather.1
  567.5 38.5 reduce-scatter.4
where the time goes:
time: 622 us; the launch traced here: 616 us
  waiting for transfers between devices  245 us (39%)
  local copies, waits for them, and re-layouts  231 us (37%)
  matrix products  84.6 us (14%)
  other arithmetic  20.4 us (3%)
  blocking collectives  19.7 us (3%)
  between operations  15.1 us (2%)
    reduce_scatter x1, waiting for transfers between devices, on_device(): lax.psum_scatter(lax.dot_general(coefficients, flat, (((0,), (0,)), ((),...  125 us
    psum x1, waiting for transfers between devices, on_device(): chosen = lax.psum(picked.astype(jnp.bfloat16), 'snap')  120 us
    mul x18, local copies, waits for them, and re-layouts, weighted_pairs(): term = left * right  93 us
    mul x13, local copies, waits for them, and re-layouts, gradients(): combined = combined + metric[direction][None, None, :, :] * derived  69.2 us
    dot_general x1, matrix products, on_device(): lax.dot_general(product, lax.all_gather(own_flat, 'snap', axis=0, tiled=T...  32 us
    unnamed x69, local copies, waits for them, and re-layouts  22.7 us
    convert_element_type x3, local copies, waits for them, and re-layouts, weighted_pairs(): left = paired[:, None, :, component, None, :].astype(jnp.float32)  21.5 us
    dot_general x1, matrix products, on_device(): lax.dot_general(scaled_chosen, grads_owned.astype(jnp.float32).reshape(ow...  20.1 us
  transfers between devices with their start and end apart: 4, of which 2 were waited for; matrix products, arithmetic and copies ran while one was open for 43% of the time, Pallas kernels for 0%

commit v1 on v0

v1 whole, which is shorter than its diff:
```python
import math

import jax
import jax.numpy as jnp
import numpy as np
from jax import lax
from jax.experimental import pallas as pl
from jax.experimental.pallas import tpu as pltpu
from jax.sharding import PartitionSpec as P

GLL = 8
NPE = 512
AXES = ("elem", "snap")
BF = jnp.bfloat16
F32 = jnp.float32


def legendre_pair(value, points):
    before, current = (1.0, value)
    for degree in range(2, points):
        before, current = (
            current,
            ((2 * degree - 1) * value * current - (degree - 1) * before) / degree,
        )
    return (before, current)


def derivative_tables(points):
    degree = points - 1
    nodes = [math.cos(math.pi * index / degree) for index in range(points)]
    for sweep in range(100):
        updated = []
        for value in nodes:
            before, current = legendre_pair(value, points)
            updated.append(value - (value * current - before) / (points * current))
        nodes = updated
    abscissae = sorted(nodes)
    evaluated = [legendre_pair(value, points)[1] for value in abscissae]
    matrix = np.zeros((points, points))
    for first in range(points):
        for second in range(points):
            if first != second:
                matrix[first, second] = evaluated[first] / (
                    evaluated[second] * (abscissae[first] - abscissae[second])
                )
    matrix[0, 0] = -degree * (degree + 1) / 4.0
    matrix[degree, degree] = degree * (degree + 1) / 4.0
    identity = np.eye(points)
    stacked = np.concatenate(
        [
            np.kron(identity, np.kron(identity, matrix.T)),
            np.kron(identity, np.kron(matrix.T, identity)),
            np.kron(matrix.T, np.kron(identity, identity)),
        ],
        axis=1,
    )
    return jnp.asarray(stacked, jnp.float32).astype(jnp.bfloat16)


def place(x, y, z, core):
    return (z * 2 + y % 2) * 16 + (x * 2 + y // 2) * 2 + core


def moves(shift):
    pairs = []
    for x in range(4):
        for y in range(4):
            for z in range(4):
                for core in range(2):
                    nx, ny, nz, ncore = shift(x, y, z, core)
                    pairs.append((place(x, y, z, core), place(nx % 4, ny % 4, nz % 4, ncore)))
    return pairs


CORE = moves(lambda x, y, z, c: (x, y, z, 1 - c))
XP = moves(lambda x, y, z, c: (x + 1, y, z, c))
XM = moves(lambda x, y, z, c: (x - 1, y, z, c))
Y2 = moves(lambda x, y, z, c: (x, y + 2, z, c))


def send(value, pairs):
    return lax.ppermute(value, AXES, pairs)


ITEM = (3, 128, NPE)
ITEM_BYTES = 3 * 128 * NPE * 2
VMEM = 56 * 1024 * 1024


def item_cost(items, reads):
    return pl.CostEstimate(
        flops=2 * items * 3 * 128 * 128 * NPE,
        bytes_accessed=ITEM_BYTES * reads,
        transcendentals=0,
    )


def partials_kernel(ids, halves, coef_ref, x_ref, out_ref):
    coef = coef_ref[...].T
    for c in range(3):
        out_ref[0, c] = jnp.dot(coef, x_ref[c], preferred_element_type=F32).astype(BF)


def partials(fields, coef, ids, halves, name):
    count = len(ids)
    return pl.pallas_call(
        partials_kernel,
        grid_spec=pltpu.PrefetchScalarGridSpec(
            num_scalar_prefetch=2,
            grid=(count,),
            in_specs=[
                pl.BlockSpec((128, 128), lambda i, ids, halves: (0, 0)),
                pl.BlockSpec(ITEM, lambda i, ids, halves: (halves[i], 0, ids[i])),
            ],
            out_specs=pl.BlockSpec((1,) + ITEM, lambda i, ids, halves: (i, 0, 0, 0)),
        ),
        out_shape=jax.ShapeDtypeStruct((count,) + ITEM, BF),
        compiler_params=pltpu.CompilerParams(vmem_limit_bytes=VMEM),
        cost_estimate=item_cost(count, 2 * count),
        name=name,
    )(jnp.stack(ids), jnp.array(halves, jnp.int32), coef, fields)


def fixed(row):
    return lambda i, ids: (row, 0, 0, 0)


def sums(fields, coef, items, outs, name):
    plan, operands, specs = [], [], []
    for slot, (element, half, adds) in enumerate(items):
        operands.append(fields)
        specs.append(pl.BlockSpec(ITEM, lambda i, ids, slot=slot, half=half: (half, 0, ids[slot])))
    for element, half, adds in items:
        entry = []
        for array, row, span in adds:
            entry.append((len(operands), span))
            operands.append(array)
            specs.append(pl.BlockSpec((1,) + array.shape[1:], fixed(row)))
        plan.append(entry)

    def kernel(ids, coef_ref, *refs):
        ins, results = refs[: len(operands)], refs[len(operands) :]
        coef = coef_ref[...].T
        for slot, entry in enumerate(plan):
            for c in range(3):
                total = jnp.dot(coef, ins[slot][c], preferred_element_type=F32)
                whole = [position for position, span in entry if span is None]
                for position in whole:
                    total = total + ins[position][0, c].astype(F32)
                parts = {0: total[:64], 64: total[64:]}
                for position, span in entry:
                    if span is not None:
                        parts[span] = parts[span] + ins[position][0, c].astype(F32)
                for number, group in enumerate(outs):
                    for place_in, (item, span) in enumerate(group):
                        if item == slot and span is None:
                            results[number][place_in, c, :64] = parts[0].astype(BF)
                            results[number][place_in, c, 64:] = parts[64].astype(BF)
                        elif item == slot:
                            results[number][place_in, c] = parts[span].astype(BF)

    shapes = [(len(group), 3, 128 if group[0][1] is None else 64, NPE) for group in outs]
    return pl.pallas_call(
        kernel,
        grid_spec=pltpu.PrefetchScalarGridSpec(
            num_scalar_prefetch=1,
            grid=(1,),
            in_specs=[pl.BlockSpec((128, 128), lambda i, ids: (0, 0))] + specs,
            out_specs=[pl.BlockSpec(shape, lambda i, ids: (0, 0, 0, 0)) for shape in shapes],
        ),
        out_shape=[jax.ShapeDtypeStruct(shape, BF) for shape in shapes],
        compiler_params=pltpu.CompilerParams(vmem_limit_bytes=VMEM),
        cost_estimate=item_cost(len(items), len(operands) + len(items)),
        name=name,
    )(jnp.stack([element for element, half, adds in items]), coef, *operands)


KS = 34


def assemble_kernel(counts, ids, coef_ref, tables_ref, weight_ref, metric_ref, order_j, order_i, pick_k, pick_d,
                    xu_ref, xb_ref, *refs):
    adds_u, adds_b = refs[: counts[0]], refs[counts[0] : counts[0] + counts[1]]
    keep_ref, send_ref, zi_ref, zj_ref, g_ref, cb_ref = refs[counts[0] + counts[1] :]
    coef = coef_ref[...].T
    weight = weight_ref[...]
    half_weight = 0.5 * weight
    for a in range(3):
        u = jnp.dot(coef, xu_ref[a], preferred_element_type=F32)
        for ref in adds_u:
            u = u + ref[0, a].astype(F32)
        b = jnp.dot(coef, xb_ref[a], preferred_element_type=F32)
        for ref in adds_b:
            b = b + ref[0, a].astype(F32)
        for sign, z in ((0, u + b), (1, u - b)):
            z = z.astype(BF)
            zi_ref[:, ((1 - sign) * 3 + a) * NPE : ((1 - sign) * 3 + a + 1) * NPE] = jnp.dot(
                order_i[...], z, preferred_element_type=F32
            ).astype(BF)
            zj_ref[sign, a] = jnp.dot(order_j[...], z, preferred_element_type=F32).astype(BF)
            cb_ref[sign, a] = (
                jnp.dot(pick_k[...], z, preferred_element_type=F32) * half_weight
            ).astype(BF)

    diffusion = None
    for sign in range(2):
        for a in range(3):
            derived = jnp.dot(zj_ref[sign, a], tables_ref[...], preferred_element_type=F32)
            for b in range(3):
                grad = metric_ref[0, b : b + 1, :] * derived[:, :NPE]
                grad = grad + metric_ref[1, b : b + 1, :] * derived[:, NPE : 2 * NPE]
                grad = grad + metric_ref[2, b : b + 1, :] * derived[:, 2 * NPE :]
                grad = grad.astype(BF)
                g_ref[sign, a, b] = grad
                picked = jnp.dot(pick_d[...], grad, preferred_element_type=F32) * half_weight
                term = lax.dot_general(
                    grad, picked.astype(BF), (((1,), (1,)), ((), ())), preferred_element_type=F32
                )
                diffusion = term if diffusion is None else diffusion + term

    def put(k, block):
        block = block.astype(BF).reshape(2, 8, 8, 128)
        keep_ref[:, pl.ds(k, 1)] = block[0][:, None]
        send_ref[:, pl.ds(k, 1)] = block[1][:, None]

    put(32, diffusion)
    put(33, jnp.zeros((128, 128), F32))

    def row(k, carry):
        pieces = []
        for sign in range(2):
            picked = [cb_ref[sign, a, pl.ds(pl.multiple_of(k * 16, 16), 16), :][None] for a in range(3)]
            for b in range(3):
                total = None
                for a in range(3):
                    term = g_ref[sign, a, b].reshape(8, 16, NPE) * picked[a]
                    total = term if total is None else total + term
                pieces.append(total.reshape(128, NPE))
        product = jnp.concatenate(pieces, axis=1)
        put(k, lax.dot_general(product, zi_ref[...], (((1,), (1,)), ((), ())), preferred_element_type=F32))
        return carry

    lax.fori_loop(0, 32, row, 0)


def assemble(fields, coef, tables, weights, metric, order_j, order_i, pick_k, pick_d, element, adds_u, adds_b):
    def kernel(*args):
        assemble_kernel((len(adds_u), len(adds_b)), *args)

    def whole(shape):
        return pl.BlockSpec(shape, lambda i, ids: (0,) * len(shape))

    adds = adds_u + adds_b
    out = jax.ShapeDtypeStruct((8, KS, 8, 128), BF)
    return pl.pallas_call(
        kernel,
        grid_spec=pltpu.PrefetchScalarGridSpec(
            num_scalar_prefetch=1,
            grid=(1,),
            in_specs=[
                whole((128, 128)),
                whole(tables.shape),
                pl.BlockSpec((1, NPE), lambda i, ids: (0, ids[0])),
                pl.BlockSpec((3, 3, NPE), lambda i, ids: (0, 0, ids[0])),
                whole((128, 128)),
                whole((128, 128)),
                whole((512, 128)),
                whole((128, 128)),
                pl.BlockSpec(ITEM, lambda i, ids: (0, 0, ids[0])),
                pl.BlockSpec(ITEM, lambda i, ids: (1, 0, ids[0])),
            ]
            + [pl.BlockSpec((1,) + ITEM, fixed(row)) for array, row in adds],
            out_specs=[whole(out.shape), whole(out.shape)],
            scratch_shapes=[
                pltpu.VMEM((128, 6 * NPE), BF),
                pltpu.VMEM((2, 3, 128, NPE), BF),
                pltpu.VMEM((2, 3, 3, 128, NPE), BF),
                pltpu.VMEM((2, 3, 512, NPE), BF),
            ],
        ),
        out_shape=[out, out],
        compiler_params=pltpu.CompilerParams(vmem_limit_bytes=VMEM),
        cost_estimate=pl.CostEstimate(flops=10**10, bytes_accessed=10**7, transcendentals=0),
        name="assemble",
    )(element[None], coef, tables, weights, metric, order_j, order_i, pick_k, pick_d, fields, fields,
      *[array for array, row in adds])


def whole_call(kernel, outs, name, *operands):
    return pl.pallas_call(
        kernel,
        out_shape=outs,
        compiler_params=pltpu.CompilerParams(vmem_limit_bytes=VMEM),
        name=name,
    )(*operands)


def split_kernel(keep_ref, got_ref, *outs):
    for n in range(8):
        outs[n][...] = (keep_ref[n].astype(F32) + got_ref[n].astype(F32)).astype(BF)


def turn_kernel(*refs):
    ins, outs, rows = refs[:8], refs[8:16], refs[16]
    total = ins[0][...].astype(F32)
    for n in range(1, 8):
        total = total + ins[n][...].astype(F32)
    rows[...] = total.reshape(KS * 8, 128)
    ordered = [rows[pl.ds(j, 32, stride=8), :] for j in range(8)] + [rows[256:272, :]]
    turned = jnp.concatenate(ordered, axis=0).T
    for n in range(8):
        outs[n][...] = turned[n * 16 : n * 16 + 16].astype(BF)


def finish_kernel(*refs):
    ins, tensor_ref, diffusion_ref = refs[:8], refs[8], refs[9]
    total = ins[0][...].astype(F32)
    for n in range(1, 8):
        total = total + ins[n][...].astype(F32)
    for j in range(8):
        tensor_ref[j] = total[:, 32 * j : 32 * j + 32]
    diffusion_ref[...] = total[0:4, 256:264]


def on_device(snapshots, coefficients, mass_weights, metric, out_modes):
    fields = snapshots.transpose(1, 0, 2)
    snap, elem = lax.axis_index("snap"), lax.axis_index("elem")
    x, y_hi, core = snap // 4, (snap // 2) % 2, snap % 2
    z, y_lo = elem // 2, elem % 2

    def element(dx, dy, dcore=0):
        return ((core ^ dcore) * 8 + ((x + dx) % 4) * 2 + (y_hi ^ dy)).astype(jnp.int32)

    def exchange(wanted, name):
        ids = [element(dx, dy, 1) for half, dx, dy in wanted]
        value = partials(fields, coefficients, ids, [half for half, dx, dy in wanted], name)
        got = send(value, CORE)
        return {key: (got, n) for n, key in enumerate(wanted)}

    U, B = 0, 1
    got = exchange([(U, 2, 0), (U, 2, 1), (B, 2, 1)], "part1")
    got.update(exchange([(B, 1, 1), (B, 3, 1), (B, 0, 1)], "part2"))
    got.update(exchange([(U, 1, 1), (U, 3, 0), (U, 1, 0), (U, 3, 1)], "part3"))
    got.update(exchange([(U, 0, 1), (U, 0, 0), (B, 2, 0), (B, 1, 0), (B, 3, 0), (B, 0, 0)], "part4"))

    def item(half, dx, dy, *more):
        array, row = got[(half, dx, dy)]
        return (element(dx, dy), half, [(array, row, None)] + list(more))

    def total(items, outs, name):
        return sums(fields, coefficients, items, outs, name)

    one = [[(0, None)]]
    pair = [[(0, None)], [(1, None)]]
    both = [[(0, None), (1, None)]]
    yb1 = send(total([item(B, 2, 1)], one, "yb1")[0], Y2)
    right, left = total([item(U, 2, 0), item(U, 2, 1)], pair, "xa1")
    xa1r, xa1l = send(right, XP), send(left, XM)
    yb2 = send(total([item(B, 1, 1), item(B, 3, 1)], both, "yb2")[0], Y2)
    yb3 = send(total([item(B, 0, 1)], one, "yb3")[0], Y2)
    right, left = total([item(U, 1, 1), item(U, 3, 0)], pair, "xa2")
    xa2r, xa2l = send(right, XP), send(left, XM)
    right, left = total([item(U, 1, 0, (xa1r, 0, None)), item(U, 3, 1, (xa1l, 0, None))], pair, "xa3")
    xa3r, xa3l = send(right, XP), send(left, XM)
    right, left = total([item(B, 2, 0, (yb1, 0, None))], [[(0, 0)], [(0, 64)]], "xb1")
    xb1r, xb1l = send(right, XP), send(left, XM)
    right, left = total(
        [item(B, 1, 0, (yb2, 0, None), (xb1r, 0, 0)), item(B, 3, 0, (yb2, 1, None), (xb1l, 0, 64))], pair, "xb2"
    )
    xb2r, xb2l = send(right, XP), send(left, XM)
    ya = send(total([item(U, 0, 1, (xa2r, 0, None), (xa3l, 0, None))], one, "ya")[0], Y2)

    modes = lax.iota(jnp.int32, 128)
    part, offset = modes // 8, modes % 8
    order_j = ((((x + (part // 2) % 4) % 4) * 2 + (y_hi ^ (part % 2))) * 2 + (core ^ (part // 8))) * 8 + offset
    part, offset = modes // 16, modes % 16
    block = ((z + part // 2) % 4) * 2 + (y_lo ^ (part % 2))
    order_i = block * 16 + offset
    row = block * 4 + offset % 4
    picks = jnp.sum(jnp.where(row[:, None] == lax.iota(jnp.int32, 32)[None, :], out_modes[None, :], 0), axis=1)
    pick_d = ((picks[:, None] == order_j[None, :]) & (offset < 4)[:, None]).astype(BF)
    pick_k = (jnp.repeat(out_modes, 16)[:, None] == modes[None, :]).astype(BF)

    keep, out = assemble(
        fields, coefficients, derivative_tables(GLL), mass_weights.reshape(1, -1), metric,
        (order_j[:, None] == modes[None, :]).astype(BF), (order_i[:, None] == modes[None, :]).astype(BF),
        pick_k, pick_d, element(0, 0),
        [got[(U, 0, 0)], (xa2l, 0), (xa3r, 0), (ya, 0)],
        [got[(B, 0, 0)], (yb3, 0), (xb2r, 0), (xb2l, 0)],
    )
    pieces = whole_call(
        split_kernel, [jax.ShapeDtypeStruct((KS, 8, 128), BF)] * 8, "split", keep, send(out, CORE)
    )
    pieces = [pieces[0]] + [
        send(pieces[n], moves(lambda x, y, z, c, n=n: (x + n // 2, y + 2 * (n % 2), z, c))) for n in range(1, 8)
    ]
    pieces = pl.pallas_call(
        turn_kernel,
        out_shape=[jax.ShapeDtypeStruct((16, KS * 8), BF)] * 8,
        scratch_shapes=[pltpu.VMEM((KS * 8, 128), F32)],
        compiler_params=pltpu.CompilerParams(vmem_limit_bytes=VMEM),
        name="turn",
    )(*pieces)
    pieces = [pieces[0]] + [
        send(pieces[n], moves(lambda x, y, z, c, n=n: (x, y ^ (n % 2), z + n // 2, c))) for n in range(1, 8)
    ]
    tensor, diffusion = whole_call(
        finish_kernel,
        [jax.ShapeDtypeStruct((8, 16, 32), F32), jax.ShapeDtypeStruct((4, 8), F32)],
        "finish",
        *pieces,
    )
    return tensor.transpose(2, 0, 1), diffusion


def solution(mesh):
    return jax.shard_map(
        on_device,
        mesh=mesh,
        in_specs=(P("snap", None, "elem"), P("snap", None), P("elem"), P(None, None, "elem"), P()),
        out_specs=(P(None, "snap", "elem"), P("elem", "snap")),
        check_vma=False,
    )
```

time: 622 us -> 158 us (0.25)
  waiting for transfers between devices: 245 us -> 15.1 us
  local copies, waits for them, and re-layouts: 231 us -> 8.41 us
  matrix products: 84.6 us -> 0 us
  Pallas kernels: 0 us -> 73.5 us
  starting transfers between devices: 0.16 us -> 49.6 us
  blocking collectives: 19.7 us -> 0 us
  between operations: 15.1 us -> 1.02 us
  other arithmetic: 20.4 us -> 9.92 us
    mul x33 -> x0, local copies, waits for them, and re-layouts: 163 us -> none  [the longest x18 93 us: weighted_pairs(): term = left * right]
    reduce_scatter x2 -> x0, waiting for transfers between devices: 125 us -> none  [the longest x1 125 us: on_device(): lax.psum_scatter(lax.dot_general(coefficients, flat, (((0,), (0,)), ((),...]
    psum x1 -> x0, waiting for transfers between devices: 120 us -> none  [on_device(): chosen = lax.psum(picked.astype(jnp.bfloat16), 'snap')]
    dot_general x10 -> x0, matrix products: 84.6 us -> none  [the longest x1 32 us: on_device(): lax.dot_general(product, lax.all_gather(own_flat, 'snap', axis=0, tiled=T...]
    pallas_call x0 -> x17, Pallas kernels: none -> 73.5 us  [the longest x9 26.2 us: sums(): pl.pallas_call(kernel, grid_spec=pltpu.PrefetchScalarGridSpec(num_scalar_...]
    ppermute x0 -> x33, starting transfers between devices: none -> 49.6 us  [send(): return lax.ppermute(value, AXES, pairs)]
    convert_element_type x4 -> x0, local copies, waits for them, and re-layouts: 22.4 us -> none  [the longest x3 21.5 us: weighted_pairs(): left = paired[:, None, :, component, None, :].astype(jnp.float32)]
    unnamed x1 -> x0, blocking collectives: 19.7 us -> none
  transfers between devices with their start and end apart: 4 -> 33, of which waited for: 2 -> 6; matrix products, arithmetic and copies ran while one was open for 43% -> 8% of each run, Pallas kernels for 0% -> 25%
where the time goes in v1:
time: 158 us
  Pallas kernels  73.5 us (47%)
  starting transfers between devices  49.6 us (31%)
  waiting for transfers between devices  15.1 us (10%)
  other arithmetic  9.92 us (6%)
  local copies, waits for them, and re-layouts  8.41 us (5%)
    ppermute x33, starting transfers between devices, send(): return lax.ppermute(value, AXES, pairs)  49.6 us
    pallas_call x9, Pallas kernels, sums(): pl.pallas_call(kernel, grid_spec=pltpu.PrefetchScalarGridSpec(num_scalar_...  26.2 us
    pallas_call x1, Pallas kernels, assemble(): pl.pallas_call(kernel, grid_spec=pltpu.PrefetchScalarGridSpec(num_scalar_...  22.3 us
    pallas_call x4, Pallas kernels, partials(): pl.pallas_call(partials_kernel, grid_spec=pltpu.PrefetchScalarGridSpec(nu...  19.5 us
    ppermute x33, waiting for transfers between devices, send(): return lax.ppermute(value, AXES, pairs)  15.1 us
    unnamed x64, local copies, waits for them, and re-layouts  5.38 us
    pallas_call x2, Pallas kernels, whole_call(): pl.pallas_call(kernel, out_shape=outs, compiler_params=pltpu.CompilerPara...  3.6 us
  transfers between devices with their start and end apart: 33, of which 6 were waited for; matrix products, arithmetic and copies ran while one was open for 8% of the time, Pallas kernels for 25%

profile of v1, /device:TPU:0, one launch (start us, length us, event | category | flops | bytes accessed | tf_op | source)
XLA Modules:
  0.0 157.5 jit_solution(15747966308432366604)
XLA Ops:
  1.3 6.3 %part4.1 = bf16[6,3,128,512]{3,2,1,0:T(8,128)(2,1)} custom-call(s32[6]{0:T(128)} %stack.92.ids, s32[6]{0:T(128)} %constant.265.clone.halves, bf16[128,128]{1,0:T(8,128)(2,1)} %args_1_.4, bf16[6,128,8192]{2,1,0:T(8,128)(2,1)} %bitcast.19), custom_call_target="tpu_custom_call" | custom-call | flops 301989888 | bytes 4718592 | tf_op jit(solution)/shard_map/part4/pallas_call | solution.py:106
  8.8 4.8 %part3.1 = bf16[4,3,128,512]{3,2,1,0:T(8,128)(2,1)} custom-call(s32[4]{0:T(128)} %pad_add_fusion.ids, s32[4]{0:T(128)} %call_exported.1.halves, bf16[128,128]{1,0:T(8,128)(2,1)} %args_1_.4, bf16[6,128,8192]{2,1,0:T(8,128)(2,1)} %bitcast.20), custom_call_target="tpu_custom_call" | custom-call | flops 201326592 | bytes 3145728 | tf_op jit(solution)/shard_map/part3/pallas_call | solution.py:106
  14.7 4.2 %part1.1 = bf16[3,3,128,512]{3,2,1,0:T(8,128)(2,1)} custom-call(s32[3]{0:T(128)} %pad_add_fusion.2.ids, s32[3]{0:T(128)} %constant.262.clone.halves, bf16[128,128]{1,0:T(8,128)(2,1)} %args_1_.4, bf16[6,128,8192]{2,1,0:T(8,128)(2,1)} %bitcast.21), custom_call_target="tpu_custom_call" | custom-call | flops 150994944 | bytes 2359296 | tf_op jit(solution)/shard_map/part1/pallas_call | solution.py:106
  20.0 4.2 %part2.1 = bf16[3,3,128,512]{3,2,1,0:T(8,128)(2,1)} custom-call(s32[3]{0:T(128)} %pad_add_fusion.3.ids, s32[3]{0:T(128)} %call_exported.0.halves, bf16[128,128]{1,0:T(8,128)(2,1)} %args_1_.4, bf16[6,128,8192]{2,1,0:T(8,128)(2,1)} %bitcast.22), custom_call_target="tpu_custom_call" | custom-call | flops 150994944 | bytes 2359296 | tf_op jit(solution)/shard_map/part2/pallas_call | solution.py:106
  25.9 3.3 %xa1.1 = (bf16[1,3,128,512]{3,2,1,0:T(8,128)(2,1)}, bf16[1,3,128,512]{3,2,1,0:T(8,128)(2,1)}) custom-call(s32[2]{0:T(128)} %pad_add_fusion.1.ids, bf16[128,128]{1,0:T(8,128)(2,1)} %args_1_.4, bf16[6,128,8192]{2,1,0:T(8,128)(2,1)} %bitcast.23, bf16[6,128,8192]{2,1,0:T(8,128)(2,1)} %bitcast.24, ...), custom_call_target="tpu_custom_call" | custom-call | flops 100663296 | bytes 2359296 | tf_op jit(solution)/shard_map/xa1/pallas_call | solution.py:163
  33.6 2.2 %yb1.1 = bf16[1,3,128,512]{3,2,1,0:T(8,128)(2,1)} custom-call(s32[1]{0:T(128)} %bitcast.15.ids, bf16[128,128]{1,0:T(8,128)(2,1)} %args_1_.4, bf16[6,128,8192]{2,1,0:T(8,128)(2,1)} %bitcast.25, bf16[3,3,128,512]{3,2,1,0:T(8,128)(2,1)} %collective-permute-done.3.refs_2_.refs_3_.refs_1_), custom_call_target="tpu_custom_call" | custom-call | flops 50331648 | bytes 1179648 | tf_op jit(solution)/shard_map/yb1/pallas_call | solution.py:163
  35.7 3.3 %collective-permute-start.13 = (bf16[1,3,128,512]{3,2,1,0:T(8,128)(2,1)}, bf16[1,3,128,512]{3,2,1,0:T(8,128)(2,1)}, u32[]{:S(2)}, u32[]{:S(2)}) collective-permute-start(bf16[1,3,128,512]{3,2,1,0:T(8,128)(2,1)} %yb1.1), channel_id=1, source_target_pairs={{0,2},{1,3},{32,34},{33,35},{64,66},{65,67},{96,98},{97,99},{16,18... | collective-permute-start | bytes 1179656 | tf_op jit(solution)/shard_map/ppermute | solution.py:82
  39.6 3.5 %yb2.1 = bf16[2,3,128,512]{3,2,1,0:T(8,128)(2,1)} custom-call(s32[2]{0:T(128)} %pad_add_fusion.6.ids, bf16[128,128]{1,0:T(8,128)(2,1)} %args_1_.4, bf16[6,128,8192]{2,1,0:T(8,128)(2,1)} %bitcast.26, bf16[6,128,8192]{2,1,0:T(8,128)(2,1)} %bitcast.27, bf16[3,3,128,512]{3,2,1,0:T(8,128)(2,1)} %copy-done.1, bf16[3,3,128,512]{3,2,1,0:T(8,128)(2,1)} %copy-done.1), custom_call_target="tpu_custom_call" | custom-call | flops 100663296 | bytes 2359296 | tf_op jit(solution)/shard_map/yb2/pallas_call | solution.py:163
  43.9 3.2 %xa2.1 = (bf16[1,3,128,512]{3,2,1,0:T(8,128)(2,1)}, bf16[1,3,128,512]{3,2,1,0:T(8,128)(2,1)}) custom-call(s32[2]{0:T(128)} %pad_add_fusion.5.ids, bf16[128,128]{1,0:T(8,128)(2,1)} %args_1_.4, bf16[6,128,8192]{2,1,0:T(8,128)(2,1)} %bitcast.28, bf16[6,128,8192]{2,1,0:T(8,128)(2,1)} %bitcast.29, ...), custom_call_target="tpu_custom_call" | custom-call | flops 100663296 | bytes 2359296 | tf_op jit(solution)/shard_map/xa2/pallas_call | solution.py:163
  48.6 2.2 %yb3.1 = bf16[1,3,128,512]{3,2,1,0:T(8,128)(2,1)} custom-call(s32[1]{0:T(128)} %bitcast.17.ids, bf16[128,128]{1,0:T(8,128)(2,1)} %args_1_.4, bf16[6,128,8192]{2,1,0:T(8,128)(2,1)} %bitcast.30, bf16[3,3,128,512]{3,2,1,0:T(8,128)(2,1)} %copy-done.1), custom_call_target="tpu_custom_call" | custom-call | flops 50331648 | bytes 1179648 | tf_op jit(solution)/shard_map/yb3/pallas_call | solution.py:163
  50.8 3.1 %collective-permute-start.11 = (bf16[1,3,128,512]{3,2,1,0:T(8,128)(2,1)}, bf16[1,3,128,512]{3,2,1,0:T(8,128)(2,1)}, u32[]{:S(2)}, u32[]{:S(2)}) collective-permute-start(bf16[1,3,128,512]{3,2,1,0:T(8,128)(2,1)} %yb3.1), channel_id=1, source_target_pairs={{0,2},{1,3},{32,34},{33,35},{64,66},{65,67},{96,98},{97,99},{16,18... | collective-permute-start | bytes 1179656 | tf_op jit(solution)/shard_map/ppermute | solution.py:82
  53.9 3.5 %xa3.1 = (bf16[1,3,128,512]{3,2,1,0:T(8,128)(2,1)}, bf16[1,3,128,512]{3,2,1,0:T(8,128)(2,1)}) custom-call(s32[2]{0:T(128)} %pad_add_fusion.7.ids, bf16[128,128]{1,0:T(8,128)(2,1)} %args_1_.4, bf16[6,128,8192]{2,1,0:T(8,128)(2,1)} %bitcast.31, bf16[6,128,8192]{2,1,0:T(8,128)(2,1)} %bitcast.32, ...), custom_call_target="tpu_custom_call" | custom-call | flops 100663296 | bytes 3145728 | tf_op jit(solution)/shard_map/xa3/pallas_call | solution.py:163
  57.4 3.0 %collective-permute-start.8 = (bf16[1,3,128,512]{3,2,1,0:T(8,128)(2,1)}, bf16[1,3,128,512]{3,2,1,0:T(8,128)(2,1)}, u32[]{:S(2)}, u32[]{:S(2)}) collective-permute-start(bf16[1,3,128,512]{3,2,1,0:T(8,128)(2,1)} %get-tuple-element.37), channel_id=1, source_target_pairs={{0,12},{1,13},{32,44},{33,45},{64,76},{65,77},{96,108},{97,109},{1... | collective-permute-start | bytes 1179656 | tf_op jit(solution)/shard_map/ppermute | solution.py:82
  64.6 2.3 %xb1.1 = (bf16[1,3,64,512]{3,2,1,0:T(8,128)(2,1)}, bf16[1,3,64,512]{3,2,1,0:T(8,128)(2,1)}) custom-call(s32[1]{0:T(128)} %bitcast.14.ids, bf16[128,128]{1,0:T(8,128)(2,1)} %args_1_.4, bf16[6,128,8192]{2,1,0:T(8,128)(2,1)} %bitcast.33, bf16[6,3,128,512]{3,2,1,0:T(8,128)(2,1)} %copy-done, bf16[1,3,128,512]{3,2,1,0:T(8,128)(2,1)} %collective-permute-done.13.refs_2_), custom_call_target="tpu_custom_call" | custom-call | flops 50331648 | bytes 1572864 | tf_op jit(solution)/shard_map/xb1/pallas_call | solution.py:163
  66.9 3.2 %collective-permute-start.15 = (bf16[1,3,64,512]{3,2,1,0:T(8,128)(2,1)}, bf16[1,3,64,512]{3,2,1,0:T(8,128)(2,1)S(1)}, u32[]{:S(2)}, u32[]{:S(2)}) collective-permute-start(bf16[1,3,64,512]{3,2,1,0:T(8,128)(2,1)} %get-tuple-element.39), channel_id=1, source_target_pairs={{0,12},{1,13},{32,44},{33,45},{64,76},{65,77},{96,108},{97,109},{1... | collective-permute-start | bytes 589832 | tf_op jit(solution)/shard_map/ppermute | solution.py:82
  71.2 2.5 %ya.1 = bf16[1,3,128,512]{3,2,1,0:T(8,128)(2,1)} custom-call(s32[1]{0:T(128)} %bitcast.17.ids, bf16[128,128]{1,0:T(8,128)(2,1)} %args_1_.4, bf16[6,128,8192]{2,1,0:T(8,128)(2,1)} %bitcast.34, bf16[6,3,128,512]{3,2,1,0:T(8,128)(2,1)} %copy-done, bf16[1,3,128,512]{3,2,1,0:T(8,128)(2,1)} %copy-done.4, bf16[1,3,128,512]{3,2,1,0:T(8,128)(2,1)} %collective-permute-done.8.refs_3_), custom_call_target="tpu_custom_call" | custom-call | flops 50331648 | bytes 1966080 | tf_op jit(solution)/shard_map/ya/pallas_call | solution.py:163
  76.9 3.6 %xb2.1 = (bf16[1,3,128,512]{3,2,1,0:T(8,128)(2,1)}, bf16[1,3,128,512]{3,2,1,0:T(8,128)(2,1)}) custom-call(s32[2]{0:T(128)} %pad_add_fusion.4.ids, bf16[128,128]{1,0:T(8,128)(2,1)} %args_1_.4, bf16[6,128,8192]{2,1,0:T(8,128)(2,1)} %bitcast.35, bf16[6,128,8192]{2,1,0:T(8,128)(2,1)} %bitcast.36, bf16[6,3,128,512]{3,2,1,0:T(8,128)(2,1)} %copy-done, ...), custom_call_target="tpu_custom_call" | custom-call | flops 100663296 | bytes 3932160 | tf_op jit(solution)/shard_map/xb2/pallas_call | solution.py:163
  80.7 3.2 %collective-permute-start.17 = (bf16[1,3,128,512]{3,2,1,0:T(8,128)(2,1)}, bf16[1,3,128,512]{3,2,1,0:T(8,128)(2,1)S(1)}, u32[]{:S(2)}, u32[]{:S(2)}) collective-permute-start(bf16[1,3,128,512]{3,2,1,0:T(8,128)(2,1)} %get-tuple-element.41), channel_id=1, source_target_pairs={{0,12},{1,13},{32,44},{33,45},{64,76},{65,77},{96,108},{97,109},{1... | collective-permute-start | bytes 1179656 | tf_op jit(solution)/shard_map/ppermute | solution.py:82
  85.5 6.1 %collective-permute-done.16.args_17_ = bf16[1,3,128,512]{3,2,1,0:T(8,128)(2,1)S(1)} collective-permute-done((bf16[1,3,128,512]{3,2,1,0:T(8,128)(2,1)}, bf16[1,3,128,512]{3,2,1,0:T(8,128)(2,1)S(1)}, u32[]{:S(2)}, u32[]{:S(2)}) %collective-permute-start.16) | collective-permute-done | bytes 393248 | tf_op jit(solution)/shard_map/ppermute | solution.py:82
  92.5 22.3 %assemble.1 = (bf16[8,34,8,128]{3,2,1,0:T(8,128)(2,1)}, bf16[8,34,8,128]{3,2,1,0:T(8,128)(2,1)}) custom-call(s32[1]{0:T(128)} %bitcast.args_0_, bf16[128,128]{1,0:T(8,128)(2,1)} %args_1_.4, bf16[512,1536]{1,0:T(8,128)(2,1)} %constant.267.args_2_, f32[1,8192]{1,0:T(1,128)} %bitcast.40, f32[3,3,8192]{2,1,0:T(4,128)} %args_4_.4, ...), custom_call_target="tpu_custom_call" | custom-call | flops 10000000000 | bytes 10000000 | tf_op jit(solution)/shard_map/assemble/pallas_call | solution.py:255
  114.8 2.2 %collective-permute-done.18.got_ref = bf16[8,34,8,128]{3,2,1,0:T(8,128)(2,1)S(1)} collective-permute-done((bf16[8,34,8,128]{3,2,1,0:T(8,128)(2,1)}, bf16[8,34,8,128]{3,2,1,0:T(8,128)(2,1)S(1)}, u32[]{:S(2)}, u32[]{:S(2)}) %collective-permute-start.18) | collective-permute-done | bytes 557088 | tf_op jit(solution)/shard_map/ppermute | solution.py:82
  117.8 2.1 %split.1 = (bf16[34,8,128]{2,1,0:T(8,128)(2,1)}, bf16[34,8,128]{2,1,0:T(8,128)(2,1)}, bf16[34,8,128]{2,1,0:T(8,128)(2,1)}, bf16[34,8,128]{2,1,0:T(8,128)(2,1)}, ...) custom-call(bf16[8,34,8,128]{3,2,1,0:T(8,128)(2,1)} %get-tuple-eleme, ...), custom_call_target="tpu_custom_call" | custom-call | tf_op jit(solution)/shard_map/split/pallas_call | solution.py:290
  121.0 3.2 %collective-permute-start.21 = (bf16[34,8,128]{2,1,0:T(8,128)(2,1)}, bf16[34,8,128]{2,1,0:T(8,128)(2,1)S(1)}, u32[]{:S(2)}, u32[]{:S(2)}) collective-permute-start(bf16[34,8,128]{2,1,0:T(8,128)(2,1)} %get-tuple-element.47), channel_id=1, source_target_pairs={{0,6},{1,7},{32,38},{33,39},{64,70},{65,71},{96,102},{97,103},{16,... | collective-permute-start | bytes 208904 | tf_op jit(solution)/shard_map/ppermute | solution.py:82
  124.2 3.3 %collective-permute-start.22 = (bf16[34,8,128]{2,1,0:T(8,128)(2,1)}, bf16[34,8,128]{2,1,0:T(8,128)(2,1)S(1)}, u32[]{:S(2)}, u32[]{:S(2)}) collective-permute-start(bf16[34,8,128]{2,1,0:T(8,128)(2,1)} %get-tuple-element.48), channel_id=1, source_target_pairs={{0,8},{1,9},{32,40},{33,41},{64,72},{65,73},{96,104},{97,105},{16,... | collective-permute-start | bytes 208904 | tf_op jit(solution)/shard_map/ppermute | solution.py:82
  128.4 2.1 %collective-permute-start.24 = (bf16[34,8,128]{2,1,0:T(8,128)(2,1)}, bf16[34,8,128]{2,1,0:T(8,128)(2,1)S(1)}, u32[]{:S(2)}, u32[]{:S(2)}) collective-permute-start(bf16[34,8,128]{2,1,0:T(8,128)(2,1)} %get-tuple-element.50), channel_id=1, source_target_pairs={{0,12},{1,13},{32,44},{33,45},{64,76},{65,77},{96,108},{97,109},{1... | collective-permute-start | bytes 208904 | tf_op jit(solution)/shard_map/ppermute | solution.py:82
  130.5 3.6 %collective-permute-start.25 = (bf16[34,8,128]{2,1,0:T(8,128)(2,1)}, bf16[34,8,128]{2,1,0:T(8,128)(2,1)S(1)}, u32[]{:S(2)}, u32[]{:S(2)}) collective-permute-start(bf16[34,8,128]{2,1,0:T(8,128)(2,1)} %get-tuple-element.51), channel_id=1, source_target_pairs={{0,14},{1,15},{32,46},{33,47},{64,78},{65,79},{96,110},{97,111},{1... | collective-permute-start | bytes 208904 | tf_op jit(solution)/shard_map/ppermute | solution.py:82
  134.0 2.2 %collective-permute-done.23.refs_5_ = bf16[34,8,128]{2,1,0:T(8,128)(2,1)S(1)} collective-permute-done((bf16[34,8,128]{2,1,0:T(8,128)(2,1)}, bf16[34,8,128]{2,1,0:T(8,128)(2,1)S(1)}, u32[]{:S(2)}, u32[]{:S(2)}) %collective-permute-start.23) | collective-permute-done | bytes 69664 | tf_op jit(solution)/shard_map/ppermute | solution.py:82
  138.0 1.9 %turn.1 = (bf16[16,272]{1,0:T(8,128)(2,1)}, bf16[16,272]{1,0:T(8,128)(2,1)}, bf16[16,272]{1,0:T(8,128)(2,1)}, bf16[16,272]{1,0:T(8,128)(2,1)}, bf16[16,272]{1,0:...) custom-call(bf16[34,8,128]{2,1,0:T(8,128)(2,1)} %get-tuple-element.44.refs_0_, ...), custom_call_target="tpu_custom_call" | custom-call | tf_op jit(solution)/shard_map/turn/pallas_call | solution.py:397
  141.0 1.9 %collective-permute-start.27 = (bf16[16,272]{1,0:T(8,128)(2,1)}, bf16[16,272]{1,0:T(8,128)(2,1)S(1)}, u32[]{:S(2)}, u32[]{:S(2)}) collective-permute-start(bf16[16,272]{1,0:T(8,128)(2,1)} %get-tuple-element.54), channel_id=1, source_target_pairs={{0,32},{1,33},{32,64},{33,65},{64,96},{65,97},{96,0},{97,1},{16,48... | collective-permute-start | bytes 26120 | tf_op jit(solution)/shard_map/ppermute | solution.py:82
  142.9 2.4 %collective-permute-start.28 = (bf16[16,272]{1,0:T(8,128)(2,1)}, bf16[16,272]{1,0:T(8,128)(2,1)S(1)}, u32[]{:S(2)}, u32[]{:S(2)}) collective-permute-start(bf16[16,272]{1,0:T(8,128)(2,1)} %get-tuple-element.55), channel_id=1, source_target_pairs={{0,48},{1,49},{32,80},{33,81},{64,112},{65,113},{96,16},{97,17},{1... | collective-permute-start | bytes 26120 | tf_op jit(solution)/shard_map/ppermute | solution.py:82
  146.9 2.3 %collective-permute-start.30 = (bf16[16,272]{1,0:T(8,128)(2,1)}, bf16[16,272]{1,0:T(8,128)(2,1)S(1)}, u32[]{:S(2)}, u32[]{:S(2)}) collective-permute-start(bf16[16,272]{1,0:T(8,128)(2,1)} %get-tuple-element.57), channel_id=1, source_target_pairs={{0,80},{1,81},{32,112},{33,113},{64,16},{65,17},{96,48},{97,49},{1... | collective-permute-start | bytes 26120 | tf_op jit(solution)/shard_map/ppermute | solution.py:82
  153.2 2.1 %collective-permute-done.32.refs_7_ = bf16[16,272]{1,0:T(8,128)(2,1)S(1)} collective-permute-done((bf16[16,272]{1,0:T(8,128)(2,1)}, bf16[16,272]{1,0:T(8,128)(2,1)S(1)}, u32[]{:S(2)}, u32[]{:S(2)}) %collective-permute-start.32) | collective-permute-done | bytes 8736 | tf_op jit(solution)/shard_map/ppermute | solution.py:82
  (136 shorter events, 37.3 us)
Async XLA Ops:
  7.6 55.5 %collective-permute-start = (bf16[6,3,128,512]{3,2,1,0:T(8,128)(2,1)}, bf16[6,3,128,512]{3,2,1,0:T(8,128)(2,1)S(1)}, u32[]{:S(2)}, u32[]{:S(2)}) collective-permute-start(bf16[6,3,128,512]{3,2,1,0:T(8,128)(2,1)} %part4.1), channel_id=1, source_target_pairs={{0,1},{1,0},{32,33},{33,32},{64,65},{65,64},{96,97},{97,96},{16,17... | collective-permute-start | bytes 7077896 | tf_op jit(solution)/shard_map/ppermute | solution.py:82
  13.6 29.5 %collective-permute-start.1 = (bf16[4,3,128,512]{3,2,1,0:T(8,128)(2,1)}, bf16[4,3,128,512]{3,2,1,0:T(8,128)(2,1)}, u32[]{:S(2)}, u32[]{:S(2)}) collective-permute-start(bf16[4,3,128,512]{3,2,1,0:T(8,128)(2,1)} %part3.1), channel_id=1, source_target_pairs={{0,1},{1,0},{32,33},{33,32},{64,65},{65,64},{96,97},{97,96},{16,17... | collective-permute-start | bytes 4718600 | tf_op jit(solution)/shard_map/ppermute | solution.py:82
  18.9 6.9 %collective-permute-start.3 = (bf16[3,3,128,512]{3,2,1,0:T(8,128)(2,1)}, bf16[3,3,128,512]{3,2,1,0:T(8,128)(2,1)}, u32[]{:S(2)}, u32[]{:S(2)}) collective-permute-start(bf16[3,3,128,512]{3,2,1,0:T(8,128)(2,1)} %part1.1), channel_id=1, source_target_pairs={{0,1},{1,0},{32,33},{33,32},{64,65},{65,64},{96,97},{97,96},{16,17... | collective-permute-start | bytes 3538952 | tf_op jit(solution)/shard_map/ppermute | solution.py:82
  24.3 11.5 %collective-permute-start.10 = (bf16[3,3,128,512]{3,2,1,0:T(8,128)(2,1)}, bf16[3,3,128,512]{3,2,1,0:T(8,128)(2,1)S(1)}, u32[]{:S(2)}, u32[]{:S(2)}) collective-permute-start(bf16[3,3,128,512]{3,2,1,0:T(8,128)(2,1)} %part2.1), channel_id=1, source_target_pairs={{0,1},{1,0},{32,33},{33,32},{64,65},{65,64},{96,97},{97,96},{16,17... | collective-permute-start | bytes 3538952 | tf_op jit(solution)/shard_map/ppermute | solution.py:82
  29.1 18.0 %collective-permute-start.4 = (bf16[1,3,128,512]{3,2,1,0:T(8,128)(2,1)}, bf16[1,3,128,512]{3,2,1,0:T(8,128)(2,1)}, u32[]{:S(2)}, u32[]{:S(2)}) collective-permute-start(bf16[1,3,128,512]{3,2,1,0:T(8,128)(2,1)} %get-tuple-element.33), channel_id=1, source_target_pairs={{0,4},{1,5},{32,36},{33,37},{64,68},{65,69},{96,100},{97,101},{16,... | collective-permute-start | bytes 1179656 | tf_op jit(solution)/shard_map/ppermute | solution.py:82
  31.9 18.9 %collective-permute-start.5 = (bf16[1,3,128,512]{3,2,1,0:T(8,128)(2,1)}, bf16[1,3,128,512]{3,2,1,0:T(8,128)(2,1)}, u32[]{:S(2)}, u32[]{:S(2)}) collective-permute-start(bf16[1,3,128,512]{3,2,1,0:T(8,128)(2,1)} %get-tuple-element.34), channel_id=1, source_target_pairs={{0,12},{1,13},{32,44},{33,45},{64,76},{65,77},{96,108},{97,109},{1... | collective-permute-start | bytes 1179656 | tf_op jit(solution)/shard_map/ppermute | solution.py:82
  35.7 21.7 %collective-permute-start.13 = (bf16[1,3,128,512]{3,2,1,0:T(8,128)(2,1)}, bf16[1,3,128,512]{3,2,1,0:T(8,128)(2,1)}, u32[]{:S(2)}, u32[]{:S(2)}) collective-permute-start(bf16[1,3,128,512]{3,2,1,0:T(8,128)(2,1)} %yb1.1), channel_id=1, source_target_pairs={{0,2},{1,3},{32,34},{33,35},{64,66},{65,67},{96,98},{97,99},{16,18... | collective-permute-start | bytes 1179656 | tf_op jit(solution)/shard_map/ppermute | solution.py:82
  43.1 30.6 %collective-permute-start.12 = (bf16[2,3,128,512]{3,2,1,0:T(8,128)(2,1)}, bf16[2,3,128,512]{3,2,1,0:T(8,128)(2,1)S(1)}, u32[]{:S(2)}, u32[]{:S(2)}) collective-permute-start(bf16[2,3,128,512]{3,2,1,0:T(8,128)(2,1)} %yb2.1), channel_id=1, source_target_pairs={{0,2},{1,3},{32,34},{33,35},{64,66},{65,67},{96,98},{97,99},{16,18... | collective-permute-start | bytes 2359304 | tf_op jit(solution)/shard_map/ppermute | solution.py:82
  47.2 19.7 %collective-permute-start.7 = (bf16[1,3,128,512]{3,2,1,0:T(8,128)(2,1)}, bf16[1,3,128,512]{3,2,1,0:T(8,128)(2,1)S(1)}, u32[]{:S(2)}, u32[]{:S(2)}) collective-permute-start(bf16[1,3,128,512]{3,2,1,0:T(8,128)(2,1)} %get-tuple-element.36), channel_id=1, source_target_pairs={{0,4},{1,5},{32,36},{33,37},{64,68},{65,69},{96,100},{97,101},{16,... | collective-permute-start | bytes 1179656 | tf_op jit(solution)/shard_map/ppermute | solution.py:82
  50.8 30.0 %collective-permute-start.11 = (bf16[1,3,128,512]{3,2,1,0:T(8,128)(2,1)}, bf16[1,3,128,512]{3,2,1,0:T(8,128)(2,1)}, u32[]{:S(2)}, u32[]{:S(2)}) collective-permute-start(bf16[1,3,128,512]{3,2,1,0:T(8,128)(2,1)} %yb3.1), channel_id=1, source_target_pairs={{0,2},{1,3},{32,34},{33,35},{64,66},{65,67},{96,98},{97,99},{16,18... | collective-permute-start | bytes 1179656 | tf_op jit(solution)/shard_map/ppermute | solution.py:82
  57.4 13.5 %collective-permute-start.8 = (bf16[1,3,128,512]{3,2,1,0:T(8,128)(2,1)}, bf16[1,3,128,512]{3,2,1,0:T(8,128)(2,1)}, u32[]{:S(2)}, u32[]{:S(2)}) collective-permute-start(bf16[1,3,128,512]{3,2,1,0:T(8,128)(2,1)} %get-tuple-element.37), channel_id=1, source_target_pairs={{0,12},{1,13},{32,44},{33,45},{64,76},{65,77},{96,108},{97,109},{1... | collective-permute-start | bytes 1179656 | tf_op jit(solution)/shard_map/ppermute | solution.py:82
  66.9 8.7 %collective-permute-start.14 = (bf16[1,3,64,512]{3,2,1,0:T(8,128)(2,1)}, bf16[1,3,64,512]{3,2,1,0:T(8,128)(2,1)S(1)}, u32[]{:S(2)}, u32[]{:S(2)}) collective-permute-start(bf16[1,3,64,512]{3,2,1,0:T(8,128)(2,1)} %get-tuple-element.38), channel_id=1, source_target_pairs={{0,4},{1,5},{32,36},{33,37},{64,68},{65,69},{96,100},{97,101},{16,... | collective-permute-start | bytes 589832 | tf_op jit(solution)/shard_map/ppermute | solution.py:82
  66.9 8.9 %collective-permute-start.15 = (bf16[1,3,64,512]{3,2,1,0:T(8,128)(2,1)}, bf16[1,3,64,512]{3,2,1,0:T(8,128)(2,1)S(1)}, u32[]{:S(2)}, u32[]{:S(2)}) collective-permute-start(bf16[1,3,64,512]{3,2,1,0:T(8,128)(2,1)} %get-tuple-element.39), channel_id=1, source_target_pairs={{0,12},{1,13},{32,44},{33,45},{64,76},{65,77},{96,108},{97,109},{1... | collective-permute-start | bytes 589832 | tf_op jit(solution)/shard_map/ppermute | solution.py:82
  70.9 14.6 %collective-permute-start.2 = (bf16[1,3,128,512]{3,2,1,0:T(8,128)(2,1)S(1)}, bf16[1,3,128,512]{3,2,1,0:T(8,128)(2,1)S(1)}, u32[]{:S(2)}, u32[]{:S(2)}) collective-permute-start(bf16[1,3,128,512]{3,2,1,0:T(8,128)(2,1)S(1)} %copy-done.25), channel_id=1, source_target_pairs={{0,12},{1,13},{32,44},{33,45},{64,76},{65,77},{96,108},{97,109},{1... | collective-permute-start | bytes 1179656 | tf_op jit(solution)/shard_map/ppermute | solution.py:82
  73.7 11.8 %collective-permute-start.6 = (bf16[1,3,128,512]{3,2,1,0:T(8,128)(2,1)S(1)}, bf16[1,3,128,512]{3,2,1,0:T(8,128)(2,1)S(1)}, u32[]{:S(2)}, u32[]{:S(2)}) collective-permute-start(bf16[1,3,128,512]{3,2,1,0:T(8,128)(2,1)S(1)} %copy-done.26), channel_id=1, source_target_pairs={{0,4},{1,5},{32,36},{33,37},{64,68},{65,69},{96,100},{97,101},{16,... | collective-permute-start | bytes 1179656 | tf_op jit(solution)/shard_map/ppermute | solution.py:82
  75.5 10.0 %collective-permute-start.9 = (bf16[1,3,128,512]{3,2,1,0:T(8,128)(2,1)}, bf16[1,3,128,512]{3,2,1,0:T(8,128)(2,1)S(1)}, u32[]{:S(2)}, u32[]{:S(2)}) collective-permute-start(bf16[1,3,128,512]{3,2,1,0:T(8,128)(2,1)} %ya.1), channel_id=1, source_target_pairs={{0,2},{1,3},{32,34},{33,35},{64,66},{65,67},{96,98},{97,99},{16,18... | collective-permute-start | bytes 1179656 | tf_op jit(solution)/shard_map/ppermute | solution.py:82
  80.5 11.1 %collective-permute-start.16 = (bf16[1,3,128,512]{3,2,1,0:T(8,128)(2,1)}, bf16[1,3,128,512]{3,2,1,0:T(8,128)(2,1)S(1)}, u32[]{:S(2)}, u32[]{:S(2)}) collective-permute-start(bf16[1,3,128,512]{3,2,1,0:T(8,128)(2,1)} %get-tuple-element.40), channel_id=1, source_target_pairs={{0,4},{1,5},{32,36},{33,37},{64,68},{65,69},{96,100},{97,101},{16,... | collective-permute-start | bytes 1179656 | tf_op jit(solution)/shard_map/ppermute | solution.py:82
  80.7 10.9 %collective-permute-start.17 = (bf16[1,3,128,512]{3,2,1,0:T(8,128)(2,1)}, bf16[1,3,128,512]{3,2,1,0:T(8,128)(2,1)S(1)}, u32[]{:S(2)}, u32[]{:S(2)}) collective-permute-start(bf16[1,3,128,512]{3,2,1,0:T(8,128)(2,1)} %get-tuple-element.41), channel_id=1, source_target_pairs={{0,12},{1,13},{32,44},{33,45},{64,76},{65,77},{96,108},{97,109},{1... | collective-permute-start | bytes 1179656 | tf_op jit(solution)/shard_map/ppermute | solution.py:82
  119.8 8.5 %collective-permute-start.19 = (bf16[34,8,128]{2,1,0:T(8,128)(2,1)}, bf16[34,8,128]{2,1,0:T(8,128)(2,1)S(1)}, u32[]{:S(2)}, u32[]{:S(2)}) collective-permute-start(bf16[34,8,128]{2,1,0:T(8,128)(2,1)} %get-tuple-element.45), channel_id=1, source_target_pairs={{0,2},{1,3},{32,34},{33,35},{64,66},{65,67},{96,98},{97,99},{16,18... | collective-permute-start | bytes 208904 | tf_op jit(solution)/shard_map/ppermute | solution.py:82
  120.8 9.6 %collective-permute-start.20 = (bf16[34,8,128]{2,1,0:T(8,128)(2,1)}, bf16[34,8,128]{2,1,0:T(8,128)(2,1)S(1)}, u32[]{:S(2)}, u32[]{:S(2)}) collective-permute-start(bf16[34,8,128]{2,1,0:T(8,128)(2,1)} %get-tuple-element.46), channel_id=1, source_target_pairs={{0,4},{1,5},{32,36},{33,37},{64,68},{65,69},{96,100},{97,101},{16,... | collective-permute-start | bytes 208904 | tf_op jit(solution)/shard_map/ppermute | solution.py:82
  121.0 13.0 %collective-permute-start.21 = (bf16[34,8,128]{2,1,0:T(8,128)(2,1)}, bf16[34,8,128]{2,1,0:T(8,128)(2,1)S(1)}, u32[]{:S(2)}, u32[]{:S(2)}) collective-permute-start(bf16[34,8,128]{2,1,0:T(8,128)(2,1)} %get-tuple-element.47), channel_id=1, source_target_pairs={{0,6},{1,7},{32,38},{33,39},{64,70},{65,71},{96,102},{97,103},{16,... | collective-permute-start | bytes 208904 | tf_op jit(solution)/shard_map/ppermute | solution.py:82
  124.2 9.8 %collective-permute-start.22 = (bf16[34,8,128]{2,1,0:T(8,128)(2,1)}, bf16[34,8,128]{2,1,0:T(8,128)(2,1)S(1)}, u32[]{:S(2)}, u32[]{:S(2)}) collective-permute-start(bf16[34,8,128]{2,1,0:T(8,128)(2,1)} %get-tuple-element.48), channel_id=1, source_target_pairs={{0,8},{1,9},{32,40},{33,41},{64,72},{65,73},{96,104},{97,105},{16,... | collective-permute-start | bytes 208904 | tf_op jit(solution)/shard_map/ppermute | solution.py:82
  127.5 8.8 %collective-permute-start.23 = (bf16[34,8,128]{2,1,0:T(8,128)(2,1)}, bf16[34,8,128]{2,1,0:T(8,128)(2,1)S(1)}, u32[]{:S(2)}, u32[]{:S(2)}) collective-permute-start(bf16[34,8,128]{2,1,0:T(8,128)(2,1)} %get-tuple-element.49), channel_id=1, source_target_pairs={{0,10},{1,11},{32,42},{33,43},{64,74},{65,75},{96,106},{97,107},{1... | collective-permute-start | bytes 208904 | tf_op jit(solution)/shard_map/ppermute | solution.py:82
  128.4 7.9 %collective-permute-start.24 = (bf16[34,8,128]{2,1,0:T(8,128)(2,1)}, bf16[34,8,128]{2,1,0:T(8,128)(2,1)S(1)}, u32[]{:S(2)}, u32[]{:S(2)}) collective-permute-start(bf16[34,8,128]{2,1,0:T(8,128)(2,1)} %get-tuple-element.50), channel_id=1, source_target_pairs={{0,12},{1,13},{32,44},{33,45},{64,76},{65,77},{96,108},{97,109},{1... | collective-permute-start | bytes 208904 | tf_op jit(solution)/shard_map/ppermute | solution.py:82
  130.5 6.9 %collective-permute-start.25 = (bf16[34,8,128]{2,1,0:T(8,128)(2,1)}, bf16[34,8,128]{2,1,0:T(8,128)(2,1)S(1)}, u32[]{:S(2)}, u32[]{:S(2)}) collective-permute-start(bf16[34,8,128]{2,1,0:T(8,128)(2,1)} %get-tuple-element.51), channel_id=1, source_target_pairs={{0,14},{1,15},{32,46},{33,47},{64,78},{65,79},{96,110},{97,111},{1... | collective-permute-start | bytes 208904 | tf_op jit(solution)/shard_map/ppermute | solution.py:82
  139.9 9.3 %collective-permute-start.26 = (bf16[16,272]{1,0:T(8,128)(2,1)}, bf16[16,272]{1,0:T(8,128)(2,1)S(1)}, u32[]{:S(2)}, u32[]{:S(2)}) collective-permute-start(bf16[16,272]{1,0:T(8,128)(2,1)} %get-tuple-element.53), channel_id=1, source_target_pairs={{0,16},{1,17},{32,48},{33,49},{64,80},{65,81},{96,112},{97,113},{1... | collective-permute-start | bytes 26120 | tf_op jit(solution)/shard_map/ppermute | solution.py:82
  141.0 9.6 %collective-permute-start.27 = (bf16[16,272]{1,0:T(8,128)(2,1)}, bf16[16,272]{1,0:T(8,128)(2,1)S(1)}, u32[]{:S(2)}, u32[]{:S(2)}) collective-permute-start(bf16[16,272]{1,0:T(8,128)(2,1)} %get-tuple-element.54), channel_id=1, source_target_pairs={{0,32},{1,33},{32,64},{33,65},{64,96},{65,97},{96,0},{97,1},{16,48... | collective-permute-start | bytes 26120 | tf_op jit(solution)/shard_map/ppermute | solution.py:82
  142.9 9.0 %collective-permute-start.28 = (bf16[16,272]{1,0:T(8,128)(2,1)}, bf16[16,272]{1,0:T(8,128)(2,1)S(1)}, u32[]{:S(2)}, u32[]{:S(2)}) collective-permute-start(bf16[16,272]{1,0:T(8,128)(2,1)} %get-tuple-element.55), channel_id=1, source_target_pairs={{0,48},{1,49},{32,80},{33,81},{64,112},{65,113},{96,16},{97,17},{1... | collective-permute-start | bytes 26120 | tf_op jit(solution)/shard_map/ppermute | solution.py:82
  145.3 6.7 %collective-permute-start.29 = (bf16[16,272]{1,0:T(8,128)(2,1)}, bf16[16,272]{1,0:T(8,128)(2,1)S(1)}, u32[]{:S(2)}, u32[]{:S(2)}) collective-permute-start(bf16[16,272]{1,0:T(8,128)(2,1)} %get-tuple-element.56), channel_id=1, source_target_pairs={{0,64},{1,65},{32,96},{33,97},{64,0},{65,1},{96,32},{97,33},{16,80... | collective-permute-start | bytes 26120 | tf_op jit(solution)/shard_map/ppermute | solution.py:82
  146.9 6.3 %collective-permute-start.30 = (bf16[16,272]{1,0:T(8,128)(2,1)}, bf16[16,272]{1,0:T(8,128)(2,1)S(1)}, u32[]{:S(2)}, u32[]{:S(2)}) collective-permute-start(bf16[16,272]{1,0:T(8,128)(2,1)} %get-tuple-element.57), channel_id=1, source_target_pairs={{0,80},{1,81},{32,112},{33,113},{64,16},{65,17},{96,48},{97,49},{1... | collective-permute-start | bytes 26120 | tf_op jit(solution)/shard_map/ppermute | solution.py:82
  149.2 4.0 %collective-permute-start.31 = (bf16[16,272]{1,0:T(8,128)(2,1)}, bf16[16,272]{1,0:T(8,128)(2,1)S(1)}, u32[]{:S(2)}, u32[]{:S(2)}) collective-permute-start(bf16[16,272]{1,0:T(8,128)(2,1)} %get-tuple-element.58), channel_id=1, source_target_pairs={{0,96},{1,97},{32,0},{33,1},{64,32},{65,33},{96,64},{97,65},{16,11... | collective-permute-start | bytes 26120 | tf_op jit(solution)/shard_map/ppermute | solution.py:82
  150.6 4.8 %collective-permute-start.32 = (bf16[16,272]{1,0:T(8,128)(2,1)}, bf16[16,272]{1,0:T(8,128)(2,1)S(1)}, u32[]{:S(2)}, u32[]{:S(2)}) collective-permute-start(bf16[16,272]{1,0:T(8,128)(2,1)} %get-tuple-element.59), channel_id=1, source_target_pairs={{0,112},{1,113},{32,16},{33,17},{64,48},{65,49},{96,80},{97,81},{1... | collective-permute-start | bytes 26120 | tf_op jit(solution)/shard_map/ppermute | solution.py:82
  (33 other events, 130.3 us)

commit v2 on v0

v2 whole, which is shorter than its diff:
```python
import math

import jax
import jax.numpy as jnp
import numpy as np
from jax import lax
from jax.experimental import pallas as pl
from jax.experimental.pallas import tpu as pltpu
from jax.sharding import PartitionSpec as P

GLL = 8
NPE = 512
AXES = ("elem", "snap")
BF = jnp.bfloat16
F32 = jnp.float32


def legendre_pair(value, points):
    before, current = (1.0, value)
    for degree in range(2, points):
        before, current = (
            current,
            ((2 * degree - 1) * value * current - (degree - 1) * before) / degree,
        )
    return (before, current)


def derivative_tables(points):
    degree = points - 1
    nodes = [math.cos(math.pi * index / degree) for index in range(points)]
    for sweep in range(100):
        updated = []
        for value in nodes:
            before, current = legendre_pair(value, points)
            updated.append(value - (value * current - before) / (points * current))
        nodes = updated
    abscissae = sorted(nodes)
    evaluated = [legendre_pair(value, points)[1] for value in abscissae]
    matrix = np.zeros((points, points))
    for first in range(points):
        for second in range(points):
            if first != second:
                matrix[first, second] = evaluated[first] / (
                    evaluated[second] * (abscissae[first] - abscissae[second])
                )
    matrix[0, 0] = -degree * (degree + 1) / 4.0
    matrix[degree, degree] = degree * (degree + 1) / 4.0
    identity = np.eye(points)
    stacked = np.concatenate(
        [
            np.kron(identity, np.kron(identity, matrix.T)),
            np.kron(identity, np.kron(matrix.T, identity)),
            np.kron(matrix.T, np.kron(identity, identity)),
        ],
        axis=1,
    )
    return jnp.asarray(stacked, jnp.float32).astype(jnp.bfloat16)


def place(x, y, z, core):
    return (z * 2 + y % 2) * 16 + (x * 2 + y // 2) * 2 + core


PLACES = [(x, y, z, core) for x in range(4) for y in range(4) for z in range(4) for core in range(2)]


def moves(shift):
    pairs = []
    for x, y, z, core in PLACES:
        nx, ny, nz, ncore = shift(x, y, z, core)
        pairs.append((place(x, y, z, core), place(nx % 4, ny % 4, nz % 4, ncore)))
    return pairs


CORE = moves(lambda x, y, z, c: (x, y, z, 1 - c))
FORWARD = moves(lambda x, y, z, c: (x + 1 - 2 * c, y, z, c))
BACK = moves(lambda x, y, z, c: (x - 1 + 2 * c, y, z, c))
Y2 = moves(lambda x, y, z, c: (x, y + 2, z, c))


def send(value, pairs, name):
    with jax.named_scope(name):
        return lax.ppermute(value, AXES, pairs)


ITEM = (3, 128, NPE)
ITEM_BYTES = 3 * 128 * NPE * 2
MIB = 1024 * 1024
TINY = pl.CostEstimate(flops=1, bytes_accessed=1, transcendentals=0)
TABLE = 16
TOKEN = (8, 128)


def cut(table, fields, wanted, name, coef=None, token=None):
    planes = 6 if coef is None else 7
    count = len(wanted)
    others = [array for array in (coef, token) if array is not None]

    def kernel(table_ref, fields_ref, coef_ref, *refs):
        outs, token_ref, sems = refs[:count], refs[count], refs[count + 1]
        copies = []
        for n, dx in enumerate(wanted):
            lanes = pl.ds(pl.multiple_of(table_ref[12 + dx] * 1024, 1024), 1024)
            for c in range(6):
                copies.append(
                    pltpu.make_async_copy(fields_ref.at[c, :, lanes], outs[n].at[0, c], sems.at[n * 6 + c])
                )
        for copy in copies:
            copy.start()
        token_ref[...] = jnp.zeros(TOKEN, F32)
        if coef is not None:
            outs[0][0, 6, :, :128] = coef_ref[...]
            outs[0][0, 6, :, 128:] = jnp.zeros((128, 896), BF)
        for copy in copies:
            copy.wait()

    return pl.pallas_call(
        kernel,
        grid_spec=pltpu.PrefetchScalarGridSpec(
            num_scalar_prefetch=1,
            grid=(1,),
            in_specs=[
                pl.BlockSpec(memory_space=pl.ANY),
                pl.BlockSpec(memory_space=pl.ANY) if coef is None else whole((128, 128)),
            ],
            out_specs=[whole((1, planes, 128, 1024))] * count + [whole(TOKEN)],
            scratch_shapes=[pltpu.SemaphoreType.DMA((6 * count,))],
        ),
        out_shape=[bf16(1, planes, 128, 1024)] * count + [jax.ShapeDtypeStruct(TOKEN, F32)],
        compiler_params=pltpu.CompilerParams(vmem_limit_bytes=16 * MIB),
        cost_estimate=TINY,
        name=name,
    )(table, fields, *others)


def own_spec(half, dx, dy):
    return pl.BlockSpec(ITEM, lambda i, table, *rest: (half, 0, table[dx * 2 + dy]))


def other_spec(half, dy):
    return pl.BlockSpec((1,) + ITEM, lambda i, table, *rest: (0, half, 0, table[8 + dy]))


def row_spec(array, row):
    return pl.BlockSpec((1,) + array.shape[1:], lambda i, *rest: (row, 0, 0, 0))


def whole(shape):
    return pl.BlockSpec(shape, lambda i, *rest: (0,) * len(shape))


def pin_kernel(*refs):
    refs[-1][...] = jnp.zeros(TOKEN, F32)


def pin(*arrays):
    return pl.pallas_call(
        pin_kernel,
        in_specs=[pl.BlockSpec(memory_space=pl.ANY)] * len(arrays),
        out_specs=pl.BlockSpec(memory_space=pltpu.VMEM),
        out_shape=jax.ShapeDtypeStruct(TOKEN, F32),
        compiler_params=pltpu.CompilerParams(vmem_limit_bytes=4 * MIB),
        cost_estimate=TINY,
        name="pin",
    )(*arrays)


def project(coef, own, other, c):
    rows = jnp.concatenate([own[c], other[0, c]], axis=0)
    return jnp.dot(coef, rows, preferred_element_type=F32)


def sums(shared, items, outs, name, before=(), coefs=None):
    table, fields, coef, chunks = shared
    operands, specs, plan = [], [], []
    for (half, dx, dy), adds in items:
        entry = []
        for array, spec in [(fields, own_spec(half, dx, dy)), (chunks[dx], other_spec(half, dy))] + [
            (array, row_spec(array, row)) for array, row in adds
        ]:
            entry.append(len(operands))
            operands.append(array)
            specs.append(spec)
        plan.append(entry)
    if coefs is None:
        first, first_specs = [coef], [whole((128, 256))]
    else:
        first = list(coefs)
        first_specs = [whole((128, 128)), pl.BlockSpec((1, 1, 128, 128), lambda i, table: (0, 6, 0, 0))]

    def kernel(table_ref, *refs):
        refs = refs[len(before) :]
        if coefs is None:
            rows = refs[0][...]
        else:
            rows = jnp.concatenate([refs[0][...].T, refs[1][0, 0].T], axis=1)
        refs = refs[len(first) :]
        ins, results = refs[: len(operands)], refs[len(operands) :]
        results[len(outs)][...] = jnp.zeros(TOKEN, F32)
        if coefs is not None:
            results[-1][...] = rows
        for number, group in enumerate(outs):
            for position, item in enumerate(group):
                own, other, *adds = plan[item]
                for c in range(3):
                    total = project(rows, ins[own], ins[other], c)
                    for add in adds:
                        total = total + ins[add][0, c].astype(F32)
                    results[number][position, c] = total.astype(BF)

    shapes = [bf16(len(group), *ITEM) for group in outs] + [jax.ShapeDtypeStruct(TOKEN, F32)]
    if coefs is not None:
        shapes.append(bf16(128, 256))
    return pl.pallas_call(
        kernel,
        grid_spec=pltpu.PrefetchScalarGridSpec(
            num_scalar_prefetch=1,
            grid=(1,),
            in_specs=[pl.BlockSpec(memory_space=pl.ANY)] * len(before) + first_specs + specs,
            out_specs=[whole(shape.shape) for shape in shapes],
        ),
        out_shape=shapes,
        compiler_params=pltpu.CompilerParams(vmem_limit_bytes=16 * MIB),
        cost_estimate=TINY,
        name=name,
    )(table, *before, *first, *operands)


KG = 8
BLOCKS = 32 // KG + 1


def assemble_kernel(counts, table, out_modes, token, coef_ref, tables_ref, weight_ref, metric_ref, *refs):
    fields_u, refs = refs[:2], refs[2:]
    fields_b, refs = refs[:2], refs[2:]
    adds_u, refs = refs[: counts[0]], refs[counts[0] :]
    adds_b, refs = refs[: counts[1]], refs[counts[1] :]
    out_ref, zt_ref, z_ref, g_ref, cb_ref, pick_k, pick_d = refs
    half_weight = 0.5 * weight_ref[...]

    columns = lax.broadcasted_iota(jnp.int32, (16, 128), 1)
    pick_d[...] = jnp.zeros((128, 128), F32)
    for k in range(32):
        hot = (columns == out_modes[k]).astype(F32)
        pick_k[k * 16 : k * 16 + 16, :] = hot.astype(BF)
        row = (k // 4) * 16 + k % 4
        pick_d[row : row + 1, :] = hot[:1]
    chosen_d = pick_d[...].astype(BF)

    coef = coef_ref[...]
    for a in range(3):
        u = project(coef, *fields_u, a)
        for ref in adds_u:
            u = u + ref[0, a].astype(F32)
        b = project(coef, *fields_b, a)
        for ref in adds_b:
            b = b + ref[0, a].astype(F32)
        for sign, z in ((0, u + b), (1, u - b)):
            zt_ref[1 - sign, a] = z.T.astype(BF)
            z = z.astype(BF)
            z_ref[sign, a * 128 : a * 128 + 128] = z
            cb_ref[sign, a] = (
                jnp.dot(pick_k[...], z, preferred_element_type=F32) * half_weight
            ).astype(BF)

    diffusion = None
    for sign in range(2):
        derived = jnp.dot(z_ref[sign], tables_ref[...], preferred_element_type=F32)
        for a in range(3):
            part = derived[a * 128 : a * 128 + 128]
            for b in range(3):
                grad = metric_ref[0, b : b + 1, :] * part[:, :NPE]
                grad = grad + metric_ref[1, b : b + 1, :] * part[:, NPE : 2 * NPE]
                grad = grad + metric_ref[2, b : b + 1, :] * part[:, 2 * NPE :]
                grad = grad.astype(BF)
                g_ref[sign, a, b] = grad
                picked = jnp.dot(chosen_d, grad, preferred_element_type=F32) * half_weight
                term = lax.dot_general(
                    grad, picked.astype(BF), (((1,), (1,)), ((), ())), preferred_element_type=F32
                )
                diffusion = term if diffusion is None else diffusion + term
    diffusion = diffusion.astype(BF).reshape(16, 8, 128)
    for elem in range(8):
        out_ref[elem, :, BLOCKS - 1] = diffusion
    group = lax.broadcasted_iota(jnp.int32, (128, 128), 1) // 16

    def rows_of(step, carry):
        total = None
        for sign in range(2):
            for b in range(3):
                pieces = []
                for t in range(KG):
                    start = pl.multiple_of((step * KG + t) * 16, 16)
                    product = None
                    for a in range(3):
                        picked = cb_ref[sign, a, pl.ds(start, 16), :][None]
                        term = g_ref[sign, a, b].reshape(8, 16, NPE) * picked
                        product = term if product is None else product + term
                    pieces.append(product.reshape(128, NPE))
                term = jnp.dot(jnp.concatenate(pieces, axis=0), zt_ref[sign, b], preferred_element_type=F32)
                total = term if total is None else total + term
        turned = [total[:128]] + [
            pltpu.roll(total[t * 128 : t * 128 + 128], 16 * t, 1) for t in range(1, KG)
        ]
        for elem in range(8):
            block = turned[0]
            for t in range(1, KG):
                block = jnp.where(group == (elem + t) % 8, turned[t], block)
            out_ref[elem, :, pl.ds(step, 1)] = block.astype(BF).reshape(16, 1, 8, 128)
        return carry

    lax.fori_loop(0, 32 // KG, rows_of, 0)


def assemble(shared, out_modes, tables, weights, metric, adds_u, adds_b, token):
    table, fields, coef, chunks = shared

    def kernel(*args):
        assemble_kernel((len(adds_u), len(adds_b)), *args)

    adds = adds_u + adds_b
    shape = (8, 16, BLOCKS, 8, 128)
    return pl.pallas_call(
        kernel,
        grid_spec=pltpu.PrefetchScalarGridSpec(
            num_scalar_prefetch=2,
            grid=(1,),
            in_specs=[
                pl.BlockSpec(memory_space=pl.ANY),
                whole((128, 256)),
                whole(tables.shape),
                pl.BlockSpec((1, NPE), lambda i, table, chosen: (0, table[0])),
                pl.BlockSpec((3, 3, NPE), lambda i, table, chosen: (0, 0, table[0])),
                own_spec(0, 0, 0),
                other_spec(0, 0),
                own_spec(1, 0, 0),
                other_spec(1, 0),
            ]
            + [row_spec(array, row) for array, row in adds],
            out_specs=whole(shape),
            scratch_shapes=[
                pltpu.VMEM((2, 3, NPE, 128), BF),
                pltpu.VMEM((2, 384, NPE), BF),
                pltpu.VMEM((2, 3, 3, 128, NPE), BF),
                pltpu.VMEM((2, 3, 512, NPE), BF),
                pltpu.VMEM((512, 128), BF),
                pltpu.VMEM((128, 128), F32),
            ],
        ),
        out_shape=jax.ShapeDtypeStruct(shape, BF),
        compiler_params=pltpu.CompilerParams(vmem_limit_bytes=32 * MIB),
        cost_estimate=TINY,
        name="assemble",
    )(table, out_modes, token, coef, tables, weights, metric, fields, chunks[0], fields, chunks[0],
      *[array for array, row in adds])


def finish_kernel(table, in_ref, tensor_ref, diffusion_ref):
    total = jnp.sum(in_ref[...].astype(F32), axis=0).reshape(BLOCKS * 8, 128)
    total = jnp.concatenate([total, jnp.zeros((128 - BLOCKS * 8, 128), F32)], axis=0)
    shift = lax.rem(128 - 16 * table[10], 128)
    turned = pltpu.roll(total, shift, 1).T
    lane = lax.broadcasted_iota(jnp.int32, (16, 128), 1) % 8
    for j in range(8):
        rows = None
        for t in range(8):
            part = turned[t * 16 : t * 16 + 16]
            if t != j:
                part = pltpu.roll(part, (t - j) % 128, 1)
            rows = part if rows is None else jnp.where(lane == t, part, rows)
        tensor_ref[j] = rows[:, :32]
    diffusion_ref[...] = turned[:4, 32:40]


def finish(table, shares):
    return pl.pallas_call(
        finish_kernel,
        grid_spec=pltpu.PrefetchScalarGridSpec(
            num_scalar_prefetch=1,
            grid=(1,),
            in_specs=[whole(shares.shape)],
            out_specs=[whole((8, 16, 32)), whole((4, 8))],
        ),
        out_shape=[jax.ShapeDtypeStruct((8, 16, 32), F32), jax.ShapeDtypeStruct((4, 8), F32)],
        compiler_params=pltpu.CompilerParams(vmem_limit_bytes=12 * MIB),
        name="finish",
    )(table, shares)


def bf16(*shape):
    return jax.ShapeDtypeStruct(shape, BF)


def on_device(snapshots, coefficients, mass_weights, metric, out_modes):
    fields = snapshots.transpose(1, 0, 2)
    snap, elem = lax.axis_index("snap"), lax.axis_index("elem")
    x, y_hi, core = snap // 4, (snap // 2) % 2, snap % 2
    slot = lax.iota(jnp.int32, TABLE)
    table = core * 8 + ((x + (slot // 2) * (1 + 2 * core)) % 4) * 2 + (y_hi ^ (slot % 2))
    table = jnp.where(slot < 8, table, jnp.where(slot < 10, y_hi ^ (slot % 2), elem))
    table = jnp.where(slot < 12, table, (1 - core) * 4 + (x + slot * (3 - 2 * core)) % 4).astype(jnp.int32)

    near, token = cut(table, fields, [2], "cut_near", coef=coefficients)
    *rest, token = cut(table, fields, [1, 3, 0], "cut_far", token=token)
    near = send(near, CORE, "near")
    chunks = {2: near}
    for dx, chunk in zip((1, 3, 0), rest):
        chunks[dx] = send(chunk, CORE, "far")

    U, B = 0, 1
    rows = None

    def total(items, outs, name, *before):
        nonlocal token, rows
        shared = (table, fields, rows, chunks)
        if rows is None:
            result = sums(shared, items, outs, name, (token,) + before, (coefficients, near))
            rows = result[-1]
        else:
            result = sums(shared, items, outs, name, (token,) + before)
        token = result[len(outs)]
        return result[: len(outs)]

    yb1, xa1 = total([((B, 2, 1), []), ((U, 2, 0), []), ((U, 2, 1), [])], [[0], [1, 2]], "first")
    yb1, xa1 = send(yb1, Y2, "yb1"), send(xa1, FORWARD, "xa1")
    yb2, xa2 = total(
        [((B, 1, 1), []), ((B, 3, 1), []), ((U, 3, 0), []), ((U, 3, 1), [])], [[0, 1], [2, 3]], "second"
    )
    yb2, xa2 = send(yb2, Y2, "yb2"), send(xa2, BACK, "xa2")
    xa3, xb1, yb3 = total(
        [((U, 1, 0), [(xa1, 0)]), ((U, 1, 1), [(xa1, 1)]), ((B, 2, 0), [(yb1, 0)]), ((B, 0, 1), [])],
        [[0, 1], [2], [3]], "third",
    )
    xa3, xb1, yb3 = send(xa3, FORWARD, "xa3"), send(xb1, FORWARD, "xb1"), send(yb3, Y2, "yb3")
    token = pin(token, xa2, yb2)
    (ya,) = total([((U, 0, 1), [(xa2, 1), (xa3, 1)])], [[0]], "fourth")
    ya = send(ya, Y2, "ya")
    xb3, xb2 = total([((B, 1, 0), [(yb2, 0), (xb1, 0)]), ((B, 3, 0), [(yb2, 1)])], [[0], [1]], "fifth")
    xb3, xb2 = send(xb3, FORWARD, "xb3"), send(xb2, BACK, "xb2")

    token = pin(token, ya)

    shares = assemble(
        (table, fields, rows, chunks), out_modes, derivative_tables(GLL), mass_weights.reshape(1, -1), metric,
        [(xa2, 0), (xa3, 0), (ya, 0)],
        [(yb3, 0), (xb2, 0), (xb3, 0)],
        token,
    )
    shares = lax.all_to_all(shares.reshape(128, BLOCKS, 8, 128), AXES, 0, 0, tiled=True)
    tensor, diffusion = finish(table, shares)
    return tensor.transpose(2, 0, 1), diffusion


def solution(mesh):
    return jax.shard_map(
        on_device,
        mesh=mesh,
        in_specs=(P("snap", None, "elem"), P("snap", None), P("elem"), P(None, None, "elem"), P()),
        out_specs=(P(None, "snap", "elem"), P("elem", "snap")),
        check_vma=False,
    )
```

time: 622 us -> 107 us (0.17)
  local copies, waits for them, and re-layouts: 231 us -> 5.37 us
  waiting for transfers between devices: 245 us -> 24.1 us
  matrix products: 84.6 us -> 0 us
  starting transfers between devices: 0.16 us -> 23.9 us
  Pallas kernels: 0 us -> 22 us
  other arithmetic: 20.4 us -> 0.02 us
  between operations: 15.1 us -> 0.86 us
  blocking collectives: 19.7 us -> 30.4 us
    mul x33 -> x0, local copies, waits for them, and re-layouts: 163 us -> none  [the longest x18 93 us: weighted_pairs(): term = left * right]
    reduce_scatter x2 -> x0, waiting for transfers between devices: 125 us -> none  [the longest x1 125 us: on_device(): lax.psum_scatter(lax.dot_general(coefficients, flat, (((0,), (0,)), ((),...]
    psum x1 -> x0, waiting for transfers between devices: 120 us -> none  [on_device(): chosen = lax.psum(picked.astype(jnp.bfloat16), 'snap')]
    dot_general x10 -> x0, matrix products: 84.6 us -> none  [the longest x1 32 us: on_device(): lax.dot_general(product, lax.all_gather(own_flat, 'snap', axis=0, tiled=T...]
    all_to_all x0 -> x1, blocking collectives: none -> 30.4 us  [on_device(): lax.all_to_all(shares.reshape(128, BLOCKS, 8, 128), AXES, 0, 0, tiled=True)]
    ppermute x0 -> x14, waiting for transfers between devices: none -> 24.1 us  [send(): return lax.ppermute(value, AXES, pairs)]
    ppermute x0 -> x14, starting transfers between devices: none -> 23.9 us  [send(): return lax.ppermute(value, AXES, pairs)]
    convert_element_type x4 -> x0, local copies, waits for them, and re-layouts: 22.4 us -> none  [the longest x3 21.5 us: weighted_pairs(): left = paired[:, None, :, component, None, :].astype(jnp.float32)]
  transfers between devices with their start and end apart: 4 -> 14, of which waited for: 2 -> 6; matrix products, arithmetic and copies ran while one was open for 43% -> 0% of each run, Pallas kernels for 0% -> 6%
where the time goes in v2:
time: 107 us
  blocking collectives  30.4 us (28%)
  waiting for transfers between devices  24.1 us (23%)
  starting transfers between devices  23.9 us (22%)
  Pallas kernels  22 us (21%)
  local copies, waits for them, and re-layouts  5.37 us (5%)
    all_to_all x1, blocking collectives, on_device(): lax.all_to_all(shares.reshape(128, BLOCKS, 8, 128), AXES, 0, 0, tiled=True)  30.4 us
    ppermute x14, waiting for transfers between devices, send(): return lax.ppermute(value, AXES, pairs)  24.1 us
    ppermute x14, starting transfers between devices, send(): return lax.ppermute(value, AXES, pairs)  23.9 us
    pallas_call x1, Pallas kernels, assemble(): pl.pallas_call(kernel, grid_spec=pltpu.PrefetchScalarGridSpec(num_scalar_...  13.2 us
    unnamed x20, local copies, waits for them, and re-layouts  5.37 us
    pallas_call x5, Pallas kernels, sums(): pl.pallas_call(kernel, grid_spec=pltpu.PrefetchScalarGridSpec(num_scalar_...  5.19 us
  transfers between devices with their start and end apart: 14, of which 6 were waited for; matrix products, arithmetic and copies ran while one was open for 0% of the time, Pallas kernels for 6%

profile of v2, /device:TPU:0, one launch (start us, length us, event | category | flops | bytes accessed | tf_op | source)
XLA Modules:
  0.0 106.6 jit_solution(3741664991469910783)
XLA Ops:
  0.7 4.6 %copy-done = bf16[128,6,8192]{2,0,1:T(8,128)(2,1)S(1)} copy-done((bf16[128,6,8192]{2,0,1:T(8,128)(2,1)S(1)}, bf16[128,6,8192]{2,0,1:T(8,128)(2,1)}, u32[]{:S(2)}) %copy-start) | copy-done | bytes 12582936
  5.3 0.8 copy-done.3
  6.0 0.7 cut_near.1
  6.8 0.1 collective-permute-start
  6.9 1.1 %cut_far.1 = (bf16[1,6,128,1024]{3,2,1,0:T(8,128)(2,1)S(1)}, bf16[1,6,128,1024]{3,2,1,0:T(8,128)(2,1)S(1)}, bf16[1,6,128,1024]{3,2,1,0:T(8,128)(2,1)S(1)}, f32[8,128]{1,0:T(8,128)S(1)}) custom-call(s32[16]{0:T(128)S(1)} %compare_select_fusion.6.table_ref.args_0_.table, bf16[6,128,8192]{2,1,0:T(8,128)(2,1)S(1)} %bitcast.5, ...), custom_call_target="tpu_custom_call" | custom-call | flops 1 | bytes 1 | tf_op jit(solution)/shard_map/cut_far/pallas_call | solution.py:117
  8.0 0.6 collective-permute-start.1
  8.5 0.1 collective-permute-start.2
  8.6 0.4 collective-permute-start.5
  9.0 1.6 %collective-permute-done.refs_2_.refs_4_.refs_6_.refs_8_.refs_9_ = bf16[1,7,128,1024]{3,2,1,0:T(8,128)(2,1)S(1)} collective-permute-done((bf16[1,7,128,1024]{3,2,1,0:T(8,128)(2,1)S(1)}, bf16[1,7,128,1024]{3,2,1,0:T(8,128)(2,1)S(1)}, u32[]{:S(2)}, u32[]{:S(2)}) %collective-permute-start) | collective-permute-done | bytes 1835040 | tf_op jit(solution)/shard_map/near/ppermute | solution.py:83
  10.7 1.0 first.1
  11.7 1.6 %collective-permute-start.3 = (bf16[2,3,128,512]{3,2,1,0:T(8,128)(2,1)S(1)}, bf16[2,3,128,512]{3,2,1,0:T(8,128)(2,1)S(1)}, u32[]{:S(2)}, u32[]{:S(2)}) collective-permute-start(bf16[2,3,128,512]{3,2,1,0:T(8,128)(2,1)S(1)} %get-tuple-element.34), channel_id=1, source_target_pairs={{0,4},{1,13},{32,36},{33,45},{64,68},{65,77},{96,100},{97,109},{16... | collective-permute-start | bytes 2359304 | tf_op jit(solution)/shard_map/xa1/ppermute | solution.py:83
  13.3 3.2 %collective-permute-start.4 = (bf16[1,3,128,512]{3,2,1,0:T(8,128)(2,1)S(1)}, bf16[1,3,128,512]{3,2,1,0:T(8,128)(2,1)S(1)}, u32[]{:S(2)}, u32[]{:S(2)}) collective-permute-start(bf16[1,3,128,512]{3,2,1,0:T(8,128)(2,1)S(1)} %get-tuple-element.35), channel_id=1, source_target_pairs={{0,2},{1,3},{32,34},{33,35},{64,66},{65,67},{96,98},{97,99},{16,18... | collective-permute-start | bytes 1179656 | tf_op jit(solution)/shard_map/yb1/ppermute | solution.py:83
  16.5 1.1 %second.1 = (bf16[2,3,128,512]{3,2,1,0:T(8,128)(2,1)S(1)}, bf16[2,3,128,512]{3,2,1,0:T(8,128)(2,1)S(1)}, f32[8,128]{1,0:T(8,128)S(1)}) custom-call(s32[16]{0:T(128)S(1)} %compare_select_fusion.6.table_ref.args_0_.table, f32[8,128]{1,0:T(8,128)S(1)} %get-tuple-element.29.refs_0_, bf16[128,256]{1,0:T(8,128)(2,1)S(1)} %get-tuple-element.30.refs_1_.args_3_, ...), custom_call_target="tpu_custom_call" | custom-call | flops 1 | bytes 1 | tf_op jit(solution)/shard_map/second/pallas_call | solution.py:214
  17.7 1.8 %collective-permute-start.6 = (bf16[2,3,128,512]{3,2,1,0:T(8,128)(2,1)S(1)}, bf16[2,3,128,512]{3,2,1,0:T(8,128)(2,1)S(1)}, u32[]{:S(2)}, u32[]{:S(2)}) collective-permute-start(bf16[2,3,128,512]{3,2,1,0:T(8,128)(2,1)S(1)} %get-tuple-element.38), channel_id=1, source_target_pairs={{0,12},{1,5},{32,44},{33,37},{64,76},{65,69},{96,108},{97,101},{16... | collective-permute-start | bytes 2359304 | tf_op jit(solution)/shard_map/xa2/ppermute | solution.py:83
  19.5 2.9 %collective-permute-start.7 = (bf16[2,3,128,512]{3,2,1,0:T(8,128)(2,1)S(1)}, bf16[2,3,128,512]{3,2,1,0:T(8,128)(2,1)S(1)}, u32[]{:S(2)}, u32[]{:S(2)}) collective-permute-start(bf16[2,3,128,512]{3,2,1,0:T(8,128)(2,1)S(1)} %get-tuple-element.39), channel_id=1, source_target_pairs={{0,2},{1,3},{32,34},{33,35},{64,66},{65,67},{96,98},{97,99},{16,18... | collective-permute-start | bytes 2359304 | tf_op jit(solution)/shard_map/yb2/ppermute | solution.py:83
  22.4 4.3 %collective-permute-done.4.refs_10_ = bf16[1,3,128,512]{3,2,1,0:T(8,128)(2,1)S(1)} collective-permute-done((bf16[1,3,128,512]{3,2,1,0:T(8,128)(2,1)S(1)}, bf16[1,3,128,512]{3,2,1,0:T(8,128)(2,1)S(1)}, u32[]{:S(2)}, u32[]{:S(2)}) %collective-permute-start.4) | collective-permute-done | bytes 393248 | tf_op jit(solution)/shard_map/yb1/ppermute | solution.py:83
  26.7 0.8 collective-permute-done.3.refs_4_.refs_7_
  27.5 1.2 %third.1 = (bf16[2,3,128,512]{3,2,1,0:T(8,128)(2,1)S(1)}, bf16[1,3,128,512]{3,2,1,0:T(8,128)(2,1)S(1)}, bf16[1,3,128,512]{3,2,1,0:T(8,128)(2,1)S(1)}, f32[8,128]{1,0:T(8,128)S(1)}) custom-call(s32[16]{0:T(128)S(1)} %compare_select_fusion.6.table_ref.args_0_.table, f32[8,128]{1,0:T(8,128)S(1)} %get-tuple-element.33.refs_0_, ...), custom_call_target="tpu_custom_call" | custom-call | flops 1 | bytes 1 | tf_op jit(solution)/shard_map/third/pallas_call | solution.py:214
  28.6 1.7 %collective-permute-start.8 = (bf16[2,3,128,512]{3,2,1,0:T(8,128)(2,1)S(1)}, bf16[2,3,128,512]{3,2,1,0:T(8,128)(2,1)S(1)}, u32[]{:S(2)}, u32[]{:S(2)}) collective-permute-start(bf16[2,3,128,512]{3,2,1,0:T(8,128)(2,1)S(1)} %get-tuple-element.40), channel_id=1, source_target_pairs={{0,4},{1,13},{32,36},{33,45},{64,68},{65,77},{96,100},{97,109},{16... | collective-permute-start | bytes 2359304 | tf_op jit(solution)/shard_map/xa3/ppermute | solution.py:83
  30.4 2.3 %collective-permute-start.9 = (bf16[1,3,128,512]{3,2,1,0:T(8,128)(2,1)S(1)}, bf16[1,3,128,512]{3,2,1,0:T(8,128)(2,1)S(1)}, u32[]{:S(2)}, u32[]{:S(2)}) collective-permute-start(bf16[1,3,128,512]{3,2,1,0:T(8,128)(2,1)S(1)} %get-tuple-element.42), channel_id=1, source_target_pairs={{0,4},{1,13},{32,36},{33,45},{64,68},{65,77},{96,100},{97,109},{16... | collective-permute-start | bytes 1179656 | tf_op jit(solution)/shard_map/xb1/ppermute | solution.py:83
  32.7 3.2 %collective-permute-start.11 = (bf16[1,3,128,512]{3,2,1,0:T(8,128)(2,1)S(1)}, bf16[1,3,128,512]{3,2,1,0:T(8,128)(2,1)S(1)}, u32[]{:S(2)}, u32[]{:S(2)}) collective-permute-start(bf16[1,3,128,512]{3,2,1,0:T(8,128)(2,1)S(1)} %get-tuple-element.45), channel_id=1, source_target_pairs={{0,2},{1,3},{32,34},{33,35},{64,66},{65,67},{96,98},{97,99},{16,18... | collective-permute-start | bytes 1179656 | tf_op jit(solution)/shard_map/yb3/ppermute | solution.py:83
  35.9 7.7 %collective-permute-done.7.refs_2_.refs_4_.refs_8_ = bf16[2,3,128,512]{3,2,1,0:T(8,128)(2,1)S(1)} collective-permute-done((bf16[2,3,128,512]{3,2,1,0:T(8,128)(2,1)S(1)}, bf16[2,3,128,512]{3,2,1,0:T(8,128)(2,1)S(1)}, u32[]{:S(2)}, u32[]{:S(2)}) %collective-permute-start.7) | collective-permute-done | bytes 786464 | tf_op jit(solution)/shard_map/yb2/ppermute | solution.py:83
  43.5 0.8 fourth.1
  44.4 3.9 %collective-permute-start.10 = (bf16[1,3,128,512]{3,2,1,0:T(8,128)(2,1)S(1)}, bf16[1,3,128,512]{3,2,1,0:T(8,128)(2,1)S(1)}, u32[]{:S(2)}, u32[]{:S(2)}) collective-permute-start(bf16[1,3,128,512]{3,2,1,0:T(8,128)(2,1)S(1)} %get-tuple-element.44), channel_id=1, source_target_pairs={{0,2},{1,3},{32,34},{33,35},{64,66},{65,67},{96,98},{97,99},{16,18... | collective-permute-start | bytes 1179656 | tf_op jit(solution)/shard_map/ya/ppermute | solution.py:83
  48.3 1.0 fifth.1
  49.3 1.4 %collective-permute-start.12 = (bf16[1,3,128,512]{3,2,1,0:T(8,128)(2,1)S(1)}, bf16[1,3,128,512]{3,2,1,0:T(8,128)(2,1)S(1)}, u32[]{:S(2)}, u32[]{:S(2)}) collective-permute-start(bf16[1,3,128,512]{3,2,1,0:T(8,128)(2,1)S(1)} %get-tuple-element.46), channel_id=1, source_target_pairs={{0,12},{1,5},{32,44},{33,37},{64,76},{65,69},{96,108},{97,101},{16... | collective-permute-start | bytes 1179656 | tf_op jit(solution)/shard_map/xb2/ppermute | solution.py:83
  50.7 0.7 collective-permute-start.13
  51.4 9.0 %collective-permute-done.10.refs_1_.args_13_ = bf16[1,3,128,512]{3,2,1,0:T(8,128)(2,1)S(1)} collective-permute-done((bf16[1,3,128,512]{3,2,1,0:T(8,128)(2,1)S(1)}, bf16[1,3,128,512]{3,2,1,0:T(8,128)(2,1)S(1)}, u32[]{:S(2)}, u32[]{:S(2)}) %collective-permute-start.10) | collective-permute-done | bytes 393248 | tf_op jit(solution)/shard_map/ya/ppermute | solution.py:83
  60.4 0.8 collective-permute-done.13.args_16_
  61.2 13.2 %assemble.1 = bf16[8,16,5,8,128]{4,3,2,1,0:T(8,128)(2,1)S(1)} custom-call(s32[16]{0:T(128)S(1)} %compare_select_fusion.6.table_ref.args_0_.table, s32[32]{0:T(128)S(1)} %copy-done.6, f32[8,128]{1,0:T(8,128)S(1)} %pin.3.args_2_, bf16[128,256]{1,0:T(8,128)(2,1)S(1)} %get-tuple-element.30.refs_1_.args_3_, bf16[512,1536]{1,0:T(8,128)(2,1)S(1)} %copy-done.1, ...), custom_call_target="tpu_custom_call" | custom-call | flops 1 | bytes 1 | tf_op jit(solution)/shard_map/assemble/pallas_call | solution.py:323
  74.5 30.4 %all_to_all.5.in_ref = bf16[128,5,8,128]{3,2,1,0:T(8,128)(2,1)S(1)} all-to-all(bf16[128,5,8,128]{3,2,1,0:T(8,128)(2,1)S(1)} %bitcast.24), channel_id=1, replica_groups=mesh['elem'=8,'snap'=16] {'elem','snap'}, dimensions={0} | all-to-all | bytes 2621440 | tf_op jit(solution)/shard_map/all_to_all | solution.py:449
  104.9 1.8 %finish.1 = (f32[8,16,32]{2,1,0:T(8,128)}, f32[4,8]{1,0:T(4,128)}) custom-call(s32[16]{0:T(128)S(1)} %compare_select_fusion.6.table_ref.args_0_.table, bf16[128,5,8,128]{3,2,1,0:T(8,128)(2,1)S(1)} %all_to_all.5.in_ref), custom_call_target="tpu_custom_call" | custom-call | tf_op jit(solution)/shard_map/finish/pallas_call | solution.py:376
  (30 shorter events, 0.1 us)
Async XLA Ops:
  0.7 4.6 %copy-start = (bf16[128,6,8192]{2,0,1:T(8,128)(2,1)S(1)}, bf16[128,6,8192]{2,0,1:T(8,128)(2,1)}, u32[]{:S(2)}) copy-start(bf16[128,6,8192]{2,0,1:T(8,128)(2,1)} %param.6) | copy-start | bytes 37748740
  5.3 0.8 copy-start.3
  6.8 3.9 %collective-permute-start = (bf16[1,7,128,1024]{3,2,1,0:T(8,128)(2,1)S(1)}, bf16[1,7,128,1024]{3,2,1,0:T(8,128)(2,1)S(1)}, u32[]{:S(2)}, u32[]{:S(2)}) collective-permute-start(bf16[1,7,128,1024]{3,2,1,0:T(8,128)(2,1)S(1)} %get-tuple-element.28), channel_id=1, source_target_pairs={{0,1},{1,0},{32,33},{33,32},{64,65},{65,64},{96,97},{97,96},{16,17... | collective-permute-start | bytes 5505032 | tf_op jit(solution)/shard_map/near/ppermute | solution.py:83
  6.9 3.8 %copy-start.4 = (bf16[128,128]{1,0:T(8,128)(2,1)S(1)}, bf16[128,128]{1,0:T(8,128)(2,1)}, u32[]{:S(2)}) copy-start(bf16[128,128]{1,0:T(8,128)(2,1)} %refs_1_.1) | copy-start | bytes 98308
  8.0 8.6 %collective-permute-start.1 = (bf16[1,6,128,1024]{3,2,1,0:T(8,128)(2,1)S(1)}, bf16[1,6,128,1024]{3,2,1,0:T(8,128)(2,1)S(1)}, u32[]{:S(2)}, u32[]{:S(2)}) collective-permute-start(bf16[1,6,128,1024]{3,2,1,0:T(8,128)(2,1)S(1)} %get-tuple-element.31), channel_id=1, source_target_pairs={{0,1},{1,0},{32,33},{33,32},{64,65},{65,64},{96,97},{97,96},{16,17... | collective-permute-start | bytes 4718600 | tf_op jit(solution)/shard_map/far/ppermute | solution.py:83
  8.5 8.0 %collective-permute-start.2 = (bf16[1,6,128,1024]{3,2,1,0:T(8,128)(2,1)S(1)}, bf16[1,6,128,1024]{3,2,1,0:T(8,128)(2,1)S(1)}, u32[]{:S(2)}, u32[]{:S(2)}) collective-permute-start(bf16[1,6,128,1024]{3,2,1,0:T(8,128)(2,1)S(1)} %get-tuple-element.32), channel_id=1, source_target_pairs={{0,1},{1,0},{32,33},{33,32},{64,65},{65,64},{96,97},{97,96},{16,17... | collective-permute-start | bytes 4718600 | tf_op jit(solution)/shard_map/far/ppermute | solution.py:83
  8.6 13.8 %collective-permute-start.5 = (bf16[1,6,128,1024]{3,2,1,0:T(8,128)(2,1)S(1)}, bf16[1,6,128,1024]{3,2,1,0:T(8,128)(2,1)S(1)}, u32[]{:S(2)}, u32[]{:S(2)}) collective-permute-start(bf16[1,6,128,1024]{3,2,1,0:T(8,128)(2,1)S(1)} %get-tuple-element.36), channel_id=1, source_target_pairs={{0,1},{1,0},{32,33},{33,32},{64,65},{65,64},{96,97},{97,96},{16,17... | collective-permute-start | bytes 4718600 | tf_op jit(solution)/shard_map/far/ppermute | solution.py:83
  11.7 15.8 %collective-permute-start.3 = (bf16[2,3,128,512]{3,2,1,0:T(8,128)(2,1)S(1)}, bf16[2,3,128,512]{3,2,1,0:T(8,128)(2,1)S(1)}, u32[]{:S(2)}, u32[]{:S(2)}) collective-permute-start(bf16[2,3,128,512]{3,2,1,0:T(8,128)(2,1)S(1)} %get-tuple-element.34), channel_id=1, source_target_pairs={{0,4},{1,13},{32,36},{33,45},{64,68},{65,77},{96,100},{97,109},{16... | collective-permute-start | bytes 2359304 | tf_op jit(solution)/shard_map/xa1/ppermute | solution.py:83
  13.3 13.3 %collective-permute-start.4 = (bf16[1,3,128,512]{3,2,1,0:T(8,128)(2,1)S(1)}, bf16[1,3,128,512]{3,2,1,0:T(8,128)(2,1)S(1)}, u32[]{:S(2)}, u32[]{:S(2)}) collective-permute-start(bf16[1,3,128,512]{3,2,1,0:T(8,128)(2,1)S(1)} %get-tuple-element.35), channel_id=1, source_target_pairs={{0,2},{1,3},{32,34},{33,35},{64,66},{65,67},{96,98},{97,99},{16,18... | collective-permute-start | bytes 1179656 | tf_op jit(solution)/shard_map/yb1/ppermute | solution.py:83
  17.7 18.2 %collective-permute-start.6 = (bf16[2,3,128,512]{3,2,1,0:T(8,128)(2,1)S(1)}, bf16[2,3,128,512]{3,2,1,0:T(8,128)(2,1)S(1)}, u32[]{:S(2)}, u32[]{:S(2)}) collective-permute-start(bf16[2,3,128,512]{3,2,1,0:T(8,128)(2,1)S(1)} %get-tuple-element.38), channel_id=1, source_target_pairs={{0,12},{1,5},{32,44},{33,37},{64,76},{65,69},{96,108},{97,101},{16... | collective-permute-start | bytes 2359304 | tf_op jit(solution)/shard_map/xa2/ppermute | solution.py:83
  19.5 24.0 %collective-permute-start.7 = (bf16[2,3,128,512]{3,2,1,0:T(8,128)(2,1)S(1)}, bf16[2,3,128,512]{3,2,1,0:T(8,128)(2,1)S(1)}, u32[]{:S(2)}, u32[]{:S(2)}) collective-permute-start(bf16[2,3,128,512]{3,2,1,0:T(8,128)(2,1)S(1)} %get-tuple-element.39), channel_id=1, source_target_pairs={{0,2},{1,3},{32,34},{33,35},{64,66},{65,67},{96,98},{97,99},{16,18... | collective-permute-start | bytes 2359304 | tf_op jit(solution)/shard_map/yb2/ppermute | solution.py:83
  28.6 14.9 %collective-permute-start.8 = (bf16[2,3,128,512]{3,2,1,0:T(8,128)(2,1)S(1)}, bf16[2,3,128,512]{3,2,1,0:T(8,128)(2,1)S(1)}, u32[]{:S(2)}, u32[]{:S(2)}) collective-permute-start(bf16[2,3,128,512]{3,2,1,0:T(8,128)(2,1)S(1)} %get-tuple-element.40), channel_id=1, source_target_pairs={{0,4},{1,13},{32,36},{33,45},{64,68},{65,77},{96,100},{97,109},{16... | collective-permute-start | bytes 2359304 | tf_op jit(solution)/shard_map/xa3/ppermute | solution.py:83
  30.4 17.9 %collective-permute-start.9 = (bf16[1,3,128,512]{3,2,1,0:T(8,128)(2,1)S(1)}, bf16[1,3,128,512]{3,2,1,0:T(8,128)(2,1)S(1)}, u32[]{:S(2)}, u32[]{:S(2)}) collective-permute-start(bf16[1,3,128,512]{3,2,1,0:T(8,128)(2,1)S(1)} %get-tuple-element.42), channel_id=1, source_target_pairs={{0,4},{1,13},{32,36},{33,45},{64,68},{65,77},{96,100},{97,109},{16... | collective-permute-start | bytes 1179656 | tf_op jit(solution)/shard_map/xb1/ppermute | solution.py:83
  32.7 27.7 %collective-permute-start.11 = (bf16[1,3,128,512]{3,2,1,0:T(8,128)(2,1)S(1)}, bf16[1,3,128,512]{3,2,1,0:T(8,128)(2,1)S(1)}, u32[]{:S(2)}, u32[]{:S(2)}) collective-permute-start(bf16[1,3,128,512]{3,2,1,0:T(8,128)(2,1)S(1)} %get-tuple-element.45), channel_id=1, source_target_pairs={{0,2},{1,3},{32,34},{33,35},{64,66},{65,67},{96,98},{97,99},{16,18... | collective-permute-start | bytes 1179656 | tf_op jit(solution)/shard_map/yb3/ppermute | solution.py:83
  44.4 16.0 %collective-permute-start.10 = (bf16[1,3,128,512]{3,2,1,0:T(8,128)(2,1)S(1)}, bf16[1,3,128,512]{3,2,1,0:T(8,128)(2,1)S(1)}, u32[]{:S(2)}, u32[]{:S(2)}) collective-permute-start(bf16[1,3,128,512]{3,2,1,0:T(8,128)(2,1)S(1)} %get-tuple-element.44), channel_id=1, source_target_pairs={{0,2},{1,3},{32,34},{33,35},{64,66},{65,67},{96,98},{97,99},{16,18... | collective-permute-start | bytes 1179656 | tf_op jit(solution)/shard_map/ya/ppermute | solution.py:83
  48.2 12.9 %slice-start = ((s8[12582912]{0:T(1024)(128)(4,1)}), s8[4194304]{0:T(1024)(128)(4,1)S(1)}, s32[]{:S(2)}) async-start(s8[12582912]{0:T(1024)(128)(4,1)} %bitcast.20), calls=%async_computation.1 | async-start | bytes 8388608
  48.2 12.9 %slice-start.1 = ((s8[12582912]{0:T(1024)(128)(4,1)}), s8[4194304]{0:T(1024)(128)(4,1)S(1)}, s32[]{:S(2)}) async-start(s8[12582912]{0:T(1024)(128)(4,1)} %bitcast.20), calls=%async_computation.2 | async-start | bytes 8388608
  48.2 12.9 %slice-start.2 = ((s8[12582912]{0:T(1024)(128)(4,1)}), s8[4194304]{0:T(1024)(128)(4,1)S(1)}, s32[]{:S(2)}) async-start(s8[12582912]{0:T(1024)(128)(4,1)} %bitcast.20), calls=%async_computation.3 | async-start | bytes 8388608
  48.3 12.9 %copy-start.1 = (bf16[512,1536]{1,0:T(8,128)(2,1)S(1)}, bf16[512,1536]{1,0:T(8,128)(2,1)}, u32[]{:S(2)}) copy-start(bf16[512,1536]{1,0:T(8,128)(2,1)} %constant.97.args_4_) | copy-start | bytes 4718596
  48.3 12.9 %copy-start.2 = (f32[3,3,8192]{2,1,0:T(4,128)S(1)}, f32[3,3,8192]{2,1,0:T(4,128)}, u32[]{:S(2)}) copy-start(f32[3,3,8192]{2,1,0:T(4,128)} %args_6_.1) | copy-start | bytes 884740
  48.3 12.9 %copy-start.5 = (f32[8192]{0:T(1024)S(1)}, f32[8192]{0:T(1024)}, u32[]{:S(2)}) copy-start(f32[8192]{0:T(1024)} %param.8) | copy-start | bytes 98308
  48.3 12.9 %copy-start.6 = (s32[32]{0:T(128)S(1)}, s32[32]{0:T(128)}, u32[]{:S(2)}) copy-start(s32[32]{0:T(128)} %args_1_.4) | copy-start | bytes 388
  49.3 11.1 %collective-permute-start.12 = (bf16[1,3,128,512]{3,2,1,0:T(8,128)(2,1)S(1)}, bf16[1,3,128,512]{3,2,1,0:T(8,128)(2,1)S(1)}, u32[]{:S(2)}, u32[]{:S(2)}) collective-permute-start(bf16[1,3,128,512]{3,2,1,0:T(8,128)(2,1)S(1)} %get-tuple-element.46), channel_id=1, source_target_pairs={{0,12},{1,5},{32,44},{33,37},{64,76},{65,69},{96,108},{97,101},{16... | collective-permute-start | bytes 1179656 | tf_op jit(solution)/shard_map/xb2/ppermute | solution.py:83
  50.7 10.5 %collective-permute-start.13 = (bf16[1,3,128,512]{3,2,1,0:T(8,128)(2,1)S(1)}, bf16[1,3,128,512]{3,2,1,0:T(8,128)(2,1)S(1)}, u32[]{:S(2)}, u32[]{:S(2)}) collective-permute-start(bf16[1,3,128,512]{3,2,1,0:T(8,128)(2,1)S(1)} %get-tuple-element.47), channel_id=1, source_target_pairs={{0,4},{1,13},{32,36},{33,45},{64,68},{65,77},{96,100},{97,109},{16... | collective-permute-start | bytes 1179656 | tf_op jit(solution)/shard_map/xb3/ppermute | solution.py:83

commit v3 on v2

--- a/solution.py
+++ b/solution.py
@@ -78,6 +78,16 @@
 Y2 = moves(lambda x, y, z, c: (x, y + 2, z, c))
 
 
+def lines(key):
+    groups = {}
+    for where in PLACES:
+        groups.setdefault(key(*where), []).append(place(*where))
+    return [sorted(group) for group in groups.values()]
+
+
+SAME_CORE = lines(lambda x, y, z, c: c)
+
+
 def send(value, pairs, name):
     with jax.named_scope(name):
         return lax.ppermute(value, AXES, pairs)
@@ -87,46 +97,57 @@
 ITEM_BYTES = 3 * 128 * NPE * 2
 MIB = 1024 * 1024
 TINY = pl.CostEstimate(flops=1, bytes_accessed=1, transcendentals=0)
-TABLE = 16
+TABLE = 18
 TOKEN = (8, 128)
 
 
-def cut(table, fields, wanted, name, coef=None, token=None):
-    planes = 6 if coef is None else 7
-    count = len(wanted)
-    others = [array for array in (coef, token) if array is not None]
-
-    def kernel(table_ref, fields_ref, coef_ref, *refs):
-        outs, token_ref, sems = refs[:count], refs[count], refs[count + 1]
+def cut(table, fields, groups, name, space, token, coef=None):
+    extra = 0 if coef is None else 1
+    count = len(groups)
+    total = sum(len(group) for group in groups)
+
+    def kernel(table_ref, fields_ref, token_in, *refs):
+        outs, token_ref, sems = refs[extra : extra + count], refs[-2], refs[-1]
         copies = []
-        for n, dx in enumerate(wanted):
-            lanes = pl.ds(pl.multiple_of(table_ref[12 + dx] * 1024, 1024), 1024)
-            for c in range(6):
+        if coef is not None:
+            copies.append(
+                pltpu.make_async_copy(
+                    refs[0], outs[0].at[3 * total, :, pl.ds(0, 128)], sems.at[total]
+                )
+            )
+        slot = 0
+        for number, group in enumerate(groups):
+            for n, (half, dx, dy) in enumerate(group):
+                lanes = pl.ds(pl.multiple_of(table_ref[8 + dx * 2 + dy] * NPE, NPE), NPE)
                 copies.append(
-                    pltpu.make_async_copy(fields_ref.at[c, :, lanes], outs[n].at[0, c], sems.at[n * 6 + c])
+                    pltpu.make_async_copy(
+                        fields_ref.at[pl.ds(half * 3, 3), :, lanes],
+                        outs[number].at[pl.ds(3 * n, 3)],
+                        sems.at[slot],
+                    )
                 )
+                slot += 1
         for copy in copies:
             copy.start()
         token_ref[...] = jnp.zeros(TOKEN, F32)
         if coef is not None:
-            outs[0][0, 6, :, :128] = coef_ref[...]
-            outs[0][0, 6, :, 128:] = jnp.zeros((128, 896), BF)
+            outs[0][3 * total, :, 128:] = jnp.zeros((128, NPE - 128), BF)
         for copy in copies:
             copy.wait()
 
+    anywhere = pl.BlockSpec(memory_space=pl.ANY)
+    others = [token] if coef is None else [token, coef]
+    shapes = [bf16(3 * len(group) + extra, 128, NPE) for group in groups]
     return pl.pallas_call(
         kernel,
         grid_spec=pltpu.PrefetchScalarGridSpec(
             num_scalar_prefetch=1,
             grid=(1,),
-            in_specs=[
-                pl.BlockSpec(memory_space=pl.ANY),
-                pl.BlockSpec(memory_space=pl.ANY) if coef is None else whole((128, 128)),
-            ],
-            out_specs=[whole((1, planes, 128, 1024))] * count + [whole(TOKEN)],
-            scratch_shapes=[pltpu.SemaphoreType.DMA((6 * count,))],
+            in_specs=[pl.BlockSpec(memory_space=space)] + [anywhere] * len(others),
+            out_specs=[whole(shape.shape) for shape in shapes] + [whole(TOKEN)],
+            scratch_shapes=[pltpu.SemaphoreType.DMA((total + 1,))],
         ),
-        out_shape=[bf16(1, planes, 128, 1024)] * count + [jax.ShapeDtypeStruct(TOKEN, F32)],
+        out_shape=shapes + [jax.ShapeDtypeStruct(TOKEN, F32)],
         compiler_params=pltpu.CompilerParams(vmem_limit_bytes=16 * MIB),
         cost_estimate=TINY,
         name=name,
@@ -137,12 +158,12 @@
     return pl.BlockSpec(ITEM, lambda i, table, *rest: (half, 0, table[dx * 2 + dy]))
 
 
-def other_spec(half, dy):
-    return pl.BlockSpec((1,) + ITEM, lambda i, table, *rest: (0, half, 0, table[8 + dy]))
-
-
-def row_spec(array, row):
-    return pl.BlockSpec((1,) + array.shape[1:], lambda i, *rest: (row, 0, 0, 0))
+def other_spec(row):
+    return pl.BlockSpec(ITEM, lambda i, *rest: (row, 0, 0))
+
+
+def row_spec(row):
+    return pl.BlockSpec((1,) + ITEM, lambda i, *rest: (row, 0, 0, 0))
 
 
 def whole(shape):
@@ -166,7 +187,7 @@
 
 
 def project(coef, own, other, c):
-    rows = jnp.concatenate([own[c], other[0, c]], axis=0)
+    rows = jnp.concatenate([own[c], other[c]], axis=0)
     return jnp.dot(coef, rows, preferred_element_type=F32)
 
 
@@ -175,8 +196,9 @@
     operands, specs, plan = [], [], []
     for (half, dx, dy), adds in items:
         entry = []
-        for array, spec in [(fields, own_spec(half, dx, dy)), (chunks[dx], other_spec(half, dy))] + [
-            (array, row_spec(array, row)) for array, row in adds
+        other, row = chunks[(half, dx, dy)]
+        for array, spec in [(fields, own_spec(half, dx, dy)), (other, other_spec(row))] + [
+            (array, row_spec(row)) for array, row in adds
         ]:
             entry.append(len(operands))
             operands.append(array)
@@ -186,14 +208,14 @@
         first, first_specs = [coef], [whole((128, 256))]
     else:
         first = list(coefs)
-        first_specs = [whole((128, 128)), pl.BlockSpec((1, 1, 128, 128), lambda i, table: (0, 6, 0, 0))]
+        first_specs = [whole((128, 128)), pl.BlockSpec((1, 128, 128), lambda i, table: (9, 0, 0))]
 
     def kernel(table_ref, *refs):
         refs = refs[len(before) :]
         if coefs is None:
             rows = refs[0][...]
         else:
-            rows = jnp.concatenate([refs[0][...].T, refs[1][0, 0].T], axis=1)
+            rows = jnp.concatenate([refs[0][...], refs[1][0]], axis=1)
         refs = refs[len(first) :]
         ins, results = refs[: len(operands)], refs[len(operands) :]
         results[len(outs)][...] = jnp.zeros(TOKEN, F32)
@@ -235,17 +257,24 @@
     fields_b, refs = refs[:2], refs[2:]
     adds_u, refs = refs[: counts[0]], refs[counts[0] :]
     adds_b, refs = refs[: counts[1]], refs[counts[1] :]
-    out_ref, zt_ref, z_ref, g_ref, cb_ref, pick_k, pick_d = refs
+    keep_ref, send_ref, z_ref, g_ref, cb_ref, pick_k, pick_d = refs
+    first = table[17] == 0
+
+    def put(elem, step, block):
+        sides = block.reshape(8, 2, 8, 128)
+        keep_ref[elem, :, step] = jnp.where(first, sides[:, 0], sides[:, 1]).astype(BF)
+        send_ref[elem, :, step] = jnp.where(first, sides[:, 1], sides[:, 0]).astype(BF)
+
     half_weight = 0.5 * weight_ref[...]
 
-    columns = lax.broadcasted_iota(jnp.int32, (16, 128), 1)
+    columns = lax.broadcasted_iota(jnp.int32, (1, 128), 1)
     pick_d[...] = jnp.zeros((128, 128), F32)
     for k in range(32):
         hot = (columns == out_modes[k]).astype(F32)
-        pick_k[k * 16 : k * 16 + 16, :] = hot.astype(BF)
+        pick_k[k : k + 1, :] = hot
         row = (k // 4) * 16 + k % 4
-        pick_d[row : row + 1, :] = hot[:1]
-    chosen_d = pick_d[...].astype(BF)
+        pick_d[row : row + 1, :] = hot
+    chosen = pick_k[...].astype(BF)
 
     coef = coef_ref[...]
     for a in range(3):
@@ -256,48 +285,68 @@
         for ref in adds_b:
             b = b + ref[0, a].astype(F32)
         for sign, z in ((0, u + b), (1, u - b)):
-            zt_ref[1 - sign, a] = z.T.astype(BF)
             z = z.astype(BF)
             z_ref[sign, a * 128 : a * 128 + 128] = z
-            cb_ref[sign, a] = (
-                jnp.dot(pick_k[...], z, preferred_element_type=F32) * half_weight
-            ).astype(BF)
-
-    diffusion = None
+            picked = jnp.dot(chosen, z, preferred_element_type=F32) * half_weight
+            for k in range(32):
+                cb_ref[sign, a, k * 16 : k * 16 + 16, :] = jnp.broadcast_to(
+                    picked[k : k + 1], (16, NPE)
+                ).astype(BF)
+
+    half = NPE // 2
+    gram = None
     for sign in range(2):
-        derived = jnp.dot(z_ref[sign], tables_ref[...], preferred_element_type=F32)
+        z = z_ref[sign]
+        derived = []
+        for r in range(2):
+            block = tables_ref[:half, r * NPE : r * NPE + half]
+            derived.append([
+                jnp.dot(z[:, side * half : side * half + half], block, preferred_element_type=F32)
+                for side in range(2)
+            ])
+        full = jnp.dot(z, tables_ref[:, 2 * NPE :], preferred_element_type=F32)
+        derived.append([full[:, :half], full[:, half:]])
         for a in range(3):
-            part = derived[a * 128 : a * 128 + 128]
             for b in range(3):
-                grad = metric_ref[0, b : b + 1, :] * part[:, :NPE]
-                grad = grad + metric_ref[1, b : b + 1, :] * part[:, NPE : 2 * NPE]
-                grad = grad + metric_ref[2, b : b + 1, :] * part[:, 2 * NPE :]
-                grad = grad.astype(BF)
+                sides = []
+                for side in range(2):
+                    lanes = slice(side * half, side * half + half)
+                    grad = None
+                    for r in range(3):
+                        term = metric_ref[r, b : b + 1, lanes] * derived[r][side][a * 128 : a * 128 + 128]
+                        grad = term if grad is None else grad + term
+                    sides.append(grad)
+                grad = jnp.concatenate(sides, axis=1).astype(BF)
                 g_ref[sign, a, b] = grad
-                picked = jnp.dot(chosen_d, grad, preferred_element_type=F32) * half_weight
+                weighted = (grad.astype(F32) * half_weight).astype(BF)
                 term = lax.dot_general(
-                    grad, picked.astype(BF), (((1,), (1,)), ((), ())), preferred_element_type=F32
+                    grad, weighted, (((1,), (1,)), ((), ())), preferred_element_type=F32
                 )
-                diffusion = term if diffusion is None else diffusion + term
-    diffusion = diffusion.astype(BF).reshape(16, 8, 128)
+                gram = term if gram is None else gram + term
+    diffusion = lax.dot_general(
+        gram.astype(BF), pick_d[...].astype(BF), (((1,), (1,)), ((), ())), preferred_element_type=F32
+    )
     for elem in range(8):
-        out_ref[elem, :, BLOCKS - 1] = diffusion
+        put(elem, BLOCKS - 1, diffusion)
     group = lax.broadcasted_iota(jnp.int32, (128, 128), 1) // 16
 
-    def rows_of(step, carry):
+    def rows_of(step):
         total = None
         for sign in range(2):
             for b in range(3):
                 pieces = []
                 for t in range(KG):
-                    start = pl.multiple_of((step * KG + t) * 16, 16)
+                    start = (step * KG + t) * 16
                     product = None
                     for a in range(3):
                         picked = cb_ref[sign, a, pl.ds(start, 16), :][None]
                         term = g_ref[sign, a, b].reshape(8, 16, NPE) * picked
                         product = term if product is None else product + term
                     pieces.append(product.reshape(128, NPE))
-                term = jnp.dot(jnp.concatenate(pieces, axis=0), zt_ref[sign, b], preferred_element_type=F32)
+                modes = z_ref[1 - sign, b * 128 : b * 128 + 128]
+                term = lax.dot_general(
+                    jnp.concatenate(pieces, axis=0), modes, (((1,), (1,)), ((), ())), preferred_element_type=F32
+                )
                 total = term if total is None else total + term
         turned = [total[:128]] + [
             pltpu.roll(total[t * 128 : t * 128 + 128], 16 * t, 1) for t in range(1, KG)
@@ -306,10 +355,10 @@
             block = turned[0]
             for t in range(1, KG):
                 block = jnp.where(group == (elem + t) % 8, turned[t], block)
-            out_ref[elem, :, pl.ds(step, 1)] = block.astype(BF).reshape(16, 1, 8, 128)
-        return carry
-
-    lax.fori_loop(0, 32 // KG, rows_of, 0)
+            put(elem, step, block)
+
+    for step in range(32 // KG):
+        rows_of(step)
 
 
 def assemble(shared, out_modes, tables, weights, metric, adds_u, adds_b, token):
@@ -319,7 +368,7 @@
         assemble_kernel((len(adds_u), len(adds_b)), *args)
 
     adds = adds_u + adds_b
-    shape = (8, 16, BLOCKS, 8, 128)
+    out = bf16(8, 8, BLOCKS, 8, 128)
     return pl.pallas_call(
         kernel,
         grid_spec=pltpu.PrefetchScalarGridSpec(
@@ -332,33 +381,45 @@
                 pl.BlockSpec((1, NPE), lambda i, table, chosen: (0, table[0])),
                 pl.BlockSpec((3, 3, NPE), lambda i, table, chosen: (0, 0, table[0])),
                 own_spec(0, 0, 0),
-                other_spec(0, 0),
+                other_spec(chunks[(0, 0, 0)][1]),
                 own_spec(1, 0, 0),
-                other_spec(1, 0),
+                other_spec(chunks[(1, 0, 0)][1]),
             ]
-            + [row_spec(array, row) for array, row in adds],
-            out_specs=whole(shape),
+            + [row_spec(row) for array, row in adds],
+            out_specs=[whole(out.shape)] * 2,
             scratch_shapes=[
-                pltpu.VMEM((2, 3, NPE, 128), BF),
                 pltpu.VMEM((2, 384, NPE), BF),
                 pltpu.VMEM((2, 3, 3, 128, NPE), BF),
                 pltpu.VMEM((2, 3, 512, NPE), BF),
-                pltpu.VMEM((512, 128), BF),
+                pltpu.VMEM((32, 128), F32),
                 pltpu.VMEM((128, 128), F32),
             ],
         ),
-        out_shape=jax.ShapeDtypeStruct(shape, BF),
+        out_shape=[out] * 2,
         compiler_params=pltpu.CompilerParams(vmem_limit_bytes=32 * MIB),
         cost_estimate=TINY,
         name="assemble",
-    )(table, out_modes, token, coef, tables, weights, metric, fields, chunks[0], fields, chunks[0],
+    )(table, out_modes, token, coef, tables, weights, metric, fields, chunks[(0, 0, 0)][0], fields, chunks[(1, 0, 0)][0],
       *[array for array, row in adds])
+
+
+def add_kernel(keep_ref, got_ref, out_ref):
+    out_ref[...] = (keep_ref[...].astype(F32) + got_ref[...].astype(F32)).astype(BF)
+
+
+def add(keep, got):
+    return pl.pallas_call(
+        add_kernel,
+        out_shape=bf16(*keep.shape),
+        compiler_params=pltpu.CompilerParams(vmem_limit_bytes=12 * MIB),
+        name="add",
+    )(keep, got)
 
 
 def finish_kernel(table, in_ref, tensor_ref, diffusion_ref):
     total = jnp.sum(in_ref[...].astype(F32), axis=0).reshape(BLOCKS * 8, 128)
     total = jnp.concatenate([total, jnp.zeros((128 - BLOCKS * 8, 128), F32)], axis=0)
-    shift = lax.rem(128 - 16 * table[10], 128)
+    shift = lax.rem(128 - 16 * table[16], 128)
     turned = pltpu.roll(total, shift, 1).T
     lane = lax.broadcasted_iota(jnp.int32, (16, 128), 1) % 8
     for j in range(8):
@@ -393,60 +454,69 @@
 
 def on_device(snapshots, coefficients, mass_weights, metric, out_modes):
     fields = snapshots.transpose(1, 0, 2)
+    coefficients = coefficients.T
     snap, elem = lax.axis_index("snap"), lax.axis_index("elem")
     x, y_hi, core = snap // 4, (snap // 2) % 2, snap % 2
     slot = lax.iota(jnp.int32, TABLE)
-    table = core * 8 + ((x + (slot // 2) * (1 + 2 * core)) % 4) * 2 + (y_hi ^ (slot % 2))
-    table = jnp.where(slot < 8, table, jnp.where(slot < 10, y_hi ^ (slot % 2), elem))
-    table = jnp.where(slot < 12, table, (1 - core) * 4 + (x + slot * (3 - 2 * core)) % 4).astype(jnp.int32)
-
-    near, token = cut(table, fields, [2], "cut_near", coef=coefficients)
-    *rest, token = cut(table, fields, [1, 3, 0], "cut_far", token=token)
-    near = send(near, CORE, "near")
-    chunks = {2: near}
-    for dx, chunk in zip((1, 3, 0), rest):
-        chunks[dx] = send(chunk, CORE, "far")
+    side = jnp.where(slot < 8, core, 1 - core)
+    table = side * 8 + ((x + ((slot // 2) % 4) * (1 + 2 * side)) % 4) * 2 + (y_hi ^ (slot % 2))
+    table = jnp.where(slot < 16, table, jnp.where(slot < 17, elem, core)).astype(jnp.int32)
 
     U, B = 0, 1
-    rows = None
+    chunks, token, rows = {}, jnp.zeros(TOKEN, F32), None
+
+    def trade(groups, name, space, coef=None):
+        nonlocal token
+        *values, token = cut(table, fields, groups, "cut_" + name, space, token, coef)
+        for value, group in zip(values, groups):
+            got = send(value, CORE, name)
+            for row, key in enumerate(group):
+                chunks[key] = (got, row)
 
     def total(items, outs, name, *before):
         nonlocal token, rows
-        shared = (table, fields, rows, chunks)
-        if rows is None:
-            result = sums(shared, items, outs, name, (token,) + before, (coefficients, near))
+        coefs = (coefficients, chunks[(B, 2, 1)][0]) if rows is None else None
+        result = sums((table, fields, rows, chunks), items, outs, name, (token,) + before, coefs)
+        if coefs is not None:
             rows = result[-1]
-        else:
-            result = sums(shared, items, outs, name, (token,) + before)
         token = result[len(outs)]
         return result[: len(outs)]
 
+    trade([[(B, 2, 1), (U, 2, 0), (U, 2, 1)]], "near", pltpu.HBM, coefficients)
+    trade(
+        [
+            [(B, 1, 1), (B, 3, 1), (U, 3, 0), (U, 3, 1)],
+            [(B, 2, 0), (B, 0, 1), (U, 1, 0), (U, 1, 1)],
+            [(B, 1, 0), (B, 3, 0), (U, 0, 1), (U, 0, 0), (B, 0, 0)],
+        ],
+        "far", pl.ANY,
+    )
     yb1, xa1 = total([((B, 2, 1), []), ((U, 2, 0), []), ((U, 2, 1), [])], [[0], [1, 2]], "first")
     yb1, xa1 = send(yb1, Y2, "yb1"), send(xa1, FORWARD, "xa1")
     yb2, xa2 = total(
         [((B, 1, 1), []), ((B, 3, 1), []), ((U, 3, 0), []), ((U, 3, 1), [])], [[0, 1], [2, 3]], "second"
     )
     yb2, xa2 = send(yb2, Y2, "yb2"), send(xa2, BACK, "xa2")
-    xa3, xb1, yb3 = total(
-        [((U, 1, 0), [(xa1, 0)]), ((U, 1, 1), [(xa1, 1)]), ((B, 2, 0), [(yb1, 0)]), ((B, 0, 1), [])],
-        [[0, 1], [2], [3]], "third",
-    )
-    xa3, xb1, yb3 = send(xa3, FORWARD, "xa3"), send(xb1, FORWARD, "xb1"), send(yb3, Y2, "yb3")
+    xb1, xa3, yb3 = total(
+        [((B, 2, 0), [(yb1, 0)]), ((U, 1, 0), [(xa1, 0)]), ((U, 1, 1), [(xa1, 1)]), ((B, 0, 1), [])],
+        [[0], [1, 2], [3]], "third",
+    )
+    xb1, xa3, yb3 = send(xb1, FORWARD, "xb1"), send(xa3, FORWARD, "xa3"), send(yb3, Y2, "yb3")
     token = pin(token, xa2, yb2)
     (ya,) = total([((U, 0, 1), [(xa2, 1), (xa3, 1)])], [[0]], "fourth")
     ya = send(ya, Y2, "ya")
     xb3, xb2 = total([((B, 1, 0), [(yb2, 0), (xb1, 0)]), ((B, 3, 0), [(yb2, 1)])], [[0], [1]], "fifth")
     xb3, xb2 = send(xb3, FORWARD, "xb3"), send(xb2, BACK, "xb2")
-
     token = pin(token, ya)
 
-    shares = assemble(
+    keep, shares = assemble(
         (table, fields, rows, chunks), out_modes, derivative_tables(GLL), mass_weights.reshape(1, -1), metric,
         [(xa2, 0), (xa3, 0), (ya, 0)],
         [(yb3, 0), (xb2, 0), (xb3, 0)],
         token,
     )
-    shares = lax.all_to_all(shares.reshape(128, BLOCKS, 8, 128), AXES, 0, 0, tiled=True)
+    shares = add(keep, send(shares, CORE, "shares")).reshape(64, BLOCKS, 8, 128)
+    shares = lax.all_to_all(shares, AXES, 0, 0, axis_index_groups=SAME_CORE, tiled=True)
     tensor, diffusion = finish(table, shares)
     return tensor.transpose(2, 0, 1), diffusion
 

time: 107 us -> 102 us (0.953)
  blocking collectives: 30.4 us -> 25.5 us
  Pallas kernels: 22 us -> 20.2 us
    all_to_all x1, blocking collectives: 30.4 us -> 25.5 us  [on_device(): lax.all_to_all(shares, AXES, 0, 0, axis_index_groups=SAME_CORE, tiled=True)]
    pallas_call x1, Pallas kernels: 13.2 us -> 11.5 us  [assemble(): pl.pallas_call(kernel, grid_spec=pltpu.PrefetchScalarGridSpec(num_scalar_...]
    ppermute x14 -> x15, starting transfers between devices: 23.9 us -> 24.8 us  [send(): return lax.ppermute(value, AXES, pairs)]
    ppermute x14 -> x15, waiting for transfers between devices: 24.1 us -> 24.7 us  [send(): return lax.ppermute(value, AXES, pairs)]
    unnamed x20 -> x17, local copies, waits for them, and re-layouts: 5.37 us -> 5.47 us
  transfers between devices with their start and end apart: 14 -> 15, of which waited for: 6 -> 7; matrix products, arithmetic and copies ran while one was open for 0% -> 0% of each run, Pallas kernels for 6% -> 6%
where the time goes in v3:
time: 102 us
  blocking collectives  25.5 us (25%)
  starting transfers between devices  24.8 us (24%)
  waiting for transfers between devices  24.7 us (24%)
  Pallas kernels  20.2 us (20%)
  local copies, waits for them, and re-layouts  5.47 us (5%)
    all_to_all x1, blocking collectives, on_device(): lax.all_to_all(shares, AXES, 0, 0, axis_index_groups=SAME_CORE, tiled=True)  25.5 us
    ppermute x15, starting transfers between devices, send(): return lax.ppermute(value, AXES, pairs)  24.8 us
    ppermute x15, waiting for transfers between devices, send(): return lax.ppermute(value, AXES, pairs)  24.7 us
    pallas_call x1, Pallas kernels, assemble(): pl.pallas_call(kernel, grid_spec=pltpu.PrefetchScalarGridSpec(num_scalar_...  11.5 us
    unnamed x17, local copies, waits for them, and re-layouts  5.47 us
    pallas_call x5, Pallas kernels, sums(): pl.pallas_call(kernel, grid_spec=pltpu.PrefetchScalarGridSpec(num_scalar_...  5.13 us
  transfers between devices with their start and end apart: 15, of which 7 were waited for; matrix products, arithmetic and copies ran while one was open for 0% of the time, Pallas kernels for 6%

profile of v3, /device:TPU:0, one launch (start us, length us, event | category | flops | bytes accessed | tf_op | source)
XLA Modules:
  0.0 101.6 jit_solution(2418380639366858851)
XLA Ops:
  0.7 0.9 copy.8
  1.6 4.6 %copy-done = bf16[128,6,8192]{2,0,1:T(8,128)(2,1)S(1)} copy-done((bf16[128,6,8192]{2,0,1:T(8,128)(2,1)S(1)}, bf16[128,6,8192]{2,0,1:T(8,128)(2,1)}, u32[]{:S(2)}) %copy-start) | copy-done | bytes 12582936
  6.2 0.7 cut_near.1
  7.0 1.1 %cut_far.1 = (bf16[12,128,512]{2,1,0:T(8,128)(2,1)S(1)}, bf16[12,128,512]{2,1,0:T(8,128)(2,1)S(1)}, bf16[15,128,512]{2,1,0:T(8,128)(2,1)S(1)}, f32[8,128]{1,0:T(8,128)S(1)}) custom-call(s32[18]{0:T(128)S(1)} %compare_select_fusion.6.table_ref.args_0_.table, bf16[6,128,8192]{2,1,0:T(8,128)(2,1)S(1)} %bitcast.6, f32[8,128]{1,0:T(8,128)S(1)} %get-tuple-element.28.token_in), custom_call_target="tpu_custom_call" | custom-call | flops 1 | bytes 1 | tf_op jit(solution)/shard_map/cut_far/pallas_call | solution.py:141
  8.1 0.6 collective-permute-start.1
  8.7 0.4 collective-permute-start.7
  9.1 0.8 collective-permute-done.refs_2_.refs_4_.refs_6_.refs_8_
  10.0 1.0 %first.1 = (bf16[1,3,128,512]{3,2,1,0:T(8,128)(2,1)S(1)}, bf16[2,3,128,512]{3,2,1,0:T(8,128)(2,1)S(1)}, f32[8,128]{1,0:T(8,128)S(1)}, bf16[128,256]{1,0:T(8,128)(2,1)S(1)}) custom-call(s32[18]{0:T(128)S(1)} %compare_select_fusion.6.table_ref.args_0_.table, f32[8,128]{1,0:T(8,128)S(1)} %get-tuple-element.29.refs_0_, bf16[128,128]{1,0:T(8,128)(2,1)S(1)} %bitcast.27, ...), custom_call_target="tpu_custom_call" | custom-call | flops 1 | bytes 1 | tf_op jit(solution)/shard_map/first/pallas_call | solution.py:236
  11.0 1.6 %collective-permute-start.4 = (bf16[2,3,128,512]{3,2,1,0:T(8,128)(2,1)S(1)}, bf16[2,3,128,512]{3,2,1,0:T(8,128)(2,1)S(1)}, u32[]{:S(2)}, u32[]{:S(2)}) collective-permute-start(bf16[2,3,128,512]{3,2,1,0:T(8,128)(2,1)S(1)} %get-tuple-element.37), channel_id=1, source_target_pairs={{0,4},{1,13},{32,36},{33,45},{64,68},{65,77},{96,100},{97,109},{16... | collective-permute-start | bytes 2359304 | tf_op jit(solution)/shard_map/xa1/ppermute | solution.py:93
  12.7 3.2 %collective-permute-start.3 = (bf16[1,3,128,512]{3,2,1,0:T(8,128)(2,1)S(1)}, bf16[1,3,128,512]{3,2,1,0:T(8,128)(2,1)S(1)}, u32[]{:S(2)}, u32[]{:S(2)}) collective-permute-start(bf16[1,3,128,512]{3,2,1,0:T(8,128)(2,1)S(1)} %get-tuple-element.36), channel_id=1, source_target_pairs={{0,2},{1,3},{32,34},{33,35},{64,66},{65,67},{96,98},{97,99},{16,18... | collective-permute-start | bytes 1179656 | tf_op jit(solution)/shard_map/yb1/ppermute | solution.py:93
  15.9 1.1 %second.1 = (bf16[2,3,128,512]{3,2,1,0:T(8,128)(2,1)S(1)}, bf16[2,3,128,512]{3,2,1,0:T(8,128)(2,1)S(1)}, f32[8,128]{1,0:T(8,128)S(1)}) custom-call(s32[18]{0:T(128)S(1)} %compare_select_fusion.6.table_ref.args_0_.table, f32[8,128]{1,0:T(8,128)S(1)} %get-tuple-element.31.refs_0_, bf16[128,256]{1,0:T(8,128)(2,1)S(1)} %get-tuple-element.32.refs_1_.args_3_, ...), custom_call_target="tpu_custom_call" | custom-call | flops 1 | bytes 1 | tf_op jit(solution)/shard_map/second/pallas_call | solution.py:236
  17.0 1.8 %collective-permute-start.5 = (bf16[2,3,128,512]{3,2,1,0:T(8,128)(2,1)S(1)}, bf16[2,3,128,512]{3,2,1,0:T(8,128)(2,1)S(1)}, u32[]{:S(2)}, u32[]{:S(2)}) collective-permute-start(bf16[2,3,128,512]{3,2,1,0:T(8,128)(2,1)S(1)} %get-tuple-element.39), channel_id=1, source_target_pairs={{0,12},{1,5},{32,44},{33,37},{64,76},{65,69},{96,108},{97,101},{16... | collective-permute-start | bytes 2359304 | tf_op jit(solution)/shard_map/xa2/ppermute | solution.py:93
  18.8 0.6 collective-permute-start.6
  19.5 6.5 %collective-permute-done.3.refs_4_ = bf16[1,3,128,512]{3,2,1,0:T(8,128)(2,1)S(1)} collective-permute-done((bf16[1,3,128,512]{3,2,1,0:T(8,128)(2,1)S(1)}, bf16[1,3,128,512]{3,2,1,0:T(8,128)(2,1)S(1)}, u32[]{:S(2)}, u32[]{:S(2)}) %collective-permute-start.3) | collective-permute-done | bytes 393248 | tf_op jit(solution)/shard_map/yb1/ppermute | solution.py:93
  26.0 0.8 collective-permute-done.4.refs_7_.refs_10_
  26.8 1.1 %third.1 = (bf16[1,3,128,512]{3,2,1,0:T(8,128)(2,1)S(1)}, bf16[2,3,128,512]{3,2,1,0:T(8,128)(2,1)S(1)}, bf16[1,3,128,512]{3,2,1,0:T(8,128)(2,1)S(1)}, f32[8,128]{1,0:T(8,128)S(1)}) custom-call(s32[18]{0:T(128)S(1)} %compare_select_fusion.6.table_ref.args_0_.table, f32[8,128]{1,0:T(8,128)S(1)} %get-tuple-element.34.refs_0_, ...), custom_call_target="tpu_custom_call" | custom-call | flops 1 | bytes 1 | tf_op jit(solution)/shard_map/third/pallas_call | solution.py:236
  28.0 1.7 %collective-permute-start.8 = (bf16[2,3,128,512]{3,2,1,0:T(8,128)(2,1)S(1)}, bf16[2,3,128,512]{3,2,1,0:T(8,128)(2,1)S(1)}, u32[]{:S(2)}, u32[]{:S(2)}) collective-permute-start(bf16[2,3,128,512]{3,2,1,0:T(8,128)(2,1)S(1)} %get-tuple-element.42), channel_id=1, source_target_pairs={{0,4},{1,13},{32,36},{33,45},{64,68},{65,77},{96,100},{97,109},{16... | collective-permute-start | bytes 2359304 | tf_op jit(solution)/shard_map/xa3/ppermute | solution.py:93
  29.7 2.5 %collective-permute-start.9 = (bf16[1,3,128,512]{3,2,1,0:T(8,128)(2,1)S(1)}, bf16[1,3,128,512]{3,2,1,0:T(8,128)(2,1)S(1)}, u32[]{:S(2)}, u32[]{:S(2)}) collective-permute-start(bf16[1,3,128,512]{3,2,1,0:T(8,128)(2,1)S(1)} %get-tuple-element.44), channel_id=1, source_target_pairs={{0,4},{1,13},{32,36},{33,45},{64,68},{65,77},{96,100},{97,109},{16... | collective-permute-start | bytes 1179656 | tf_op jit(solution)/shard_map/xb1/ppermute | solution.py:93
  32.2 5.2 %collective-permute-start.11 = (bf16[1,3,128,512]{3,2,1,0:T(8,128)(2,1)S(1)}, bf16[1,3,128,512]{3,2,1,0:T(8,128)(2,1)S(1)}, u32[]{:S(2)}, u32[]{:S(2)}) collective-permute-start(bf16[1,3,128,512]{3,2,1,0:T(8,128)(2,1)S(1)} %get-tuple-element.47), channel_id=1, source_target_pairs={{0,2},{1,3},{32,34},{33,35},{64,66},{65,67},{96,98},{97,99},{16,18... | collective-permute-start | bytes 1179656 | tf_op jit(solution)/shard_map/yb3/ppermute | solution.py:93
  37.4 5.4 %collective-permute-done.6.refs_2_.refs_4_.refs_8_ = bf16[2,3,128,512]{3,2,1,0:T(8,128)(2,1)S(1)} collective-permute-done((bf16[2,3,128,512]{3,2,1,0:T(8,128)(2,1)S(1)}, bf16[2,3,128,512]{3,2,1,0:T(8,128)(2,1)S(1)}, u32[]{:S(2)}, u32[]{:S(2)}) %collective-permute-start.6) | collective-permute-done | bytes 786464 | tf_op jit(solution)/shard_map/yb2/ppermute | solution.py:93
  42.9 0.8 fourth.1
  43.7 4.6 %collective-permute-start.10 = (bf16[1,3,128,512]{3,2,1,0:T(8,128)(2,1)S(1)}, bf16[1,3,128,512]{3,2,1,0:T(8,128)(2,1)S(1)}, u32[]{:S(2)}, u32[]{:S(2)}) collective-permute-start(bf16[1,3,128,512]{3,2,1,0:T(8,128)(2,1)S(1)} %get-tuple-element.46), channel_id=1, source_target_pairs={{0,2},{1,3},{32,34},{33,35},{64,66},{65,67},{96,98},{97,99},{16,18... | collective-permute-start | bytes 1179656 | tf_op jit(solution)/shard_map/ya/ppermute | solution.py:93
  48.4 1.0 fifth.1
  49.4 1.8 %collective-permute-start.12 = (bf16[1,3,128,512]{3,2,1,0:T(8,128)(2,1)S(1)}, bf16[1,3,128,512]{3,2,1,0:T(8,128)(2,1)S(1)}, u32[]{:S(2)}, u32[]{:S(2)}) collective-permute-start(bf16[1,3,128,512]{3,2,1,0:T(8,128)(2,1)S(1)} %get-tuple-element.48), channel_id=1, source_target_pairs={{0,12},{1,5},{32,44},{33,37},{64,76},{65,69},{96,108},{97,101},{16... | collective-permute-start | bytes 1179656 | tf_op jit(solution)/shard_map/xb2/ppermute | solution.py:93
  51.2 0.3 collective-permute-start.13
  51.5 8.2 %collective-permute-done.10.refs_1_.args_13_ = bf16[1,3,128,512]{3,2,1,0:T(8,128)(2,1)S(1)} collective-permute-done((bf16[1,3,128,512]{3,2,1,0:T(8,128)(2,1)S(1)}, bf16[1,3,128,512]{3,2,1,0:T(8,128)(2,1)S(1)}, u32[]{:S(2)}, u32[]{:S(2)}) %collective-permute-start.10) | collective-permute-done | bytes 393248 | tf_op jit(solution)/shard_map/ya/ppermute | solution.py:93
  59.7 0.7 collective-permute-done.13.args_16_
  60.5 11.5 %assemble.1 = (bf16[8,8,5,8,128]{4,3,2,1,0:T(8,128)(2,1)S(1)}, bf16[8,8,5,8,128]{4,3,2,1,0:T(8,128)(2,1)S(1)}) custom-call(s32[18]{0:T(128)S(1)} %compare_select_fusion.6.table_ref.args_0_.table, s32[32]{0:T(128)S(1)} %copy-done.4, f32[8,128]{1,0:T(8,128)S(1)} %pin.3.args_2_, bf16[128,256]{1,0:T(8,128)(2,1)S(1)} %get-tuple-element.32.refs_1_.args_3_, ...), custom_call_target="tpu_custom_call" | custom-call | flops 1 | bytes 1 | tf_op jit(solution)/shard_map/assemble/pallas_call | solution.py:372
  72.2 2.1 %collective-permute-done.14.got_ref = bf16[8,8,5,8,128]{4,3,2,1,0:T(8,128)(2,1)S(1)} collective-permute-done((bf16[8,8,5,8,128]{4,3,2,1,0:T(8,128)(2,1)S(1)}, bf16[8,8,5,8,128]{4,3,2,1,0:T(8,128)(2,1)S(1)}, u32[]{:S(2)}, u32[]{:S(2)}) %collective-permute-start.14) | collective-permute-done | bytes 655392 | tf_op jit(solution)/shard_map/shares/ppermute | solution.py:93
  74.2 0.2 add.82
  74.4 25.5 %all_to_all.5.in_ref = bf16[64,5,8,128]{3,2,1,0:T(8,128)(2,1)S(1)} all-to-all(bf16[64,5,8,128]{3,2,1,0:T(8,128)(2,1)S(1)} %bitcast.25), channel_id=1, replica_groups={{0,2,4,6,8,10,12,14,16,18,20,22,24,26,28,30,32,34,36,38,40,42,44,46,48,..., dimensions={0} | all-to-all | bytes 1310720 | tf_op jit(solution)/shard_map/all_to_all | solution.py:519
  99.9 1.6 %finish.1 = (f32[8,16,32]{2,1,0:T(8,128)}, f32[4,8]{1,0:T(4,128)}) custom-call(s32[18]{0:T(128)S(1)} %compare_select_fusion.6.table_ref.args_0_.table, bf16[64,5,8,128]{3,2,1,0:T(8,128)(2,1)S(1)} %all_to_all.5.in_ref), custom_call_target="tpu_custom_call" | custom-call | tf_op jit(solution)/shard_map/finish/pallas_call | solution.py:437
  (31 shorter events, 0.4 us)
Async XLA Ops:
  1.6 4.6 %copy-start = (bf16[128,6,8192]{2,0,1:T(8,128)(2,1)S(1)}, bf16[128,6,8192]{2,0,1:T(8,128)(2,1)}, u32[]{:S(2)}) copy-start(bf16[128,6,8192]{2,0,1:T(8,128)(2,1)} %param.6) | copy-start | bytes 37748740
  6.9 3.1 %collective-permute-start = (bf16[10,128,512]{2,1,0:T(8,128)(2,1)S(1)}, bf16[10,128,512]{2,1,0:T(8,128)(2,1)S(1)}, u32[]{:S(2)}, u32[]{:S(2)}) collective-permute-start(bf16[10,128,512]{2,1,0:T(8,128)(2,1)S(1)} %get-tuple-element.30), channel_id=1, source_target_pairs={{0,1},{1,0},{32,33},{33,32},{64,65},{65,64},{96,97},{97,96},{16,17... | collective-permute-start | bytes 3932168 | tf_op jit(solution)/shard_map/near/ppermute | solution.py:93
  8.1 7.8 %collective-permute-start.1 = (bf16[12,128,512]{2,1,0:T(8,128)(2,1)S(1)}, bf16[12,128,512]{2,1,0:T(8,128)(2,1)S(1)}, u32[]{:S(2)}, u32[]{:S(2)}) collective-permute-start(bf16[12,128,512]{2,1,0:T(8,128)(2,1)S(1)} %get-tuple-element.33), channel_id=1, source_target_pairs={{0,1},{1,0},{32,33},{33,32},{64,65},{65,64},{96,97},{97,96},{16,17... | collective-permute-start | bytes 4718600 | tf_op jit(solution)/shard_map/far/ppermute | solution.py:93
  8.6 10.2 %collective-permute-start.2 = (bf16[12,128,512]{2,1,0:T(8,128)(2,1)S(1)}, bf16[12,128,512]{2,1,0:T(8,128)(2,1)S(1)}, u32[]{:S(2)}, u32[]{:S(2)}) collective-permute-start(bf16[12,128,512]{2,1,0:T(8,128)(2,1)S(1)} %get-tuple-element.35), channel_id=1, source_target_pairs={{0,1},{1,0},{32,33},{33,32},{64,65},{65,64},{96,97},{97,96},{16,17... | collective-permute-start | bytes 4718600 | tf_op jit(solution)/shard_map/far/ppermute | solution.py:93
  8.7 34.1 %collective-permute-start.7 = (bf16[15,128,512]{2,1,0:T(8,128)(2,1)S(1)}, bf16[15,128,512]{2,1,0:T(8,128)(2,1)S(1)}, u32[]{:S(2)}, u32[]{:S(2)}) collective-permute-start(bf16[15,128,512]{2,1,0:T(8,128)(2,1)S(1)} %get-tuple-element.41), channel_id=1, source_target_pairs={{0,1},{1,0},{32,33},{33,32},{64,65},{65,64},{96,97},{97,96},{16,17... | collective-permute-start | bytes 5898248 | tf_op jit(solution)/shard_map/far/ppermute | solution.py:93
  11.0 15.8 %collective-permute-start.4 = (bf16[2,3,128,512]{3,2,1,0:T(8,128)(2,1)S(1)}, bf16[2,3,128,512]{3,2,1,0:T(8,128)(2,1)S(1)}, u32[]{:S(2)}, u32[]{:S(2)}) collective-permute-start(bf16[2,3,128,512]{3,2,1,0:T(8,128)(2,1)S(1)} %get-tuple-element.37), channel_id=1, source_target_pairs={{0,4},{1,13},{32,36},{33,45},{64,68},{65,77},{96,100},{97,109},{16... | collective-permute-start | bytes 2359304 | tf_op jit(solution)/shard_map/xa1/ppermute | solution.py:93
  12.7 13.3 %collective-permute-start.3 = (bf16[1,3,128,512]{3,2,1,0:T(8,128)(2,1)S(1)}, bf16[1,3,128,512]{3,2,1,0:T(8,128)(2,1)S(1)}, u32[]{:S(2)}, u32[]{:S(2)}) collective-permute-start(bf16[1,3,128,512]{3,2,1,0:T(8,128)(2,1)S(1)} %get-tuple-element.36), channel_id=1, source_target_pairs={{0,2},{1,3},{32,34},{33,35},{64,66},{65,67},{96,98},{97,99},{16,18... | collective-permute-start | bytes 1179656 | tf_op jit(solution)/shard_map/yb1/ppermute | solution.py:93
  17.0 15.2 %collective-permute-start.5 = (bf16[2,3,128,512]{3,2,1,0:T(8,128)(2,1)S(1)}, bf16[2,3,128,512]{3,2,1,0:T(8,128)(2,1)S(1)}, u32[]{:S(2)}, u32[]{:S(2)}) collective-permute-start(bf16[2,3,128,512]{3,2,1,0:T(8,128)(2,1)S(1)} %get-tuple-element.39), channel_id=1, source_target_pairs={{0,12},{1,5},{32,44},{33,37},{64,76},{65,69},{96,108},{97,101},{16... | collective-permute-start | bytes 2359304 | tf_op jit(solution)/shard_map/xa2/ppermute | solution.py:93
  18.8 24.0 %collective-permute-start.6 = (bf16[2,3,128,512]{3,2,1,0:T(8,128)(2,1)S(1)}, bf16[2,3,128,512]{3,2,1,0:T(8,128)(2,1)S(1)}, u32[]{:S(2)}, u32[]{:S(2)}) collective-permute-start(bf16[2,3,128,512]{3,2,1,0:T(8,128)(2,1)S(1)} %get-tuple-element.40), channel_id=1, source_target_pairs={{0,2},{1,3},{32,34},{33,35},{64,66},{65,67},{96,98},{97,99},{16,18... | collective-permute-start | bytes 2359304 | tf_op jit(solution)/shard_map/yb2/ppermute | solution.py:93
  28.0 14.9 %collective-permute-start.8 = (bf16[2,3,128,512]{3,2,1,0:T(8,128)(2,1)S(1)}, bf16[2,3,128,512]{3,2,1,0:T(8,128)(2,1)S(1)}, u32[]{:S(2)}, u32[]{:S(2)}) collective-permute-start(bf16[2,3,128,512]{3,2,1,0:T(8,128)(2,1)S(1)} %get-tuple-element.42), channel_id=1, source_target_pairs={{0,4},{1,13},{32,36},{33,45},{64,68},{65,77},{96,100},{97,109},{16... | collective-permute-start | bytes 2359304 | tf_op jit(solution)/shard_map/xa3/ppermute | solution.py:93
  29.7 18.7 %collective-permute-start.9 = (bf16[1,3,128,512]{3,2,1,0:T(8,128)(2,1)S(1)}, bf16[1,3,128,512]{3,2,1,0:T(8,128)(2,1)S(1)}, u32[]{:S(2)}, u32[]{:S(2)}) collective-permute-start(bf16[1,3,128,512]{3,2,1,0:T(8,128)(2,1)S(1)} %get-tuple-element.44), channel_id=1, source_target_pairs={{0,4},{1,13},{32,36},{33,45},{64,68},{65,77},{96,100},{97,109},{16... | collective-permute-start | bytes 1179656 | tf_op jit(solution)/shard_map/xb1/ppermute | solution.py:93
  32.2 27.5 %collective-permute-start.11 = (bf16[1,3,128,512]{3,2,1,0:T(8,128)(2,1)S(1)}, bf16[1,3,128,512]{3,2,1,0:T(8,128)(2,1)S(1)}, u32[]{:S(2)}, u32[]{:S(2)}) collective-permute-start(bf16[1,3,128,512]{3,2,1,0:T(8,128)(2,1)S(1)} %get-tuple-element.47), channel_id=1, source_target_pairs={{0,2},{1,3},{32,34},{33,35},{64,66},{65,67},{96,98},{97,99},{16,18... | collective-permute-start | bytes 1179656 | tf_op jit(solution)/shard_map/yb3/ppermute | solution.py:93
  43.7 16.0 %collective-permute-start.10 = (bf16[1,3,128,512]{3,2,1,0:T(8,128)(2,1)S(1)}, bf16[1,3,128,512]{3,2,1,0:T(8,128)(2,1)S(1)}, u32[]{:S(2)}, u32[]{:S(2)}) collective-permute-start(bf16[1,3,128,512]{3,2,1,0:T(8,128)(2,1)S(1)} %get-tuple-element.46), channel_id=1, source_target_pairs={{0,2},{1,3},{32,34},{33,35},{64,66},{65,67},{96,98},{97,99},{16,18... | collective-permute-start | bytes 1179656 | tf_op jit(solution)/shard_map/ya/ppermute | solution.py:93
  48.4 12.1 %slice-start = ((s8[12582912]{0:T(1024)(128)(4,1)}), s8[4194304]{0:T(1024)(128)(4,1)S(1)}, s32[]{:S(2)}) async-start(s8[12582912]{0:T(1024)(128)(4,1)} %bitcast.21), calls=%async_computation.1 | async-start | bytes 8388608
  48.4 12.1 %slice-start.1 = ((s8[12582912]{0:T(1024)(128)(4,1)}), s8[4194304]{0:T(1024)(128)(4,1)S(1)}, s32[]{:S(2)}) async-start(s8[12582912]{0:T(1024)(128)(4,1)} %bitcast.21), calls=%async_computation.2 | async-start | bytes 8388608
  48.4 12.1 %slice-start.2 = ((s8[12582912]{0:T(1024)(128)(4,1)}), s8[4194304]{0:T(1024)(128)(4,1)S(1)}, s32[]{:S(2)}) async-start(s8[12582912]{0:T(1024)(128)(4,1)} %bitcast.21), calls=%async_computation.3 | async-start | bytes 8388608
  48.4 12.1 %copy-start.1 = (bf16[512,1536]{1,0:T(8,128)(2,1)S(1)}, bf16[512,1536]{1,0:T(8,128)(2,1)}, u32[]{:S(2)}) copy-start(bf16[512,1536]{1,0:T(8,128)(2,1)} %constant.95.args_4_) | copy-start | bytes 4718596
  48.4 12.1 %copy-start.2 = (f32[3,3,8192]{2,1,0:T(4,128)S(1)}, f32[3,3,8192]{2,1,0:T(4,128)}, u32[]{:S(2)}) copy-start(f32[3,3,8192]{2,1,0:T(4,128)} %args_6_.1) | copy-start | bytes 884740
  48.4 12.1 %copy-start.3 = (f32[8192]{0:T(1024)S(1)}, f32[8192]{0:T(1024)}, u32[]{:S(2)}) copy-start(f32[8192]{0:T(1024)} %param.8) | copy-start | bytes 98308
  48.4 12.1 %copy-start.4 = (s32[32]{0:T(128)S(1)}, s32[32]{0:T(128)}, u32[]{:S(2)}) copy-start(s32[32]{0:T(128)} %args_1_.4) | copy-start | bytes 388
  49.4 10.3 %collective-permute-start.12 = (bf16[1,3,128,512]{3,2,1,0:T(8,128)(2,1)S(1)}, bf16[1,3,128,512]{3,2,1,0:T(8,128)(2,1)S(1)}, u32[]{:S(2)}, u32[]{:S(2)}) collective-permute-start(bf16[1,3,128,512]{3,2,1,0:T(8,128)(2,1)S(1)} %get-tuple-element.48), channel_id=1, source_target_pairs={{0,12},{1,5},{32,44},{33,37},{64,76},{65,69},{96,108},{97,101},{16... | collective-permute-start | bytes 1179656 | tf_op jit(solution)/shard_map/xb2/ppermute | solution.py:93
  51.2 9.3 %collective-permute-start.13 = (bf16[1,3,128,512]{3,2,1,0:T(8,128)(2,1)S(1)}, bf16[1,3,128,512]{3,2,1,0:T(8,128)(2,1)S(1)}, u32[]{:S(2)}, u32[]{:S(2)}) collective-permute-start(bf16[1,3,128,512]{3,2,1,0:T(8,128)(2,1)S(1)} %get-tuple-element.49), channel_id=1, source_target_pairs={{0,4},{1,13},{32,36},{33,45},{64,68},{65,77},{96,100},{97,109},{16... | collective-permute-start | bytes 1179656 | tf_op jit(solution)/shard_map/xb3/ppermute | solution.py:93
  72.1 2.2 %collective-permute-start.14 = (bf16[8,8,5,8,128]{4,3,2,1,0:T(8,128)(2,1)S(1)}, bf16[8,8,5,8,128]{4,3,2,1,0:T(8,128)(2,1)S(1)}, u32[]{:S(2)}, u32[]{:S(2)}) collective-permute-start(bf16[8,8,5,8,128]{4,3,2,1,0:T(8,128)(2,1)S(1)} %get-tuple-element.51), channel_id=1, source_target_pairs={{0,1},{1,0},{32,33},{33,32},{64,65},{65,64},{96,97},{97,96},{16,17... | collective-permute-start | bytes 1966088 | tf_op jit(solution)/shard_map/shares/ppermute | solution.py:93

commit v4 on v3

--- a/solution.py
+++ b/solution.py
@@ -96,6 +96,7 @@
 ITEM = (3, 128, NPE)
 ITEM_BYTES = 3 * 128 * NPE * 2
 MIB = 1024 * 1024
+INSIDE = pl.BlockSpec(memory_space=pltpu.VMEM)
 TINY = pl.CostEstimate(flops=1, bytes_accessed=1, transcendentals=0)
 TABLE = 18
 TOKEN = (8, 128)
@@ -154,18 +155,6 @@
     )(table, fields, *others)
 
 
-def own_spec(half, dx, dy):
-    return pl.BlockSpec(ITEM, lambda i, table, *rest: (half, 0, table[dx * 2 + dy]))
-
-
-def other_spec(row):
-    return pl.BlockSpec(ITEM, lambda i, *rest: (row, 0, 0))
-
-
-def row_spec(row):
-    return pl.BlockSpec((1,) + ITEM, lambda i, *rest: (row, 0, 0, 0))
-
-
 def whole(shape):
     return pl.BlockSpec(shape, lambda i, *rest: (0,) * len(shape))
 
@@ -193,41 +182,39 @@
 
 def sums(shared, items, outs, name, before=(), coefs=None):
     table, fields, coef, chunks = shared
-    operands, specs, plan = [], [], []
-    for (half, dx, dy), adds in items:
-        entry = []
-        other, row = chunks[(half, dx, dy)]
-        for array, spec in [(fields, own_spec(half, dx, dy)), (other, other_spec(row))] + [
-            (array, row_spec(row)) for array, row in adds
-        ]:
-            entry.append(len(operands))
-            operands.append(array)
-            specs.append(spec)
-        plan.append(entry)
-    if coefs is None:
-        first, first_specs = [coef], [whole((128, 256))]
-    else:
-        first = list(coefs)
-        first_specs = [whole((128, 128)), pl.BlockSpec((1, 128, 128), lambda i, table: (9, 0, 0))]
+    moved = [fields]
+    for key, adds in items:
+        for array in [chunks[key][0]] + [array for array, row in adds]:
+            if not any(array is known for known in moved):
+                moved.append(array)
+
+    def index(array):
+        return [array is known for known in moved].index(True)
+
+    first = [coef] if coefs is None else list(coefs)
 
     def kernel(table_ref, *refs):
         refs = refs[len(before) :]
         if coefs is None:
             rows = refs[0][...]
         else:
-            rows = jnp.concatenate([refs[0][...], refs[1][0]], axis=1)
+            rows = jnp.concatenate([refs[0][...], refs[1][9, :, :128]], axis=1)
         refs = refs[len(first) :]
-        ins, results = refs[: len(operands)], refs[len(operands) :]
+        ins, results = refs[: len(moved)], refs[len(moved) :]
         results[len(outs)][...] = jnp.zeros(TOKEN, F32)
         if coefs is not None:
             results[-1][...] = rows
         for number, group in enumerate(outs):
             for position, item in enumerate(group):
-                own, other, *adds = plan[item]
+                (half, dx, dy), adds = items[item]
+                chunk, row = chunks[(half, dx, dy)]
+                lanes = pl.ds(pl.multiple_of(table_ref[dx * 2 + dy] * NPE, NPE), NPE)
+                own = ins[0].at[pl.ds(half * 3, 3), :, lanes]
+                other = ins[index(chunk)].at[pl.ds(row * 3, 3)]
                 for c in range(3):
-                    total = project(rows, ins[own], ins[other], c)
-                    for add in adds:
-                        total = total + ins[add][0, c].astype(F32)
+                    total = project(rows, own, other, c)
+                    for array, place_in in adds:
+                        total = total + ins[index(array)][place_in, c].astype(F32)
                     results[number][position, c] = total.astype(BF)
 
     shapes = [bf16(len(group), *ITEM) for group in outs] + [jax.ShapeDtypeStruct(TOKEN, F32)]
@@ -235,28 +222,31 @@
         shapes.append(bf16(128, 256))
     return pl.pallas_call(
         kernel,
-        grid_spec=pltpu.PrefetchScalarGridSpec(
-            num_scalar_prefetch=1,
-            grid=(1,),
-            in_specs=[pl.BlockSpec(memory_space=pl.ANY)] * len(before) + first_specs + specs,
-            out_specs=[whole(shape.shape) for shape in shapes],
-        ),
+        in_specs=[pl.BlockSpec(memory_space=pltpu.SMEM)]
+        + [pl.BlockSpec(memory_space=pl.ANY)] * len(before)
+        + [INSIDE] * (len(first) + len(moved)),
+        out_specs=[INSIDE] * len(shapes),
         out_shape=shapes,
         compiler_params=pltpu.CompilerParams(vmem_limit_bytes=16 * MIB),
         cost_estimate=TINY,
         name=name,
-    )(table, *before, *first, *operands)
+    )(table, *before, *first, *moved)
 
 
 KG = 8
 BLOCKS = 32 // KG + 1
 
 
-def assemble_kernel(counts, table, out_modes, token, coef_ref, tables_ref, weight_ref, metric_ref, *refs):
-    fields_u, refs = refs[:2], refs[2:]
-    fields_b, refs = refs[:2], refs[2:]
-    adds_u, refs = refs[: counts[0]], refs[counts[0] :]
-    adds_b, refs = refs[: counts[1]], refs[counts[1] :]
+def assemble_kernel(rows, table, out_modes, token, coef_ref, tables_ref, weight_ref, metric_ref, *refs):
+    count = len(rows[1]) + len(rows[2])
+    fields_ref, chunk_ref, *add_refs = refs[: count + 2]
+    refs = refs[count + 2 :]
+    lanes = pl.ds(pl.multiple_of(table[0] * NPE, NPE), NPE)
+    fields_u, fields_b = [
+        [fields_ref.at[pl.ds(3 * half, 3), :, lanes], chunk_ref.at[pl.ds(3 * rows[0][half], 3)]] for half in range(2)
+    ]
+    adds_u = [ref.at[row] for ref, row in zip(add_refs, rows[1])]
+    adds_b = [ref.at[row] for ref, row in zip(add_refs[len(adds_u) :], rows[2])]
     keep_ref, send_ref, z_ref, g_ref, cb_ref, pick_k, pick_d = refs
     first = table[17] == 0
 
@@ -280,10 +270,10 @@
     for a in range(3):
         u = project(coef, *fields_u, a)
         for ref in adds_u:
-            u = u + ref[0, a].astype(F32)
+            u = u + ref[a].astype(F32)
         b = project(coef, *fields_b, a)
         for ref in adds_b:
-            b = b + ref[0, a].astype(F32)
+            b = b + ref[a].astype(F32)
         for sign, z in ((0, u + b), (1, u - b)):
             z = z.astype(BF)
             z_ref[sign, a * 128 : a * 128 + 128] = z
@@ -364,10 +354,13 @@
 def assemble(shared, out_modes, tables, weights, metric, adds_u, adds_b, token):
     table, fields, coef, chunks = shared
 
+    adds = adds_u + adds_b
+    (chunk, row_u), (same, row_b) = chunks[(0, 0, 0)], chunks[(1, 0, 0)]
+    rows = ((row_u, row_b), [row for array, row in adds_u], [row for array, row in adds_b])
+
     def kernel(*args):
-        assemble_kernel((len(adds_u), len(adds_b)), *args)
-
-    adds = adds_u + adds_b
+        assemble_kernel(rows, *args)
+
     out = bf16(8, 8, BLOCKS, 8, 128)
     return pl.pallas_call(
         kernel,
@@ -380,13 +373,9 @@
                 whole(tables.shape),
                 pl.BlockSpec((1, NPE), lambda i, table, chosen: (0, table[0])),
                 pl.BlockSpec((3, 3, NPE), lambda i, table, chosen: (0, 0, table[0])),
-                own_spec(0, 0, 0),
-                other_spec(chunks[(0, 0, 0)][1]),
-                own_spec(1, 0, 0),
-                other_spec(chunks[(1, 0, 0)][1]),
             ]
-            + [row_spec(row) for array, row in adds],
-            out_specs=[whole(out.shape)] * 2,
+            + [INSIDE] * (2 + len(adds)),
+            out_specs=[INSIDE] * 2,
             scratch_shapes=[
                 pltpu.VMEM((2, 384, NPE), BF),
                 pltpu.VMEM((2, 3, 3, 128, NPE), BF),
@@ -399,7 +388,7 @@
         compiler_params=pltpu.CompilerParams(vmem_limit_bytes=32 * MIB),
         cost_estimate=TINY,
         name="assemble",
-    )(table, out_modes, token, coef, tables, weights, metric, fields, chunks[(0, 0, 0)][0], fields, chunks[(1, 0, 0)][0],
+    )(table, out_modes, token, coef, tables, weights, metric, fields, chunk,
       *[array for array, row in adds])
 
 
@@ -436,12 +425,8 @@
 def finish(table, shares):
     return pl.pallas_call(
         finish_kernel,
-        grid_spec=pltpu.PrefetchScalarGridSpec(
-            num_scalar_prefetch=1,
-            grid=(1,),
-            in_specs=[whole(shares.shape)],
-            out_specs=[whole((8, 16, 32)), whole((4, 8))],
-        ),
+        in_specs=[pl.BlockSpec(memory_space=pltpu.SMEM), INSIDE],
+        out_specs=[INSIDE] * 2,
         out_shape=[jax.ShapeDtypeStruct((8, 16, 32), F32), jax.ShapeDtypeStruct((4, 8), F32)],
         compiler_params=pltpu.CompilerParams(vmem_limit_bytes=12 * MIB),
         name="finish",

time: 102 us -> 102 us (level)
  no operation moved by 1% of the time
where the time goes in v4:
time: 102 us
  blocking collectives  25.5 us (25%)
  starting transfers between devices  24.8 us (24%)
  waiting for transfers between devices  24.6 us (24%)
  Pallas kernels  20.3 us (20%)
  local copies, waits for them, and re-layouts  5.47 us (5%)
    all_to_all x1, blocking collectives, on_device(): lax.all_to_all(shares, AXES, 0, 0, axis_index_groups=SAME_CORE, tiled=True)  25.5 us
    ppermute x15, starting transfers between devices, send(): return lax.ppermute(value, AXES, pairs)  24.8 us
    ppermute x15, waiting for transfers between devices, send(): return lax.ppermute(value, AXES, pairs)  24.6 us
    pallas_call x1, Pallas kernels, assemble(): pl.pallas_call(kernel, grid_spec=pltpu.PrefetchScalarGridSpec(num_scalar_...  11.5 us
    unnamed x17, local copies, waits for them, and re-layouts  5.47 us
    pallas_call x5, Pallas kernels, sums(): pl.pallas_call(kernel, in_specs=[pl.BlockSpec(memory_space=pltpu.SMEM)] +...  5.13 us
  transfers between devices with their start and end apart: 15, of which 7 were waited for; matrix products, arithmetic and copies ran while one was open for 0% of the time, Pallas kernels for 6%

profile of v4, /device:TPU:0, one launch (start us, length us, event | category | flops | bytes accessed | tf_op | source)
XLA Modules:
  0.0 101.6 jit_solution(11734736683993443944)
XLA Ops:
  0.7 0.9 copy.8
  1.6 4.6 %copy-done = bf16[128,6,8192]{2,0,1:T(8,128)(2,1)S(1)} copy-done((bf16[128,6,8192]{2,0,1:T(8,128)(2,1)S(1)}, bf16[128,6,8192]{2,0,1:T(8,128)(2,1)}, u32[]{:S(2)}) %copy-start) | copy-done | bytes 12582936
  6.2 0.7 cut_near.1
  7.0 1.1 %cut_far.1 = (bf16[12,128,512]{2,1,0:T(8,128)(2,1)S(1)}, bf16[12,128,512]{2,1,0:T(8,128)(2,1)S(1)}, bf16[15,128,512]{2,1,0:T(8,128)(2,1)S(1)}, f32[8,128]{1,0:T(8,128)S(1)}) custom-call(s32[18]{0:T(128)S(1)} %compare_select_fusion.6.table_ref.args_0_.table, bf16[6,128,8192]{2,1,0:T(8,128)(2,1)S(1)} %bitcast.6, f32[8,128]{1,0:T(8,128)S(1)} %get-tuple-element.28.token_in), custom_call_target="tpu_custom_call" | custom-call | flops 1 | bytes 1 | tf_op jit(solution)/shard_map/cut_far/pallas_call | solution.py:142
  8.1 0.6 collective-permute-start.1
  8.7 0.4 collective-permute-start.7
  9.1 0.8 collective-permute-done.refs_2_.refs_4_
  10.0 1.0 %first.1 = (bf16[1,3,128,512]{3,2,1,0:T(8,128)(2,1)S(1)}, bf16[2,3,128,512]{3,2,1,0:T(8,128)(2,1)S(1)}, f32[8,128]{1,0:T(8,128)S(1)}, bf16[128,256]{1,0:T(8,128)(2,1)S(1)}) custom-call(s32[18]{0:T(128)S(1)} %compare_select_fusion.6.table_ref.args_0_.table, f32[8,128]{1,0:T(8,128)S(1)} %get-tuple-element.29.refs_0_, bf16[128,128]{1,0:T(8,128)(2,1)S(1)} %bitcast.17, ...), custom_call_target="tpu_custom_call" | custom-call | flops 1 | bytes 1 | tf_op jit(solution)/shard_map/first/pallas_call | solution.py:223
  11.0 1.6 %collective-permute-start.4 = (bf16[2,3,128,512]{3,2,1,0:T(8,128)(2,1)S(1)}, bf16[2,3,128,512]{3,2,1,0:T(8,128)(2,1)S(1)}, u32[]{:S(2)}, u32[]{:S(2)}) collective-permute-start(bf16[2,3,128,512]{3,2,1,0:T(8,128)(2,1)S(1)} %get-tuple-element.37), channel_id=1, source_target_pairs={{0,4},{1,13},{32,36},{33,45},{64,68},{65,77},{96,100},{97,109},{16... | collective-permute-start | bytes 2359304 | tf_op jit(solution)/shard_map/xa1/ppermute | solution.py:93
  12.7 3.2 %collective-permute-start.3 = (bf16[1,3,128,512]{3,2,1,0:T(8,128)(2,1)S(1)}, bf16[1,3,128,512]{3,2,1,0:T(8,128)(2,1)S(1)}, u32[]{:S(2)}, u32[]{:S(2)}) collective-permute-start(bf16[1,3,128,512]{3,2,1,0:T(8,128)(2,1)S(1)} %get-tuple-element.36), channel_id=1, source_target_pairs={{0,2},{1,3},{32,34},{33,35},{64,66},{65,67},{96,98},{97,99},{16,18... | collective-permute-start | bytes 1179656 | tf_op jit(solution)/shard_map/yb1/ppermute | solution.py:93
  15.9 1.1 %second.1 = (bf16[2,3,128,512]{3,2,1,0:T(8,128)(2,1)S(1)}, bf16[2,3,128,512]{3,2,1,0:T(8,128)(2,1)S(1)}, f32[8,128]{1,0:T(8,128)S(1)}) custom-call(s32[18]{0:T(128)S(1)} %compare_select_fusion.6.table_ref.args_0_.table, f32[8,128]{1,0:T(8,128)S(1)} %get-tuple-element.31.refs_0_, bf16[128,256]{1,0:T(8,128)(2,1)S(1)} %get-tuple-element.32.refs_1_.args_3_, ...), custom_call_target="tpu_custom_call" | custom-call | flops 1 | bytes 1 | tf_op jit(solution)/shard_map/second/pallas_call | solution.py:223
  17.0 1.8 %collective-permute-start.5 = (bf16[2,3,128,512]{3,2,1,0:T(8,128)(2,1)S(1)}, bf16[2,3,128,512]{3,2,1,0:T(8,128)(2,1)S(1)}, u32[]{:S(2)}, u32[]{:S(2)}) collective-permute-start(bf16[2,3,128,512]{3,2,1,0:T(8,128)(2,1)S(1)} %get-tuple-element.39), channel_id=1, source_target_pairs={{0,12},{1,5},{32,44},{33,37},{64,76},{65,69},{96,108},{97,101},{16... | collective-permute-start | bytes 2359304 | tf_op jit(solution)/shard_map/xa2/ppermute | solution.py:93
  18.8 0.7 collective-permute-start.6
  19.5 6.5 %collective-permute-done.3.refs_4_ = bf16[1,3,128,512]{3,2,1,0:T(8,128)(2,1)S(1)} collective-permute-done((bf16[1,3,128,512]{3,2,1,0:T(8,128)(2,1)S(1)}, bf16[1,3,128,512]{3,2,1,0:T(8,128)(2,1)S(1)}, u32[]{:S(2)}, u32[]{:S(2)}) %collective-permute-start.3) | collective-permute-done | bytes 393248 | tf_op jit(solution)/shard_map/yb1/ppermute | solution.py:93
  26.0 0.8 collective-permute-done.4.refs_5_
  26.8 1.2 %third.1 = (bf16[1,3,128,512]{3,2,1,0:T(8,128)(2,1)S(1)}, bf16[2,3,128,512]{3,2,1,0:T(8,128)(2,1)S(1)}, bf16[1,3,128,512]{3,2,1,0:T(8,128)(2,1)S(1)}, f32[8,128]{1,0:T(8,128)S(1)}) custom-call(s32[18]{0:T(128)S(1)} %compare_select_fusion.6.table_ref.args_0_.table, f32[8,128]{1,0:T(8,128)S(1)} %get-tuple-element.34.refs_0_, ...), custom_call_target="tpu_custom_call" | custom-call | flops 1 | bytes 1 | tf_op jit(solution)/shard_map/third/pallas_call | solution.py:223
  28.0 1.7 %collective-permute-start.8 = (bf16[2,3,128,512]{3,2,1,0:T(8,128)(2,1)S(1)}, bf16[2,3,128,512]{3,2,1,0:T(8,128)(2,1)S(1)}, u32[]{:S(2)}, u32[]{:S(2)}) collective-permute-start(bf16[2,3,128,512]{3,2,1,0:T(8,128)(2,1)S(1)} %get-tuple-element.42), channel_id=1, source_target_pairs={{0,4},{1,13},{32,36},{33,45},{64,68},{65,77},{96,100},{97,109},{16... | collective-permute-start | bytes 2359304 | tf_op jit(solution)/shard_map/xa3/ppermute | solution.py:93
  29.7 2.5 %collective-permute-start.9 = (bf16[1,3,128,512]{3,2,1,0:T(8,128)(2,1)S(1)}, bf16[1,3,128,512]{3,2,1,0:T(8,128)(2,1)S(1)}, u32[]{:S(2)}, u32[]{:S(2)}) collective-permute-start(bf16[1,3,128,512]{3,2,1,0:T(8,128)(2,1)S(1)} %get-tuple-element.44), channel_id=1, source_target_pairs={{0,4},{1,13},{32,36},{33,45},{64,68},{65,77},{96,100},{97,109},{16... | collective-permute-start | bytes 1179656 | tf_op jit(solution)/shard_map/xb1/ppermute | solution.py:93
  32.2 5.2 %collective-permute-start.11 = (bf16[1,3,128,512]{3,2,1,0:T(8,128)(2,1)S(1)}, bf16[1,3,128,512]{3,2,1,0:T(8,128)(2,1)S(1)}, u32[]{:S(2)}, u32[]{:S(2)}) collective-permute-start(bf16[1,3,128,512]{3,2,1,0:T(8,128)(2,1)S(1)} %get-tuple-element.47), channel_id=1, source_target_pairs={{0,2},{1,3},{32,34},{33,35},{64,66},{65,67},{96,98},{97,99},{16,18... | collective-permute-start | bytes 1179656 | tf_op jit(solution)/shard_map/yb3/ppermute | solution.py:93
  37.4 5.4 %collective-permute-done.6.refs_2_.refs_4_ = bf16[2,3,128,512]{3,2,1,0:T(8,128)(2,1)S(1)} collective-permute-done((bf16[2,3,128,512]{3,2,1,0:T(8,128)(2,1)S(1)}, bf16[2,3,128,512]{3,2,1,0:T(8,128)(2,1)S(1)}, u32[]{:S(2)}, u32[]{:S(2)}) %collective-permute-start.6) | collective-permute-done | bytes 786464 | tf_op jit(solution)/shard_map/yb2/ppermute | solution.py:93
  42.9 0.8 fourth.1
  43.7 4.7 %collective-permute-start.10 = (bf16[1,3,128,512]{3,2,1,0:T(8,128)(2,1)S(1)}, bf16[1,3,128,512]{3,2,1,0:T(8,128)(2,1)S(1)}, u32[]{:S(2)}, u32[]{:S(2)}) collective-permute-start(bf16[1,3,128,512]{3,2,1,0:T(8,128)(2,1)S(1)} %get-tuple-element.46), channel_id=1, source_target_pairs={{0,2},{1,3},{32,34},{33,35},{64,66},{65,67},{96,98},{97,99},{16,18... | collective-permute-start | bytes 1179656 | tf_op jit(solution)/shard_map/ya/ppermute | solution.py:93
  48.4 1.0 fifth.1
  49.4 1.8 %collective-permute-start.12 = (bf16[1,3,128,512]{3,2,1,0:T(8,128)(2,1)S(1)}, bf16[1,3,128,512]{3,2,1,0:T(8,128)(2,1)S(1)}, u32[]{:S(2)}, u32[]{:S(2)}) collective-permute-start(bf16[1,3,128,512]{3,2,1,0:T(8,128)(2,1)S(1)} %get-tuple-element.48), channel_id=1, source_target_pairs={{0,12},{1,5},{32,44},{33,37},{64,76},{65,69},{96,108},{97,101},{16... | collective-permute-start | bytes 1179656 | tf_op jit(solution)/shard_map/xb2/ppermute | solution.py:93
  51.2 0.3 collective-permute-start.13
  51.5 8.2 %collective-permute-done.10.refs_1_.args_11_ = bf16[1,3,128,512]{3,2,1,0:T(8,128)(2,1)S(1)} collective-permute-done((bf16[1,3,128,512]{3,2,1,0:T(8,128)(2,1)S(1)}, bf16[1,3,128,512]{3,2,1,0:T(8,128)(2,1)S(1)}, u32[]{:S(2)}, u32[]{:S(2)}) %collective-permute-start.10) | collective-permute-done | bytes 393248 | tf_op jit(solution)/shard_map/ya/ppermute | solution.py:93
  59.7 0.7 collective-permute-done.13.args_14_
  60.5 11.5 %assemble.1 = (bf16[8,8,5,8,128]{4,3,2,1,0:T(8,128)(2,1)S(1)}, bf16[8,8,5,8,128]{4,3,2,1,0:T(8,128)(2,1)S(1)}) custom-call(s32[18]{0:T(128)S(1)} %compare_select_fusion.6.table_ref.args_0_.table, s32[32]{0:T(128)S(1)} %copy-done.4, f32[8,128]{1,0:T(8,128)S(1)} %pin.3.args_2_, bf16[128,256]{1,0:T(8,128)(2,1)S(1)} %get-tuple-element.32.refs_1_.args_3_, ...), custom_call_target="tpu_custom_call" | custom-call | flops 1 | bytes 1 | tf_op jit(solution)/shard_map/assemble/pallas_call | solution.py:365
  72.1 2.1 %collective-permute-done.14.got_ref = bf16[8,8,5,8,128]{4,3,2,1,0:T(8,128)(2,1)S(1)} collective-permute-done((bf16[8,8,5,8,128]{4,3,2,1,0:T(8,128)(2,1)S(1)}, bf16[8,8,5,8,128]{4,3,2,1,0:T(8,128)(2,1)S(1)}, u32[]{:S(2)}, u32[]{:S(2)}) %collective-permute-start.14) | collective-permute-done | bytes 655392 | tf_op jit(solution)/shard_map/shares/ppermute | solution.py:93
  74.2 0.2 add.82
  74.4 25.5 %all_to_all.5.in_ref = bf16[64,5,8,128]{3,2,1,0:T(8,128)(2,1)S(1)} all-to-all(bf16[64,5,8,128]{3,2,1,0:T(8,128)(2,1)S(1)} %bitcast.15), channel_id=1, replica_groups={{0,2,4,6,8,10,12,14,16,18,20,22,24,26,28,30,32,34,36,38,40,42,44,46,48,..., dimensions={0} | all-to-all | bytes 1310720 | tf_op jit(solution)/shard_map/all_to_all | solution.py:504
  99.9 1.6 %finish.1 = (f32[8,16,32]{2,1,0:T(8,128)}, f32[4,8]{1,0:T(4,128)}) custom-call(s32[18]{0:T(128)S(1)} %compare_select_fusion.6.table_ref.args_0_.table, bf16[64,5,8,128]{3,2,1,0:T(8,128)(2,1)S(1)} %all_to_all.5.in_ref), custom_call_target="tpu_custom_call" | custom-call | tf_op jit(solution)/shard_map/finish/pallas_call | solution.py:426
  (31 shorter events, 0.4 us)
Async XLA Ops:
  1.6 4.6 %copy-start = (bf16[128,6,8192]{2,0,1:T(8,128)(2,1)S(1)}, bf16[128,6,8192]{2,0,1:T(8,128)(2,1)}, u32[]{:S(2)}) copy-start(bf16[128,6,8192]{2,0,1:T(8,128)(2,1)} %param.6) | copy-start | bytes 37748740
  6.9 3.1 %collective-permute-start = (bf16[10,128,512]{2,1,0:T(8,128)(2,1)S(1)}, bf16[10,128,512]{2,1,0:T(8,128)(2,1)S(1)}, u32[]{:S(2)}, u32[]{:S(2)}) collective-permute-start(bf16[10,128,512]{2,1,0:T(8,128)(2,1)S(1)} %get-tuple-element.30), channel_id=1, source_target_pairs={{0,1},{1,0},{32,33},{33,32},{64,65},{65,64},{96,97},{97,96},{16,17... | collective-permute-start | bytes 3932168 | tf_op jit(solution)/shard_map/near/ppermute | solution.py:93
  8.1 7.8 %collective-permute-start.1 = (bf16[12,128,512]{2,1,0:T(8,128)(2,1)S(1)}, bf16[12,128,512]{2,1,0:T(8,128)(2,1)S(1)}, u32[]{:S(2)}, u32[]{:S(2)}) collective-permute-start(bf16[12,128,512]{2,1,0:T(8,128)(2,1)S(1)} %get-tuple-element.33), channel_id=1, source_target_pairs={{0,1},{1,0},{32,33},{33,32},{64,65},{65,64},{96,97},{97,96},{16,17... | collective-permute-start | bytes 4718600 | tf_op jit(solution)/shard_map/far/ppermute | solution.py:93
  8.6 10.2 %collective-permute-start.2 = (bf16[12,128,512]{2,1,0:T(8,128)(2,1)S(1)}, bf16[12,128,512]{2,1,0:T(8,128)(2,1)S(1)}, u32[]{:S(2)}, u32[]{:S(2)}) collective-permute-start(bf16[12,128,512]{2,1,0:T(8,128)(2,1)S(1)} %get-tuple-element.35), channel_id=1, source_target_pairs={{0,1},{1,0},{32,33},{33,32},{64,65},{65,64},{96,97},{97,96},{16,17... | collective-permute-start | bytes 4718600 | tf_op jit(solution)/shard_map/far/ppermute | solution.py:93
  8.7 34.1 %collective-permute-start.7 = (bf16[15,128,512]{2,1,0:T(8,128)(2,1)S(1)}, bf16[15,128,512]{2,1,0:T(8,128)(2,1)S(1)}, u32[]{:S(2)}, u32[]{:S(2)}) collective-permute-start(bf16[15,128,512]{2,1,0:T(8,128)(2,1)S(1)} %get-tuple-element.41), channel_id=1, source_target_pairs={{0,1},{1,0},{32,33},{33,32},{64,65},{65,64},{96,97},{97,96},{16,17... | collective-permute-start | bytes 5898248 | tf_op jit(solution)/shard_map/far/ppermute | solution.py:93
  11.0 15.8 %collective-permute-start.4 = (bf16[2,3,128,512]{3,2,1,0:T(8,128)(2,1)S(1)}, bf16[2,3,128,512]{3,2,1,0:T(8,128)(2,1)S(1)}, u32[]{:S(2)}, u32[]{:S(2)}) collective-permute-start(bf16[2,3,128,512]{3,2,1,0:T(8,128)(2,1)S(1)} %get-tuple-element.37), channel_id=1, source_target_pairs={{0,4},{1,13},{32,36},{33,45},{64,68},{65,77},{96,100},{97,109},{16... | collective-permute-start | bytes 2359304 | tf_op jit(solution)/shard_map/xa1/ppermute | solution.py:93
  12.7 13.3 %collective-permute-start.3 = (bf16[1,3,128,512]{3,2,1,0:T(8,128)(2,1)S(1)}, bf16[1,3,128,512]{3,2,1,0:T(8,128)(2,1)S(1)}, u32[]{:S(2)}, u32[]{:S(2)}) collective-permute-start(bf16[1,3,128,512]{3,2,1,0:T(8,128)(2,1)S(1)} %get-tuple-element.36), channel_id=1, source_target_pairs={{0,2},{1,3},{32,34},{33,35},{64,66},{65,67},{96,98},{97,99},{16,18... | collective-permute-start | bytes 1179656 | tf_op jit(solution)/shard_map/yb1/ppermute | solution.py:93
  17.0 15.2 %collective-permute-start.5 = (bf16[2,3,128,512]{3,2,1,0:T(8,128)(2,1)S(1)}, bf16[2,3,128,512]{3,2,1,0:T(8,128)(2,1)S(1)}, u32[]{:S(2)}, u32[]{:S(2)}) collective-permute-start(bf16[2,3,128,512]{3,2,1,0:T(8,128)(2,1)S(1)} %get-tuple-element.39), channel_id=1, source_target_pairs={{0,12},{1,5},{32,44},{33,37},{64,76},{65,69},{96,108},{97,101},{16... | collective-permute-start | bytes 2359304 | tf_op jit(solution)/shard_map/xa2/ppermute | solution.py:93
  18.8 24.0 %collective-permute-start.6 = (bf16[2,3,128,512]{3,2,1,0:T(8,128)(2,1)S(1)}, bf16[2,3,128,512]{3,2,1,0:T(8,128)(2,1)S(1)}, u32[]{:S(2)}, u32[]{:S(2)}) collective-permute-start(bf16[2,3,128,512]{3,2,1,0:T(8,128)(2,1)S(1)} %get-tuple-element.40), channel_id=1, source_target_pairs={{0,2},{1,3},{32,34},{33,35},{64,66},{65,67},{96,98},{97,99},{16,18... | collective-permute-start | bytes 2359304 | tf_op jit(solution)/shard_map/yb2/ppermute | solution.py:93
  28.0 14.9 %collective-permute-start.8 = (bf16[2,3,128,512]{3,2,1,0:T(8,128)(2,1)S(1)}, bf16[2,3,128,512]{3,2,1,0:T(8,128)(2,1)S(1)}, u32[]{:S(2)}, u32[]{:S(2)}) collective-permute-start(bf16[2,3,128,512]{3,2,1,0:T(8,128)(2,1)S(1)} %get-tuple-element.42), channel_id=1, source_target_pairs={{0,4},{1,13},{32,36},{33,45},{64,68},{65,77},{96,100},{97,109},{16... | collective-permute-start | bytes 2359304 | tf_op jit(solution)/shard_map/xa3/ppermute | solution.py:93
  29.7 18.7 %collective-permute-start.9 = (bf16[1,3,128,512]{3,2,1,0:T(8,128)(2,1)S(1)}, bf16[1,3,128,512]{3,2,1,0:T(8,128)(2,1)S(1)}, u32[]{:S(2)}, u32[]{:S(2)}) collective-permute-start(bf16[1,3,128,512]{3,2,1,0:T(8,128)(2,1)S(1)} %get-tuple-element.44), channel_id=1, source_target_pairs={{0,4},{1,13},{32,36},{33,45},{64,68},{65,77},{96,100},{97,109},{16... | collective-permute-start | bytes 1179656 | tf_op jit(solution)/shard_map/xb1/ppermute | solution.py:93
  32.2 27.5 %collective-permute-start.11 = (bf16[1,3,128,512]{3,2,1,0:T(8,128)(2,1)S(1)}, bf16[1,3,128,512]{3,2,1,0:T(8,128)(2,1)S(1)}, u32[]{:S(2)}, u32[]{:S(2)}) collective-permute-start(bf16[1,3,128,512]{3,2,1,0:T(8,128)(2,1)S(1)} %get-tuple-element.47), channel_id=1, source_target_pairs={{0,2},{1,3},{32,34},{33,35},{64,66},{65,67},{96,98},{97,99},{16,18... | collective-permute-start | bytes 1179656 | tf_op jit(solution)/shard_map/yb3/ppermute | solution.py:93
  42.9 17.6 %slice-start = ((s8[12582912]{0:T(1024)(128)(4,1)}), s8[4194304]{0:T(1024)(128)(4,1)S(1)}, s32[]{:S(2)}) async-start(s8[12582912]{0:T(1024)(128)(4,1)} %bitcast.12), calls=%async_computation.1 | async-start | bytes 8388608
  42.9 17.6 %slice-start.1 = ((s8[12582912]{0:T(1024)(128)(4,1)}), s8[4194304]{0:T(1024)(128)(4,1)S(1)}, s32[]{:S(2)}) async-start(s8[12582912]{0:T(1024)(128)(4,1)} %bitcast.12), calls=%async_computation.2 | async-start | bytes 8388608
  43.7 16.0 %collective-permute-start.10 = (bf16[1,3,128,512]{3,2,1,0:T(8,128)(2,1)S(1)}, bf16[1,3,128,512]{3,2,1,0:T(8,128)(2,1)S(1)}, u32[]{:S(2)}, u32[]{:S(2)}) collective-permute-start(bf16[1,3,128,512]{3,2,1,0:T(8,128)(2,1)S(1)} %get-tuple-element.46), channel_id=1, source_target_pairs={{0,2},{1,3},{32,34},{33,35},{64,66},{65,67},{96,98},{97,99},{16,18... | collective-permute-start | bytes 1179656 | tf_op jit(solution)/shard_map/ya/ppermute | solution.py:93
  48.4 12.1 %slice-start.2 = ((s8[12582912]{0:T(1024)(128)(4,1)}), s8[4194304]{0:T(1024)(128)(4,1)S(1)}, s32[]{:S(2)}) async-start(s8[12582912]{0:T(1024)(128)(4,1)} %bitcast.12), calls=%async_computation.3 | async-start | bytes 8388608
  48.4 12.1 %copy-start.1 = (bf16[512,1536]{1,0:T(8,128)(2,1)S(1)}, bf16[512,1536]{1,0:T(8,128)(2,1)}, u32[]{:S(2)}) copy-start(bf16[512,1536]{1,0:T(8,128)(2,1)} %constant.95.args_4_) | copy-start | bytes 4718596
  48.4 12.1 %copy-start.2 = (f32[3,3,8192]{2,1,0:T(4,128)S(1)}, f32[3,3,8192]{2,1,0:T(4,128)}, u32[]{:S(2)}) copy-start(f32[3,3,8192]{2,1,0:T(4,128)} %args_6_.1) | copy-start | bytes 884740
  48.4 12.1 %copy-start.3 = (f32[8192]{0:T(1024)S(1)}, f32[8192]{0:T(1024)}, u32[]{:S(2)}) copy-start(f32[8192]{0:T(1024)} %param.8) | copy-start | bytes 98308
  48.4 12.1 %copy-start.4 = (s32[32]{0:T(128)S(1)}, s32[32]{0:T(128)}, u32[]{:S(2)}) copy-start(s32[32]{0:T(128)} %args_1_.4) | copy-start | bytes 388
  49.4 10.3 %collective-permute-start.12 = (bf16[1,3,128,512]{3,2,1,0:T(8,128)(2,1)S(1)}, bf16[1,3,128,512]{3,2,1,0:T(8,128)(2,1)S(1)}, u32[]{:S(2)}, u32[]{:S(2)}) collective-permute-start(bf16[1,3,128,512]{3,2,1,0:T(8,128)(2,1)S(1)} %get-tuple-element.48), channel_id=1, source_target_pairs={{0,12},{1,5},{32,44},{33,37},{64,76},{65,69},{96,108},{97,101},{16... | collective-permute-start | bytes 1179656 | tf_op jit(solution)/shard_map/xb2/ppermute | solution.py:93
  51.2 9.3 %collective-permute-start.13 = (bf16[1,3,128,512]{3,2,1,0:T(8,128)(2,1)S(1)}, bf16[1,3,128,512]{3,2,1,0:T(8,128)(2,1)S(1)}, u32[]{:S(2)}, u32[]{:S(2)}) collective-permute-start(bf16[1,3,128,512]{3,2,1,0:T(8,128)(2,1)S(1)} %get-tuple-element.49), channel_id=1, source_target_pairs={{0,4},{1,13},{32,36},{33,45},{64,68},{65,77},{96,100},{97,109},{16... | collective-permute-start | bytes 1179656 | tf_op jit(solution)/shard_map/xb3/ppermute | solution.py:93
  72.0 2.2 %collective-permute-start.14 = (bf16[8,8,5,8,128]{4,3,2,1,0:T(8,128)(2,1)S(1)}, bf16[8,8,5,8,128]{4,3,2,1,0:T(8,128)(2,1)S(1)}, u32[]{:S(2)}, u32[]{:S(2)}) collective-permute-start(bf16[8,8,5,8,128]{4,3,2,1,0:T(8,128)(2,1)S(1)} %get-tuple-element.51), channel_id=1, source_target_pairs={{0,1},{1,0},{32,33},{33,32},{64,65},{65,64},{96,97},{97,96},{16,17... | collective-permute-start | bytes 1966088 | tf_op jit(solution)/shard_map/shares/ppermute | solution.py:93
